TPU v7x, 256 devices: a whole 4x4x8 slice. The times are simulated.
256 devices in a mesh: blk: 128 (over z_hi, x, y, core), rep: 2 (over z_lo).
Axes of the slice: x: 4, y: 4, z: 8 (z_hi: 4, z_lo: 2; z = z_hi * 2 + z_lo), core: 2. Of those that a mesh axis runs over, the one named last changes fastest.
Arguments:
- image_hidden: bfloat16 [32768, 1152], P(('rep', 'blk')), may hold values from -6 to 6
- project_weight: bfloat16 [1152, 1152], replicated, may hold values from -0.1875 to 0.1875
- text_embed: bfloat16 [32768, 1152], P(('rep', 'blk')), may hold values from -6 to 6
- pair_ids: int32 [2, 16384], P('rep'), may hold values from 0 to 2047
- valid_count: int32 [256], P(('rep', 'blk')), may hold values from 1 to 128, as said below
- logit_scale: float32 [], replicated, may hold values from 40 to 60
- logit_bias: float32 [], replicated, may hold values from -8 to -6
Outputs:
- hidden_grad: bfloat16 [32768, 1152], P(('rep', 'blk'))
- weight_grad: float32 [1152, 1152], P('blk')
- text_grad: float32 [32768, 1152], P(('rep', 'blk'))
Inputs may be any that keep to these rules, and one draw needn't show every extreme that they name: `valid_count`: pairs at positions of a block at or beyond its count are padding; in every draw some block holds 128 live pairs and some holds 1. `pair_ids`: pairs with equal labels are positives, including each pair with itself.
All inputs are finite; a program needn't handle non-finite values.
Results may differ from a plain program's by a relative error of at most 0.0064.
Values may be sent and summed in bfloat16 or wider, within the bound.
No kernel may reach another device: no remote copies, remote signals or barrier semaphores. Data moves between devices by JAX's collectives and lax.ppermute only.
A program may use at most 128 MiB of HBM per device.

v0:
```python
import jax
import jax.numpy as jnp
from jax import lax
from jax.sharding import PartitionSpec as P

CYCLE = 16


epsilon = 1e-06


def swapped(x, axis, stride):
    return lax.ppermute(x, axis, [(i, i ^ 1 << stride) for i in range(lax.axis_size(axis))])


def pair_coefficients(left, left_labels, right, right_labels, logit_scale, logit_bias):
    scores = (
        logit_scale
        * lax.dot_general(left, right, (((1,), (1,)), ((), ())), preferred_element_type=jnp.float32)
        + logit_bias
    )
    target = jnp.where(left_labels[:, None] == right_labels[None, :], 1.0, -1.0).astype(jnp.float32)
    return (-target * jax.nn.sigmoid(-target * scores) * logit_scale).astype(jnp.bfloat16)


def spread(block, position, levels, sender):
    rows = block.shape[0]
    whole = jnp.zeros((rows * 2**levels, block.shape[1]), block.dtype)
    whole = lax.dynamic_update_slice_in_dim(whole, block, position * rows, 0)
    for level in range(levels):
        step = 2**level
        first = position // step * step
        piece = lax.dynamic_slice_in_dim(whole, first * rows, rows * step, 0)
        arrived = sender(piece, level)
        upper = position // step % 2
        other = first + (1 - 2 * upper) * step
        whole = lax.dynamic_update_slice_in_dim(whole, arrived, other * rows, 0)
    return whole


def per_device(
    image_hidden, project_weight, text_embed, pair_ids, valid_count, logit_scale, logit_bias
):
    rows_here = image_hidden.shape[0]
    width = image_hidden.shape[1]
    levels = CYCLE.bit_length() - 1
    index = lax.axis_index("blk")
    position = index % CYCLE
    group_rows = rows_here * CYCLE
    group_labels = lax.dynamic_slice_in_dim(pair_ids[0], index // CYCLE * group_rows, group_rows, 0)
    own_labels = lax.dynamic_slice_in_dim(group_labels, position * rows_here, rows_here, 0)
    projected = jnp.dot(image_hidden, project_weight, preferred_element_type=jnp.float32)
    magnitude = jnp.sqrt(jnp.sum(projected * projected, axis=1, keepdims=True) + epsilon)
    normed = projected / magnitude
    keep_row = (jnp.arange(rows_here) < valid_count[0]).astype(jnp.float32)[:, None]
    image_embed = jnp.where(keep_row > 0, normed, 0.0).astype(jnp.bfloat16)
    text_float = text_embed.astype(jnp.float32)
    text_scaled = text_float / jnp.sqrt(
        jnp.sum(text_float * text_float, axis=1, keepdims=True) + epsilon
    )
    text_normed = jnp.where(keep_row > 0, text_scaled, 0.0).astype(jnp.bfloat16)
    text_group = spread(
        text_normed, position, levels, lambda piece, level: swapped(piece, "blk", level)
    )
    coef_table = pair_coefficients(
        image_embed, own_labels, text_group, group_labels, logit_scale, logit_bias
    )
    embed_grad = jnp.dot(coef_table, text_group, preferred_element_type=jnp.float32) * keep_row

    def term(start, count):
        block_part = lax.dynamic_slice_in_dim(coef_table, start, count, 1)
        return lax.dot_general(
            block_part, image_embed, (((0,), (0,)), ((), ())), preferred_element_type=jnp.float32
        )

    held = None
    for level in range(levels - 1, -1, -1):
        step = 2**level
        half = rows_here * step
        upper = position // step % 2
        base = position // (2 * step) * (2 * step) * rows_here
        send_start = base + (1 - upper) * half
        if held is None:
            outgoing = term(send_start, half)
            keep_part = jnp.zeros((half, width), jnp.float32)
        else:
            outgoing = lax.dynamic_slice_in_dim(held, (1 - upper) * half, half, 0) + term(
                send_start, half
            )
            keep_part = lax.dynamic_slice_in_dim(held, upper * half, half, 0)
        arrived = swapped(outgoing, "blk", level)
        held = keep_part + arrived
    own_term = term(position * rows_here, rows_here)
    summed = held + own_term
    text_grad = summed * keep_row
    radial = jnp.sum(normed * embed_grad, axis=1, keepdims=True)
    normed_grad = ((embed_grad - normed * radial) / magnitude).astype(jnp.bfloat16)
    hidden_grad = lax.dot_general(
        normed_grad, project_weight, (((1,), (1,)), ((), ())), preferred_element_type=jnp.float32
    ).astype(jnp.bfloat16)
    weight_local = lax.psum_scatter(
        lax.dot_general(
            image_hidden, normed_grad, (((0,), (0,)), ((), ())), preferred_element_type=jnp.float32
        ),
        "blk",
        scatter_dimension=0,
        tiled=True,
    )
    weight_grad = lax.psum(weight_local, "rep")
    return (hidden_grad, weight_grad, text_grad)


def solution(mesh):
    return jax.shard_map(
        per_device,
        mesh=mesh,
        in_specs=(
            P(("rep", "blk"), None),
            P(),
            P(("rep", "blk"), None),
            P("rep", None),
            P(("rep", "blk")),
            P(),
            P(),
        ),
        out_specs=(P(("rep", "blk"), None), P("blk", None), P(("rep", "blk"), None)),
        check_vma=False,
    )
```

profile of v0, /device:TPU:1, one launch (start us, length us, event | category | flops | bytes accessed | tf_op | source)
XLA Modules:
  0.0 1609.2 jit_solution(8262392632271225317)
XLA Ops:
  9.8 2.1 copy-done.1
  11.9 3.3 collective-permute-start
  17.2 1.9 constant_dynamic-slice_fusion.2
  19.1 14.7 collective-permute-done.1
  34.7 2.4 constant_dynamic-slice_fusion.1
  38.3 26.8 %collective-permute-done.2 = bf16[512,1152]{1,0:T(8,128)(2,1)} collective-permute-done((bf16[512,1152]{1,0:T(8,128)(2,1)}, bf16[512,1152]{1,0:T(8,128)(2,1)}, u32[]{:S(2)}, u32[]{:S(2)}) %collective-permute-start.2) | collective-permute-done | bytes 1179680 | tf_op jit(solution)/shard_map/ppermute | solution.py:13
  65.2 2.4 constant_dynamic-update-slice_fusion.1
  67.6 3.4 constant_dynamic-slice_fusion
  74.6 47.3 %collective-permute-done.3 = bf16[1024,1152]{1,0:T(8,128)(2,1)} collective-permute-done((bf16[1024,1152]{1,0:T(8,128)(2,1)}, bf16[1024,1152]{1,0:T(8,128)(2,1)}, u32[]{:S(2)}, u32[]{:S(2)}) %collective-permute-start.3) | collective-permute-done | bytes 2359328 | tf_op jit(solution)/shard_map/ppermute | solution.py:13
  121.9 3.3 constant_dynamic-update-slice_fusion
  125.1 4.1 fusion.8
  130.0 3.0 fusion.13
  133.3 100.3 %collective-permute-done.4 = f32[1024,1152]{1,0:T(8,128)} collective-permute-done((f32[1024,1152]{1,0:T(8,128)}, f32[1024,1152]{1,0:T(8,128)}, u32[]{:S(2)}, u32[]{:S(2)}) %collective-permute-start.4) | collective-permute-done | bytes 4718624 | tf_op jit(solution)/shard_map/ppermute | solution.py:13
  233.5 3.6 dynamic-slice_add_fusion
  238.5 2.0 multiply_reduce_fusion
  241.4 3.4 convolution_bitcast_fusion
  244.8 45.0 %collective-permute-done.5 = f32[512,1152]{1,0:T(8,128)} collective-permute-done((f32[512,1152]{1,0:T(8,128)}, f32[512,1152]{1,0:T(8,128)}, u32[]{:S(2)}, u32[]{:S(2)}) %collective-permute-start.5) | collective-permute-done | bytes 2359328 | tf_op jit(solution)/shard_map/ppermute | solution.py:13
  289.8 2.6 dynamic-slice_add_fusion.1
  293.9 2.2 dynamic-slice_add_fusion.2
  298.8 21.0 %collective-permute-done.6 = f32[256,1152]{1,0:T(8,128)} collective-permute-done((f32[256,1152]{1,0:T(8,128)}, f32[256,1152]{1,0:T(8,128)}, u32[]{:S(2)}, u32[]{:S(2)}) %collective-permute-start.6) | collective-permute-done | bytes 1179680 | tf_op jit(solution)/shard_map/ppermute | solution.py:13
  324.4 6.4 collective-permute-start.7
  334.3 1246.1 %all-reduce.3.cloned.1.call-done = f32[1152,1152]{0,1:T(8,128)} async-done(((f32[1152,1152]{0,1:T(8,128)}), f32[1152,1152]{0,1:T(8,128)}) %all-reduce.3.cloned.1.call-update) | async-done | bytes 5308432
  1581.9 16.2 %psum.7 = f32[9,1152]{0,1:T(8,128)} all-reduce(f32[9,1152]{0,1:T(8,128)S(1)} %constant_dynamic-slice_fusion.6), channel_id=1, replica_groups=mesh['blk'=128,'rep'=2] {'rep'}, use_global_device_ids=true, to_apply=%region_4.5 | all-reduce | flops 10368 | bytes 82944 | tf_op jit(solution)/shard_map/psum | solution.py:109
  1600.0 2.3 add_multiply_fusion
  (54 shorter events, 26.3 us)
Async XLA Ops:
  7.2 65.9 %copy-start = (bf16[1152,1152]{1,0:T(8,128)(2,1)S(1)}, bf16[1152,1152]{1,0:T(8,128)(2,1)}, u32[]{:S(2)}) copy-start(bf16[1152,1152]{1,0:T(8,128)(2,1)} %param.8) | copy-start | bytes 7962628
  7.2 2.4 copy-start.7
  7.2 1573.2 %all-reduce.3.cloned.1.call-start = ((), (), s32[]{:S(2)}) async-start(), calls=%async_computation | async-start | bytes 10616832
  9.7 2.1 copy-start.1
  11.9 4.5 collective-permute-start
  19.1 14.7 collective-permute-start.1
  37.1 28.1 %collective-permute-start.2 = (bf16[512,1152]{1,0:T(8,128)(2,1)}, bf16[512,1152]{1,0:T(8,128)(2,1)}, u32[]{:S(2)}, u32[]{:S(2)}) collective-permute-start(bf16[512,1152]{1,0:T(8,128)(2,1)} %constant_dynamic-slice_fusion.1), channel_id=1, source_target_pairs={{0,8},{2,10},{4,12},{6,14},{8,0},{10,2},{12,4},{14,6},{16,24},{18,... | collective-permute-start | bytes 3538952 | tf_op jit(solution)/shard_map/ppermute | solution.py:13
  67.6 5.5 copy-start.5
  70.9 50.9 %collective-permute-start.3 = (bf16[1024,1152]{1,0:T(8,128)(2,1)}, bf16[1024,1152]{1,0:T(8,128)(2,1)}, u32[]{:S(2)}, u32[]{:S(2)}) collective-permute-start(bf16[1024,1152]{1,0:T(8,128)(2,1)} %constant_dynamic-slice_fusion), channel_id=1, source_target_pairs={{0,16},{2,18},{4,20},{6,22},{8,24},{10,26},{12,28},{14,30},{16,0},... | collective-permute-start | bytes 7077896 | tf_op jit(solution)/shard_map/ppermute | solution.py:13
  129.2 0.8 copy-start.10
  133.0 100.5 %collective-permute-start.4 = (f32[1024,1152]{1,0:T(8,128)}, f32[1024,1152]{1,0:T(8,128)}, u32[]{:S(2)}, u32[]{:S(2)}) collective-permute-start(f32[1024,1152]{1,0:T(8,128)} %fusion.13), channel_id=1, source_target_pairs={{0,16},{2,18},{4,20},{6,22},{8,24},{10,26},{12,28},{14,30},{16,0},... | collective-permute-start | bytes 14155784 | tf_op jit(solution)/shard_map/ppermute | solution.py:13
  133.3 105.2 %copy-start.2 = (bf16[2048,1152]{1,0:T(8,128)(2,1)S(1)}, bf16[2048,1152]{1,0:T(8,128)(2,1)}, u32[]{:S(2)}) copy-start(bf16[2048,1152]{1,0:T(8,128)(2,1)} %constant_dynamic-update-slice_fusion) | copy-start | bytes 14155780
  237.2 4.2 copy-start.6
  237.2 52.6 %collective-permute-start.5 = (f32[512,1152]{1,0:T(8,128)}, f32[512,1152]{1,0:T(8,128)}, u32[]{:S(2)}, u32[]{:S(2)}) collective-permute-start(f32[512,1152]{1,0:T(8,128)} %dynamic-slice_add_fusion), channel_id=1, source_target_pairs={{0,8},{2,10},{4,12},{6,14},{8,0},{10,2},{12,4},{14,6},{16,24},{18,... | collective-permute-start | bytes 7077896 | tf_op jit(solution)/shard_map/ppermute | solution.py:13
  240.6 0.8 copy-start.8
  292.4 1.4 copy-start.3
  293.9 3.7 copy-start.11
  296.1 23.7 %collective-permute-start.6 = (f32[256,1152]{1,0:T(8,128)}, f32[256,1152]{1,0:T(8,128)}, u32[]{:S(2)}, u32[]{:S(2)}) collective-permute-start(f32[256,1152]{1,0:T(8,128)} %dynamic-slice_add_fusion.2), channel_id=1, source_target_pairs={{0,4},{2,6},{4,0},{6,2},{8,12},{10,14},{12,8},{14,10},{16,20},{18,... | collective-permute-start | bytes 3538952 | tf_op jit(solution)/shard_map/ppermute | solution.py:13
  298.8 32.0 %copy-start.9 = (f32[128,1152]{1,0:T(8,128)S(1)}, f32[128,1152]{1,0:T(8,128)}, u32[]{:S(2)}) copy-start(f32[128,1152]{1,0:T(8,128)} %copy-done.8) | copy-start | bytes 1769476
  321.5 1.0 copy-start.4
  324.4 1275.6 %collective-permute-start.7 = (f32[128,1152]{1,0:T(8,128)}, f32[128,1152]{1,0:T(8,128)}, u32[]{:S(2)}, u32[]{:S(2)}) collective-permute-start(f32[128,1152]{1,0:T(8,128)} %dynamic-slice_add_fusion.4), channel_id=1, source_target_pairs={{0,2},{2,0},{4,6},{6,4},{8,10},{10,8},{12,14},{14,12},{16,18},{18,... | collective-permute-start | bytes 1769480 | tf_op jit(solution)/shard_map/ppermute | solution.py:13
Sparse Core Ops, SparseCore 0:
  244.9 1335.4 all-reduce.2
where the time goes:
time: 1610 us
  waiting for transfers between devices  1500 us (93%)
  local copies, waits for them, and re-layouts  27 us (2%)
  matrix products  24.5 us (2%)
  between operations  17.1 us (1%)
  blocking collectives  16.2 us (1%)
    unnamed x2, waiting for transfers between devices  1250 us
    ppermute x8, waiting for transfers between devices, swapped(): lax.ppermute(x, axis, [(i, i ^ 1 << stride) for i in range(lax.axis_size(...  256 us
  transfers between devices with their start and end apart: 9, of which 8 were waited for; matrix products, arithmetic and copies ran while one was open for 1% of the time, Pallas kernels for 0%

commit v1 on v0

v1 whole, which is shorter than its diff:
```python
import jax
import jax.numpy as jnp
import numpy as np
from jax import lax
from jax.sharding import Mesh, PartitionSpec as P

epsilon = 1e-06
AXES = ("zh", "x1", "x0", "y", "c", "zl")
SPLIT = 640
f32 = jnp.float32
bf16 = jnp.bfloat16


def dot(a, b, ca, cb):
    return lax.dot_general(a, b, (((ca,), (cb,)), ((), ())), preferred_element_type=f32)


def xor(x, axis, step):
    size = lax.axis_size(axis)
    return lax.ppermute(x, axis, [(i, i ^ step) for i in range(size)])


def row_norm(x):
    return jnp.sqrt(jnp.sum(x * x, axis=1, keepdims=True) + epsilon)


def per_device(hidden, weight, text, pair_ids, valid_count, logit_scale, logit_bias):
    rows, width = hidden.shape
    zh, y, c = (lax.axis_index(a) for a in ("zh", "y", "c"))
    x1, x0 = lax.axis_index("x1"), lax.axis_index("x0")
    x = x1 * 2 + x0
    X = ("x1", "x0")
    keep = (jnp.arange(rows) < valid_count[0])[:, None]
    with jax.named_scope("gather"):
        hid = jnp.where(keep, hidden, 0).astype(bf16)
        txt = jnp.where(keep, text, 0).astype(bf16)
        hid_x = xor(hid, "x0", 1)
        txt_2 = xor(txt, "y", 2)
        txt_1 = xor(txt, "y", 1)
        txt_3 = xor(txt, "y", 3)
        hid_2 = jnp.concatenate([hid, hid_x], 0)
        hid_c = xor(hid_2, "c", 1)
    hid_all = jnp.concatenate([hid_2, hid_c], 0)
    labels = lax.dynamic_slice_in_dim(pair_ids[0], (zh * 2 + x1) * rows * 16, rows * 16, 0)
    labels = labels.reshape(16, rows)

    def label(px, py, pc):
        return lax.dynamic_slice_in_dim(labels, (px * 4 + py) * 2 + pc, 1, 0)[0]

    hid_labels = jnp.concatenate(
        [label(x0, y, c), label(1 - x0, y, c), label(x0, y, 1 - c), label(1 - x0, y, 1 - c)]
    )
    txt_labels = jnp.concatenate([label(x0, y ^ j, c) for j in range(4)])

    def places(a, b, sa, sb, pa, pb):
        i = np.arange(576)
        r, m = i % 9, i // 9 % 4
        second, first = i // 36 % 4, i // 144
        row = ((zh ^ jnp.asarray(m)) * 288 + (pa ^ jnp.asarray(first)) * sa
               + (pb ^ jnp.asarray(second)) * sb + c * 9 + r)
        return (row[:, None] == jnp.arange(width)[None, :]).astype(bf16)

    with jax.named_scope("project"):
        projected = dot(hid_all, weight, 1, 0)
        magnitude = row_norm(projected)
        normed = projected / magnitude
        embed = normed.astype(bf16)
        hid_a = dot(places(0, 0, 72, 18, x, y), hid_all, 1, 1).astype(bf16)
        hid_b = dot(places(0, 0, 18, 72, y, x), hid_all, 1, 1).astype(bf16)
    with jax.named_scope("tile"):
        txt_all = jnp.concatenate([txt, txt_1, txt_2, txt_3], 0).astype(f32)
        txt_all = (txt_all / row_norm(txt_all)).astype(bf16)
        scores = logit_scale * dot(embed, txt_all, 1, 1) + logit_bias
        target = jnp.where(hid_labels[:, None] == txt_labels[None, :], 1.0, -1.0).astype(f32)
        coef = (-target * jax.nn.sigmoid(-target * scores) * logit_scale).astype(bf16)
        embed_grad = dot(coef, txt_all, 1, 0)
        radial = jnp.sum(normed * embed_grad, axis=1, keepdims=True)
        part = (embed_grad - normed * radial) / magnitude
        txt_part = dot(coef, embed, 0, 0)
        txt_send = txt_part.astype(bf16)
    with jax.named_scope("core"):
        arrived = xor(part.astype(bf16), "c", 1)
        half = 2 * rows
        summed = part + jnp.concatenate([arrived[half:], arrived[:half]], 0).astype(f32)
        summed_b = summed.astype(bf16)
    with jax.named_scope("weight"):
        def four(block, axis):
            got = [xor(block[k].astype(bf16), axis, k).astype(f32) for k in (2, 1, 3)]
            return block[0] + got[0] + got[1] + got[2]

        part_a = dot(hid_a, summed_b[:, :SPLIT], 1, 0).reshape(4, 144, SPLIT)
        part_b = dot(hid_b, summed_b[:, SPLIT:], 1, 0).reshape(4, 144, width - SPLIT)
        part_a = four(part_a, X)
        part_b = four(part_b, "y")
        part_a = four(part_a.reshape(4, 36, SPLIT), "y")
        part_b = four(part_b.reshape(4, 36, width - SPLIT), X)
        whole = jnp.concatenate([part_a, part_b], 1)
        whole = whole + xor(whole.astype(bf16), "zl", 1).astype(f32)
        weight_grad = four(whole.reshape(4, 9, width), "zh")
    with jax.named_scope("hidden"):
        own = summed[:rows] + xor(summed_b[rows:half], "x0", 1).astype(f32)
        hidden_grad = dot(own.astype(bf16), weight, 1, 1)
        hidden_grad = jnp.where(keep, hidden_grad, 0.0).astype(bf16)
    with jax.named_scope("text"):
        got = [xor(txt_send[j * rows : (j + 1) * rows], "y", j).astype(f32) for j in (2, 1, 3)]
        text_grad = jnp.where(keep, txt_part[:rows] + got[0] + got[1] + got[2], 0.0)
    return hidden_grad, weight_grad, text_grad


def solution(mesh):
    fine = Mesh(mesh.devices.reshape(4, 2, 2, 4, 2, 2), AXES)
    blk = ("zh", "x1", "x0", "y", "c")
    by_row = P(("zl",) + blk, None)
    return jax.shard_map(
        per_device,
        mesh=fine,
        in_specs=(by_row, P(), by_row, P("zl", None), P(("zl",) + blk), P(), P()),
        out_specs=(by_row, P(blk, None), by_row),
        check_vma=False,
    )
```

time: 1610 us -> 110 us (0.07)
  the two profiles are of different devices: /device:TPU:1 before, /device:TPU:2 now
where the time goes in v1:
time: 110 us; the launch traced here: 109 us
  starting transfers between devices  41.5 us (38%)
  matrix products  23.6 us (21%)
  waiting for transfers between devices  22.1 us (20%)
  other arithmetic  12.8 us (12%)
  local copies, waits for them, and re-layouts  6.09 us (6%)
  between operations  3.04 us (3%)
    ppermute x26, starting transfers between devices, xor(): return lax.ppermute(x, axis, [(i, i ^ step) for i in range(size)])  41.5 us
    dot_general x7, matrix products, dot(): lax.dot_general(a, b, (((ca,), (cb,)), ((), ())), preferred_element_type=...  23.6 us
    ppermute x26, waiting for transfers between devices, xor(): return lax.ppermute(x, axis, [(i, i ^ step) for i in range(size)])  22.1 us
    convert_element_type x1, other arithmetic, per_device(): summed_b = summed.astype(bf16)  2.42 us
  transfers between devices with their start and end apart: 26, of which 12 were waited for; matrix products, arithmetic and copies ran while one was open for 28% of the time, Pallas kernels for 0%

profile of v1, /device:TPU:2, one launch (start us, length us, event | category | flops | bytes accessed | tf_op | source)
XLA Modules:
  0.0 109.1 jit_solution(4664911145893945417)
XLA Ops:
  2.6 2.4 %collective-permute-start = (bf16[128,1152]{1,0:T(8,128)(2,1)S(1)}, bf16[128,1152]{1,0:T(8,128)(2,1)S(1)}, u32[]{:S(2)}, u32[]{:S(2)}) collective-permute-start(bf16[128,1152]{1,0:T(8,128)(2,1)S(1)} %get-tuple-element.41), channel_id=1, source_target_pairs={{0,16},{16,0},{1,17},{17,1},{2,18},{18,2},{3,19},{19,3},{4,20},{20... | collective-permute-start | bytes 884744 | tf_op jit(solution)/shard_map/gather/ppermute | solution.py:20
  6.9 2.2 %collective-permute-start.2 = (bf16[128,1152]{1,0:T(8,128)(2,1)S(1)}, bf16[128,1152]{1,0:T(8,128)(2,1)}, u32[]{:S(2)}, u32[]{:S(2)}) collective-permute-start(bf16[128,1152]{1,0:T(8,128)(2,1)S(1)} %get-tuple-element.40), channel_id=1, source_target_pairs={{0,4},{4,0},{8,12},{12,8},{1,5},{5,1},{9,13},{13,9},{2,6},{6,2},{1... | collective-permute-start | bytes 884744 | tf_op jit(solution)/shard_map/gather/ppermute | solution.py:20
  9.1 2.4 %collective-permute-done = bf16[128,1152]{1,0:T(8,128)(2,1)S(1)} collective-permute-done((bf16[128,1152]{1,0:T(8,128)(2,1)S(1)}, bf16[128,1152]{1,0:T(8,128)(2,1)S(1)}, u32[]{:S(2)}, u32[]{:S(2)}) %collective-permute-start) | collective-permute-done | bytes 294944 | tf_op jit(solution)/shard_map/gather/ppermute | solution.py:20
  14.4 5.0 %collective-permute-done.4 = bf16[128,1152]{1,0:T(8,128)(2,1)} collective-permute-done((bf16[128,1152]{1,0:T(8,128)(2,1)S(1)}, bf16[128,1152]{1,0:T(8,128)(2,1)}, u32[]{:S(2)}, u32[]{:S(2)}) %collective-permute-start.4) | collective-permute-done | bytes 294944 | tf_op jit(solution)/shard_map/gather/ppermute | solution.py:20
  21.5 3.0 %multiply_reduce_fusion.1 = (f32[512]{0:T(512)S(1)}, f32[512,1152]{1,0:T(8,128)S(1)}) fusion(bf16[1152,1152]{1,0:T(8,128)(2,1)S(1)} %copy-done, bf16[256,1152]{1,0:T(8,128)(2,1)} %collective-permute-done.1, bf16[128,1152]{1,0:T(8,128)(2,1)S(1)} %collective-permute-done, bf16[128,1152]{1,0:T(8,128)(2,1)S(1)} %get-tuple-element.41), kind=kOutput, calls=%fused_computation.13 | convolution fusion | flops 1363672576 | bytes 6195200 | tf_op jit(solution)/shard_map/project/dot_general | solution.py:15
  24.6 3.1 %fusion.17 = bf16[512,512]{1,0:T(8,128)(2,1)S(1)} fusion(f32[]{:T(128)S(6)} %copy.20, f32[]{:T(128)S(6)} %copy.19, s32[512]{0:T(512)S(1)} %get-tuple-element.43, s32[512]{0:T(512)S(1)} %get-tuple-element.42, f32[512]{0:T(512)S(1)} %add_sqrt_fusion, bf16[128,1152]{1,0:T(8,128)(2,1)} %collective-permute-done.4, bf16[128,1152]{1,0:T(8,128)(2,1)} %collective-permute-done.3, ...), kind=kOutput, calls=%fused_computation.27 | convolution fusion | flops 614203392 | bytes 4071432 | tf_op jit(solution)/shard_map/tile/dot_general | solution.py:15
  27.7 2.5 %multiply_reduce_fusion = (f32[512]{0:T(512)S(1)}, f32[512,1152]{1,0:T(8,128)S(1)}) fusion(f32[512,1152]{1,0:T(8,128)S(1)} %get-tuple-element.45, f32[512]{0:T(512)S(1)} %add_sqrt_fusion.1, bf16[512,512]{1,0:T(8,128)(2,1)S(1)} %fusion.17, f32[512]{0:T(512)S(1)} %add_sqrt_fusion, bf16[128,1152]{1,0:T(8,128)(2,1)} %collective-permute-done.4, ...), kind=kOutput, calls=%fused_computation.12 | convolution fusion | flops 611646976 | bytes 6428672 | tf_op jit(solution)/shard_map/tile/dot_general | solution.py:15
  32.1 4.3 %fusion.72 = (bf16[512,1152]{1,0:T(8,128)(2,1)S(1)}, f32[512,1152]{1,0:T(8,128)}) fusion(bf16[512,512]{1,0:T(8,128)(2,1)} %copy-done.11, f32[512,1152]{1,0:T(8,128)} %copy-done.1, f32[512]{0:T(512)S(1)} %add_sqrt_fusion.1), kind=kOutput, calls=%fused_computation.108 | convolution fusion | flops 605749248 | bytes 6424576 | tf_op jit(solution)/shard_map/tile/dot_general | solution.py:15
  37.3 2.9 %collective-permute-start.25 = (bf16[128,1152]{1,0:T(8,128)(2,1)}, bf16[128,1152]{1,0:T(8,128)(2,1)}, u32[]{:S(2)}, u32[]{:S(2)}) collective-permute-start(bf16[128,1152]{1,0:T(8,128)(2,1)} %get-tuple-element.12), channel_id=1, source_target_pairs={{0,12},{4,8},{8,4},{12,0},{1,13},{5,9},{9,5},{13,1},{2,14},{6,10},... | collective-permute-start | bytes 884744 | tf_op jit(solution)/shard_map/text/ppermute | solution.py:20
  41.8 2.4 %fusion.62 = (bf16[512,1152]{1,0:T(8,128)(2,1)}, f32[512,1152]{1,0:T(8,128)}) fusion(bf16[256,1152]{1,0:T(8,128)(2,1)S(1)} %get-tuple-element.15, bf16[256,1152]{1,0:T(8,128)(2,1)S(1)} %get-tuple-element.14, f32[512,1152]{1,0:T(8,128)S(1)} %copy-done.4, f32[512]{0:T(512)S(1)} %get-tuple-element.46, f32[512,1152]{1,0:T(8,128)S(1)} %copy-done.2, ...), kind=kLoop, calls=%fused_computation.98 | loop fusion | flops 5898240 | bytes 9441280 | tf_op jit(solution)/shard_map/core/convert_element_type | solution.py:85
  44.2 3.7 %fusion.70 = (bf16[576,512]{1,0:T(8,128)(2,1)S(1)}, f32[576,512]{1,0:T(8,128)}) fusion(bf16[512,1152]{1,0:T(8,128)(2,1)} %get-tuple-element.9, s32[576]{0:T(1024)S(1)} %get-tuple-element.32, bf16[256,1152]{1,0:T(8,128)(2,1)} %collective-permute-done.1, bf16[128,1152]{1,0:T(8,128)(2,1)} %copy-done.6, bf16[128,1152]{1,0:T(8,128)(2,1)S(1)} %get-tuple-element.41), kind=kOutput, calls=%fused_computation.106 | convolution fusion | flops 986259456 | bytes 3475712 | tf_op jit(solution)/shard_map/weight/dot_general | solution.py:15
  50.5 2.8 %collective-permute-start.13 = (bf16[144,512]{1,0:T(8,128)(2,1)}, bf16[144,512]{1,0:T(8,128)(2,1)S(1)}, u32[]{:S(2)}, u32[]{:S(2)}) collective-permute-start(bf16[144,512]{1,0:T(8,128)(2,1)} %get-tuple-element.19), channel_id=1, source_target_pairs={{0,8},{4,12},{8,0},{12,4},{1,9},{5,13},{9,1},{13,5},{2,10},{6,14},... | collective-permute-start | bytes 442376 | tf_op jit(solution)/shard_map/weight/ppermute | solution.py:20
  53.4 4.3 %fusion.71 = (bf16[576,640]{1,0:T(8,128)(2,1)}, f32[576,640]{1,0:T(8,128)}) fusion(bf16[512,1152]{1,0:T(8,128)(2,1)} %get-tuple-element.9, s32[576]{0:T(1024)S(1)} %get-tuple-element.31, bf16[256,1152]{1,0:T(8,128)(2,1)} %collective-permute-done.1, bf16[128,1152]{1,0:T(8,128)(2,1)} %copy-done.6, bf16[128,1152]{1,0:T(8,128)(2,1)S(1)} %get-tuple-element.41), kind=kOutput, calls=%fused_computation.107 | convolution fusion | flops 1061830656 | bytes 4049152 | tf_op jit(solution)/shard_map/weight/dot_general | solution.py:15
  58.9 2.2 %collective-permute-start.9 = (bf16[144,640]{1,0:T(8,128)(2,1)S(1)}, bf16[144,640]{1,0:T(8,128)(2,1)S(1)}, u32[]{:S(2)}, u32[]{:S(2)}) collective-permute-start(bf16[144,640]{1,0:T(8,128)(2,1)S(1)} %get-tuple-element.17), channel_id=1, source_target_pairs={{0,48},{16,32},{32,16},{48,0},{1,49},{17,33},{33,17},{49,1},{2,50}... | collective-permute-start | bytes 552968 | tf_op jit(solution)/shard_map/weight/ppermute | solution.py:20
  65.2 2.6 %collective-permute-start.18 = (bf16[36,512]{1,0:T(8,128)(2,1)S(1)}, bf16[36,512]{1,0:T(8,128)(2,1)S(1)}, u32[]{:S(2)}, u32[]{:S(2)}) collective-permute-start(bf16[36,512]{1,0:T(8,128)(2,1)S(1)} %get-tuple-element.26), channel_id=1, source_target_pairs={{0,48},{16,32},{32,16},{48,0},{1,49},{17,33},{33,17},{49,1},{2,50}... | collective-permute-start | bytes 110600 | tf_op jit(solution)/shard_map/weight/ppermute | solution.py:20
  70.9 3.0 %collective-permute-start.16 = (bf16[36,512]{1,0:T(8,128)(2,1)S(1)}, bf16[36,512]{1,0:T(8,128)(2,1)S(1)}, u32[]{:S(2)}, u32[]{:S(2)}) collective-permute-start(bf16[36,512]{1,0:T(8,128)(2,1)S(1)} %get-tuple-element.25), channel_id=1, source_target_pairs={{0,32},{16,48},{32,0},{48,16},{1,33},{17,49},{33,1},{49,17},{2,34}... | collective-permute-start | bytes 110600 | tf_op jit(solution)/shard_map/weight/ppermute | solution.py:20
  76.4 3.5 %collective-permute-start.10 = (bf16[36,640]{1,0:T(8,128)(2,1)S(1)}, bf16[36,640]{1,0:T(8,128)(2,1)S(1)}, u32[]{:S(2)}, u32[]{:S(2)}) collective-permute-start(bf16[36,640]{1,0:T(8,128)(2,1)S(1)} %get-tuple-element.22), channel_id=1, source_target_pairs={{0,8},{4,12},{8,0},{12,4},{1,9},{5,13},{9,1},{13,5},{2,10},{6,14},... | collective-permute-start | bytes 138248 | tf_op jit(solution)/shard_map/weight/ppermute | solution.py:20
  80.7 2.8 %collective-permute-done.10 = bf16[36,640]{1,0:T(8,128)(2,1)S(1)} collective-permute-done((bf16[36,640]{1,0:T(8,128)(2,1)S(1)}, bf16[36,640]{1,0:T(8,128)(2,1)S(1)}, u32[]{:S(2)}, u32[]{:S(2)}) %collective-permute-start.10) | collective-permute-done | bytes 46112 | tf_op jit(solution)/shard_map/weight/ppermute | solution.py:20
  83.6 2.0 %collective-permute-start.19 = (bf16[36,1152]{1,0:T(8,128)(2,1)S(1)}, bf16[36,1152]{1,0:T(8,128)(2,1)S(1)}, u32[]{:S(2)}, u32[]{:S(2)}) collective-permute-start(bf16[36,1152]{1,0:T(8,128)(2,1)S(1)} %fusion.34), channel_id=1, source_target_pairs={{0,1},{1,0},{2,3},{3,2},{4,5},{5,4},{6,7},{7,6},{8,9},{9,8},{10,11... | collective-permute-start | bytes 248840 | tf_op jit(solution)/shard_map/weight/ppermute | solution.py:20
  85.6 3.1 %collective-permute-done.23 = bf16[128,1152]{1,0:T(8,128)(2,1)S(1)} collective-permute-done((bf16[128,1152]{1,0:T(8,128)(2,1)S(1)}, bf16[128,1152]{1,0:T(8,128)(2,1)S(1)}, u32[]{:S(2)}, u32[]{:S(2)}) %collective-permute-start.23) | collective-permute-done | bytes 294944 | tf_op jit(solution)/shard_map/text/ppermute | solution.py:20
  88.7 2.2 %fusion.23 = f32[128,1152]{1,0:T(8,128)} fusion(f32[512,1152]{1,0:T(8,128)} %get-tuple-element.53, bf16[128,1152]{1,0:T(8,128)(2,1)} %collective-permute-done.25, bf16[128,1152]{1,0:T(8,128)(2,1)} %collective-permute-done.24, bf16[128,1152]{1,0:T(8,128)(2,1)S(1)} %collective-permute-done.23, pred[128]{0:T(512)(128)(4,1)S(1)} %iota_compare_fusion.12), kind=kLoop, calls=%fused_computation.37 | loop fusion | flops 1032192 | bytes 2064512 | tf_op jit(solution)/shard_map/text/jit(_where)/select_n | solution.py:106
  92.7 6.4 %collective-permute-start.22 = (bf16[9,1152]{1,0:T(8,128)(2,1)S(1)}, bf16[9,1152]{1,0:T(8,128)(2,1)S(1)}, u32[]{:S(2)}, u32[]{:S(2)}) collective-permute-start(bf16[9,1152]{1,0:T(8,128)(2,1)S(1)} %get-tuple-element.29), channel_id=1, source_target_pairs={{0,192},{64,128},{128,64},{192,0},{1,193},{65,129},{129,65},{193,1... | collective-permute-start | bytes 62216 | tf_op jit(solution)/shard_map/weight/ppermute | solution.py:20
  101.6 2.7 %fusion.2 = bf16[128,1152]{1,0:T(8,128)(2,1)} fusion(bf16[1152,1152]{1,0:T(8,128)(2,1)S(1)} %copy-done, f32[512,1152]{1,0:T(8,128)} %get-tuple-element.10, bf16[128,1152]{1,0:T(8,128)(2,1)S(1)} %collective-permute-done.6, pred[128]{0:T(512)(128)(4,1)S(1)} %iota_compare_fusion.12), kind=kOutput, calls=%fused_computation.7 | convolution fusion | flops 340475904 | bytes 3833984 | tf_op jit(solution)/shard_map/hidden/dot_general | solution.py:15
  104.3 4.1 %collective-permute-done.20 = bf16[9,1152]{1,0:T(8,128)(2,1)S(1)} collective-permute-done((bf16[9,1152]{1,0:T(8,128)(2,1)S(1)}, bf16[9,1152]{1,0:T(8,128)(2,1)S(1)}, u32[]{:S(2)}, u32[]{:S(2)}) %collective-permute-start.20) | collective-permute-done | bytes 20768 | tf_op jit(solution)/shard_map/weight/ppermute | solution.py:20
  (87 shorter events, 30.4 us)
Async XLA Ops:
  2.6 8.8 %collective-permute-start = (bf16[128,1152]{1,0:T(8,128)(2,1)S(1)}, bf16[128,1152]{1,0:T(8,128)(2,1)S(1)}, u32[]{:S(2)}, u32[]{:S(2)}) collective-permute-start(bf16[128,1152]{1,0:T(8,128)(2,1)S(1)} %get-tuple-element.41), channel_id=1, source_target_pairs={{0,16},{16,0},{1,17},{17,1},{2,18},{18,2},{3,19},{19,3},{4,20},{20... | collective-permute-start | bytes 884744 | tf_op jit(solution)/shard_map/gather/ppermute | solution.py:20
  5.0 14.4 %collective-permute-start.4 = (bf16[128,1152]{1,0:T(8,128)(2,1)S(1)}, bf16[128,1152]{1,0:T(8,128)(2,1)}, u32[]{:S(2)}, u32[]{:S(2)}) collective-permute-start(bf16[128,1152]{1,0:T(8,128)(2,1)S(1)} %get-tuple-element.40), channel_id=1, source_target_pairs={{0,12},{4,8},{8,4},{12,0},{1,13},{5,9},{9,5},{13,1},{2,14},{6,10},... | collective-permute-start | bytes 884744 | tf_op jit(solution)/shard_map/gather/ppermute | solution.py:20
  6.3 13.2 %collective-permute-start.3 = (bf16[128,1152]{1,0:T(8,128)(2,1)S(1)}, bf16[128,1152]{1,0:T(8,128)(2,1)}, u32[]{:S(2)}, u32[]{:S(2)}) collective-permute-start(bf16[128,1152]{1,0:T(8,128)(2,1)S(1)} %get-tuple-element.40), channel_id=1, source_target_pairs={{0,8},{4,12},{8,0},{12,4},{1,9},{5,13},{9,1},{13,5},{2,10},{6,14},... | collective-permute-start | bytes 884744 | tf_op jit(solution)/shard_map/gather/ppermute | solution.py:20
  6.9 13.1 %collective-permute-start.2 = (bf16[128,1152]{1,0:T(8,128)(2,1)S(1)}, bf16[128,1152]{1,0:T(8,128)(2,1)}, u32[]{:S(2)}, u32[]{:S(2)}) collective-permute-start(bf16[128,1152]{1,0:T(8,128)(2,1)S(1)} %get-tuple-element.40), channel_id=1, source_target_pairs={{0,4},{4,0},{8,12},{12,8},{1,5},{5,1},{9,13},{13,9},{2,6},{6,2},{1... | collective-permute-start | bytes 884744 | tf_op jit(solution)/shard_map/gather/ppermute | solution.py:20
  12.4 9.1 %collective-permute-start.1 = (bf16[256,1152]{1,0:T(8,128)(2,1)}, bf16[256,1152]{1,0:T(8,128)(2,1)}, u32[]{:S(2)}, u32[]{:S(2)}) collective-permute-start(bf16[256,1152]{1,0:T(8,128)(2,1)} %pad_maximum_fusion.2), channel_id=1, source_target_pairs={{0,2},{2,0},{1,3},{3,1},{4,6},{6,4},{5,7},{7,5},{8,10},{10,8},{9,1... | collective-permute-start | bytes 1769480 | tf_op jit(solution)/shard_map/gather/ppermute | solution.py:20
  32.0 8.4 %collective-permute-start.5 = (bf16[512,1152]{1,0:T(8,128)(2,1)}, bf16[512,1152]{1,0:T(8,128)(2,1)}, u32[]{:S(2)}, u32[]{:S(2)}) collective-permute-start(bf16[512,1152]{1,0:T(8,128)(2,1)} %fusion.53), channel_id=1, source_target_pairs={{0,2},{2,0},{1,3},{3,1},{4,6},{6,4},{5,7},{7,5},{8,10},{10,8},{9,1... | collective-permute-start | bytes 3538952 | tf_op jit(solution)/shard_map/core/ppermute | solution.py:20
  37.3 48.3 %collective-permute-start.25 = (bf16[128,1152]{1,0:T(8,128)(2,1)}, bf16[128,1152]{1,0:T(8,128)(2,1)}, u32[]{:S(2)}, u32[]{:S(2)}) collective-permute-start(bf16[128,1152]{1,0:T(8,128)(2,1)} %get-tuple-element.12), channel_id=1, source_target_pairs={{0,12},{4,8},{8,4},{12,0},{1,13},{5,9},{9,5},{13,1},{2,14},{6,10},... | collective-permute-start | bytes 884744 | tf_op jit(solution)/shard_map/text/ppermute | solution.py:20
  40.3 45.4 %collective-permute-start.24 = (bf16[128,1152]{1,0:T(8,128)(2,1)}, bf16[128,1152]{1,0:T(8,128)(2,1)}, u32[]{:S(2)}, u32[]{:S(2)}) collective-permute-start(bf16[128,1152]{1,0:T(8,128)(2,1)} %get-tuple-element.13), channel_id=1, source_target_pairs={{0,4},{4,0},{8,12},{12,8},{1,5},{5,1},{9,13},{13,9},{2,6},{6,2},{1... | collective-permute-start | bytes 884744 | tf_op jit(solution)/shard_map/text/ppermute | solution.py:20
  48.7 10.2 %collective-permute-start.15 = (bf16[144,512]{1,0:T(8,128)(2,1)}, bf16[144,512]{1,0:T(8,128)(2,1)S(1)}, u32[]{:S(2)}, u32[]{:S(2)}) collective-permute-start(bf16[144,512]{1,0:T(8,128)(2,1)} %get-tuple-element.20), channel_id=1, source_target_pairs={{0,12},{4,8},{8,4},{12,0},{1,13},{5,9},{9,5},{13,1},{2,14},{6,10},... | collective-permute-start | bytes 442376 | tf_op jit(solution)/shard_map/weight/ppermute | solution.py:20
  49.7 11.4 %collective-permute-start.14 = (bf16[144,512]{1,0:T(8,128)(2,1)}, bf16[144,512]{1,0:T(8,128)(2,1)S(1)}, u32[]{:S(2)}, u32[]{:S(2)}) collective-permute-start(bf16[144,512]{1,0:T(8,128)(2,1)} %get-tuple-element.21), channel_id=1, source_target_pairs={{0,4},{4,0},{8,12},{12,8},{1,5},{5,1},{9,13},{13,9},{2,6},{6,2},{1... | collective-permute-start | bytes 442376 | tf_op jit(solution)/shard_map/weight/ppermute | solution.py:20
  50.5 12.0 %collective-permute-start.13 = (bf16[144,512]{1,0:T(8,128)(2,1)}, bf16[144,512]{1,0:T(8,128)(2,1)S(1)}, u32[]{:S(2)}, u32[]{:S(2)}) collective-permute-start(bf16[144,512]{1,0:T(8,128)(2,1)} %get-tuple-element.19), channel_id=1, source_target_pairs={{0,8},{4,12},{8,0},{12,4},{1,9},{5,13},{9,1},{13,5},{2,10},{6,14},... | collective-permute-start | bytes 442376 | tf_op jit(solution)/shard_map/weight/ppermute | solution.py:20
  58.9 6.3 %collective-permute-start.9 = (bf16[144,640]{1,0:T(8,128)(2,1)S(1)}, bf16[144,640]{1,0:T(8,128)(2,1)S(1)}, u32[]{:S(2)}, u32[]{:S(2)}) collective-permute-start(bf16[144,640]{1,0:T(8,128)(2,1)S(1)} %get-tuple-element.17), channel_id=1, source_target_pairs={{0,48},{16,32},{32,16},{48,0},{1,49},{17,33},{33,17},{49,1},{2,50}... | collective-permute-start | bytes 552968 | tf_op jit(solution)/shard_map/weight/ppermute | solution.py:20
  61.1 7.6 %collective-permute-start.8 = (bf16[144,640]{1,0:T(8,128)(2,1)S(1)}, bf16[144,640]{1,0:T(8,128)(2,1)S(1)}, u32[]{:S(2)}, u32[]{:S(2)}) collective-permute-start(bf16[144,640]{1,0:T(8,128)(2,1)S(1)} %get-tuple-element.18), channel_id=1, source_target_pairs={{0,16},{16,0},{32,48},{48,32},{1,17},{17,1},{33,49},{49,33},{2,18}... | collective-permute-start | bytes 552968 | tf_op jit(solution)/shard_map/weight/ppermute | solution.py:20
  62.6 8.4 %collective-permute-start.7 = (bf16[144,640]{1,0:T(8,128)(2,1)S(1)}, bf16[144,640]{1,0:T(8,128)(2,1)S(1)}, u32[]{:S(2)}, u32[]{:S(2)}) collective-permute-start(bf16[144,640]{1,0:T(8,128)(2,1)S(1)} %get-tuple-element.16), channel_id=1, source_target_pairs={{0,32},{16,48},{32,0},{48,16},{1,33},{17,49},{33,1},{49,17},{2,34}... | collective-permute-start | bytes 552968 | tf_op jit(solution)/shard_map/weight/ppermute | solution.py:20
  65.2 9.9 %collective-permute-start.18 = (bf16[36,512]{1,0:T(8,128)(2,1)S(1)}, bf16[36,512]{1,0:T(8,128)(2,1)S(1)}, u32[]{:S(2)}, u32[]{:S(2)}) collective-permute-start(bf16[36,512]{1,0:T(8,128)(2,1)S(1)} %get-tuple-element.26), channel_id=1, source_target_pairs={{0,48},{16,32},{32,16},{48,0},{1,49},{17,33},{33,17},{49,1},{2,50}... | collective-permute-start | bytes 110600 | tf_op jit(solution)/shard_map/weight/ppermute | solution.py:20
  68.7 7.4 %collective-permute-start.17 = (bf16[36,512]{1,0:T(8,128)(2,1)S(1)}, bf16[36,512]{1,0:T(8,128)(2,1)S(1)}, u32[]{:S(2)}, u32[]{:S(2)}) collective-permute-start(bf16[36,512]{1,0:T(8,128)(2,1)S(1)} %get-tuple-element.27), channel_id=1, source_target_pairs={{0,16},{16,0},{32,48},{48,32},{1,17},{17,1},{33,49},{49,33},{2,18}... | collective-permute-start | bytes 110600 | tf_op jit(solution)/shard_map/weight/ppermute | solution.py:20
  70.9 5.5 %collective-permute-start.16 = (bf16[36,512]{1,0:T(8,128)(2,1)S(1)}, bf16[36,512]{1,0:T(8,128)(2,1)S(1)}, u32[]{:S(2)}, u32[]{:S(2)}) collective-permute-start(bf16[36,512]{1,0:T(8,128)(2,1)S(1)} %get-tuple-element.25), channel_id=1, source_target_pairs={{0,32},{16,48},{32,0},{48,16},{1,33},{17,49},{33,1},{49,17},{2,34}... | collective-permute-start | bytes 110600 | tf_op jit(solution)/shard_map/weight/ppermute | solution.py:20
  75.1 5.4 %collective-permute-start.12 = (bf16[36,640]{1,0:T(8,128)(2,1)S(1)}, bf16[36,640]{1,0:T(8,128)(2,1)S(1)}, u32[]{:S(2)}, u32[]{:S(2)}) collective-permute-start(bf16[36,640]{1,0:T(8,128)(2,1)S(1)} %get-tuple-element.23), channel_id=1, source_target_pairs={{0,12},{4,8},{8,4},{12,0},{1,13},{5,9},{9,5},{13,1},{2,14},{6,10},... | collective-permute-start | bytes 138248 | tf_op jit(solution)/shard_map/weight/ppermute | solution.py:20
  76.4 7.2 %collective-permute-start.10 = (bf16[36,640]{1,0:T(8,128)(2,1)S(1)}, bf16[36,640]{1,0:T(8,128)(2,1)S(1)}, u32[]{:S(2)}, u32[]{:S(2)}) collective-permute-start(bf16[36,640]{1,0:T(8,128)(2,1)S(1)} %get-tuple-element.22), channel_id=1, source_target_pairs={{0,8},{4,12},{8,0},{12,4},{1,9},{5,13},{9,1},{13,5},{2,10},{6,14},... | collective-permute-start | bytes 138248 | tf_op jit(solution)/shard_map/weight/ppermute | solution.py:20
  80.5 8.2 %collective-permute-start.23 = (bf16[128,1152]{1,0:T(8,128)(2,1)S(1)}, bf16[128,1152]{1,0:T(8,128)(2,1)S(1)}, u32[]{:S(2)}, u32[]{:S(2)}) collective-permute-start(bf16[128,1152]{1,0:T(8,128)(2,1)S(1)} %copy-done.5), channel_id=1, source_target_pairs={{0,8},{4,12},{8,0},{12,4},{1,9},{5,13},{9,1},{13,5},{2,10},{6,14},... | collective-permute-start | bytes 884744 | tf_op jit(solution)/shard_map/text/ppermute | solution.py:20
  83.6 9.0 %collective-permute-start.19 = (bf16[36,1152]{1,0:T(8,128)(2,1)S(1)}, bf16[36,1152]{1,0:T(8,128)(2,1)S(1)}, u32[]{:S(2)}, u32[]{:S(2)}) collective-permute-start(bf16[36,1152]{1,0:T(8,128)(2,1)S(1)} %fusion.34), channel_id=1, source_target_pairs={{0,1},{1,0},{2,3},{3,2},{4,5},{5,4},{6,7},{7,6},{8,9},{9,8},{10,11... | collective-permute-start | bytes 248840 | tf_op jit(solution)/shard_map/weight/ppermute | solution.py:20
  91.9 9.7 %collective-permute-start.6 = (bf16[128,1152]{1,0:T(8,128)(2,1)S(1)}, bf16[128,1152]{1,0:T(8,128)(2,1)S(1)}, u32[]{:S(2)}, u32[]{:S(2)}) collective-permute-start(bf16[128,1152]{1,0:T(8,128)(2,1)S(1)} %slice.158), channel_id=1, source_target_pairs={{0,16},{16,0},{1,17},{17,1},{2,18},{18,2},{3,19},{19,3},{4,20},{20... | collective-permute-start | bytes 884744 | tf_op jit(solution)/shard_map/hidden/ppermute | solution.py:20
  92.7 11.6 %collective-permute-start.22 = (bf16[9,1152]{1,0:T(8,128)(2,1)S(1)}, bf16[9,1152]{1,0:T(8,128)(2,1)S(1)}, u32[]{:S(2)}, u32[]{:S(2)}) collective-permute-start(bf16[9,1152]{1,0:T(8,128)(2,1)S(1)} %get-tuple-element.29), channel_id=1, source_target_pairs={{0,192},{64,128},{128,64},{192,0},{1,193},{65,129},{129,65},{193,1... | collective-permute-start | bytes 62216 | tf_op jit(solution)/shard_map/weight/ppermute | solution.py:20
  100.6 7.9 %collective-permute-start.20 = (bf16[9,1152]{1,0:T(8,128)(2,1)S(1)}, bf16[9,1152]{1,0:T(8,128)(2,1)S(1)}, u32[]{:S(2)}, u32[]{:S(2)}) collective-permute-start(bf16[9,1152]{1,0:T(8,128)(2,1)S(1)} %get-tuple-element.28), channel_id=1, source_target_pairs={{0,128},{64,192},{128,0},{192,64},{1,129},{65,193},{129,1},{193,65... | collective-permute-start | bytes 62216 | tf_op jit(solution)/shard_map/weight/ppermute | solution.py:20
  (14 other events, 98.9 us)

commit v2 on v1

v2 whole, which is shorter than its diff:
```python
import jax
import jax.numpy as jnp
import numpy as np
from jax import lax
from jax.experimental import pallas as pl
from jax.experimental.pallas import tpu as pltpu
from jax.sharding import Mesh, PartitionSpec as P

epsilon = 1e-06
AXES = ("zh", "x1", "x0", "y", "c", "zl")
f32 = jnp.float32
bf16 = jnp.bfloat16
ROWS = 128
WIDTH = 1152
VMEM = pl.BlockSpec(memory_space=pltpu.VMEM)
SMEM = pl.BlockSpec(memory_space=pltpu.SMEM)


def dot(a, b, ca, cb):
    return lax.dot_general(a, b, (((ca,), (cb,)), ((), ())), preferred_element_type=f32)


def xor(x, axis, step):
    size = lax.axis_size(axis)
    return lax.ppermute(x, axis, [(i, i ^ step) for i in range(size)])


def shape(dtype, *dims):
    return jax.ShapeDtypeStruct(dims, dtype)


def call(body, outs, specs, flops, moved, scratch=()):
    return pl.pallas_call(
        body,
        out_shape=outs,
        in_specs=specs,
        out_specs=[VMEM] * len(outs),
        scratch_shapes=scratch,
        compiler_params=pltpu.CompilerParams(vmem_limit_bytes=40 << 20),
        cost_estimate=pl.CostEstimate(flops=flops, bytes_accessed=moved, transcendentals=0),
    )


def prepare(count, hidden, text, hid_out, txt_out):
    keep = lax.broadcasted_iota(jnp.int32, (ROWS, 1), 0) < count[0]
    hid_out[...] = jnp.where(keep, hidden[...].astype(f32), 0.0).astype(bf16)
    txt = text[...].astype(f32)
    txt = txt * lax.rsqrt(jnp.sum(txt * txt, axis=1, keepdims=True) + epsilon)
    txt_out[...] = jnp.where(keep, txt, 0.0).astype(bf16)


def project(own, paired, cores, weight, places, embed, normed, inverse, turned):
    hid = jnp.concatenate([own[...], paired[...], cores[...]], 0)
    projected = dot(hid, weight[...], 1, 0)
    inv = lax.rsqrt(jnp.sum(projected * projected, axis=1, keepdims=True) + epsilon)
    unit = projected * inv
    normed[...] = unit
    embed[...] = unit.astype(bf16)
    inverse[...] = inv
    spots = lax.broadcasted_iota(jnp.int32, (576, WIDTH), 1)
    chosen = (spots == places[...]).astype(f32).astype(bf16)
    turned[...] = dot(chosen, hid, 1, 1).astype(bf16)


def tile(where, scalars, labels, embed, normed, inverse, t0, t1, t2, t3, coef_out, part_out, part_send):
    txt = jnp.concatenate([t0[...], t1[...], t2[...], t3[...]], 0)
    left = [
        jnp.transpose(jnp.broadcast_to(labels[pl.ds(where[k], 1), :], (8, ROWS)))[:, :1]
        for k in range(4)
    ]
    right = [labels[pl.ds(where[4 + k], 1), :] for k in range(4)]
    left = jnp.concatenate(left, 0)
    right = jnp.concatenate(right, 1)
    scores = scalars[0] * dot(embed[...], txt, 1, 1) + scalars[1]
    target = jnp.where(left == right, 1.0, -1.0).astype(f32)
    coef = (-target * jax.nn.sigmoid(-target * scores) * scalars[0]).astype(bf16)
    coef_out[...] = coef
    grad = dot(coef, txt, 1, 0)
    unit = normed[...]
    radial = jnp.sum(unit * grad, axis=1, keepdims=True)
    part = (grad - unit * radial) * inverse[...]
    part_out[...] = part
    part_send[...] = part.astype(bf16)


def text_terms(coef, embed, own, s1, s2, s3):
    terms = dot(coef[...], embed[...], 0, 0)
    own[...] = terms[:ROWS]
    for k, out in enumerate((s1, s2, s3)):
        out[...] = terms[(k + 1) * ROWS : (k + 2) * ROWS].astype(bf16)


def weight_terms(part, arrived, turned, own_rows, send_rows, own, s1, s2, s3):
    half = 2 * ROWS
    top = part[:half] + arrived[half:].astype(f32)
    low = part[half:] + arrived[:half].astype(f32)
    own_rows[...] = top[:ROWS]
    send_rows[...] = top[ROWS:].astype(bf16)
    summed = jnp.concatenate([top, low], 0).astype(bf16)
    terms = dot(turned[...], summed, 1, 0)
    own[...] = terms[:144]
    for k, out in enumerate((s1, s2, s3)):
        out[...] = terms[(k + 1) * 144 : (k + 2) * 144].astype(bf16)


def back(count, own, arrived, weight, out):
    rows = (own[...] + arrived[...].astype(f32)).astype(bf16)
    grad = dot(rows, weight[...], 1, 1)
    keep = lax.broadcasted_iota(jnp.int32, (ROWS, 1), 0) < count[0]
    out[...] = jnp.where(keep, grad, 0.0).astype(bf16)


def four(own, sends, axis):
    got = [xor(sends[k - 1], axis, k).astype(f32) for k in (2, 1, 3)]
    return own + got[0] + got[1] + got[2]


def per_device(hidden, weight, text, pair_ids, valid_count, logit_scale, logit_bias):
    zh, x1, x0, y, c = (lax.axis_index(a) for a in ("zh", "x1", "x0", "y", "c"))
    x = x1 * 2 + x0
    X = ("x1", "x0")
    block = ROWS * WIDTH
    labels = lax.dynamic_slice_in_dim(pair_ids[0], (zh * 2 + x1) * ROWS * 16, ROWS * 16, 0)
    labels = labels.reshape(16, ROWS)
    where = [(px * 4 + y) * 2 + pc for pc, px in ((c, x0), (c, 1 - x0), (1 - c, x0), (1 - c, 1 - x0))]
    where = jnp.stack(where + [(x0 * 4 + (y ^ j)) * 2 + c for j in range(4)]).astype(jnp.int32)
    scalars = jnp.stack([logit_scale, logit_bias])
    i = np.arange(576)
    places = (
        ((zh ^ jnp.asarray(i // 9 % 4)) * 288)
        + ((x ^ jnp.asarray(i // 144)) * 72)
        + ((y ^ jnp.asarray(i // 36 % 4)) * 18)
        + (c * 9 + jnp.asarray(i % 9))
    ).astype(jnp.int32)[:, None]
    with jax.named_scope("prepare"):
        hid, txt = call(
            prepare, [shape(bf16, ROWS, WIDTH)] * 2, [SMEM, VMEM, VMEM], block * 8, block * 8
        )(valid_count, hidden, text)
    with jax.named_scope("gather"):
        hid_x = xor(hid, "x0", 1)
        txt_2 = xor(txt, "y", 2)
        txt_1 = xor(txt, "y", 1)
        txt_3 = xor(txt, "y", 3)
        hid_c = xor(jnp.concatenate([hid, hid_x], 0), "c", 1)
    with jax.named_scope("project"):
        embed, normed, inverse, turned = call(
            project,
            [shape(bf16, 512, WIDTH), shape(f32, 512, WIDTH), shape(f32, 512, 1), shape(bf16, 576, 512)],
            [VMEM] * 5,
            2 * 512 * WIDTH * 1728,
            WIDTH * (WIDTH * 2 + 512 * 8),
        )(hid, hid_x, hid_c, weight, places)
    with jax.named_scope("tile"):
        coef, part, part_send = call(
            tile,
            [shape(bf16, 512, 512), shape(f32, 512, WIDTH), shape(bf16, 512, WIDTH)],
            [SMEM, SMEM] + [VMEM] * 8,
            4 * 512 * 512 * WIDTH,
            WIDTH * 512 * 14,
        )(where, scalars, labels, embed, normed, inverse, txt, txt_1, txt_2, txt_3)
    with jax.named_scope("core"):
        arrived = xor(part_send, "c", 1)
    with jax.named_scope("text"):
        txt_own, *txt_sends = call(
            text_terms,
            [shape(f32, ROWS, WIDTH)] + [shape(bf16, ROWS, WIDTH)] * 3,
            [VMEM] * 2,
            2 * 512 * 512 * WIDTH,
            WIDTH * 512 * 5,
        )(coef, embed)
    with jax.named_scope("weight"):
        own_rows, send_rows, own, *sends = call(
            weight_terms,
            [shape(f32, ROWS, WIDTH), shape(bf16, ROWS, WIDTH), shape(f32, 144, WIDTH)]
            + [shape(bf16, 144, WIDTH)] * 3,
            [VMEM] * 3,
            2 * 512 * 576 * WIDTH,
            WIDTH * 512 * 10,
        )(part, arrived, turned)
        whole = four(own, sends, X).reshape(4, 36, WIDTH)
        whole = four(whole[0], [whole[k].astype(bf16) for k in (1, 2, 3)], "y")
        whole = whole + xor(whole.astype(bf16), "zl", 1).astype(f32)
        whole = whole.reshape(4, 9, WIDTH)
        weight_grad = four(whole[0], [whole[k] for k in (1, 2, 3)], "zh")
    with jax.named_scope("hidden"):
        rows_x = xor(send_rows, "x0", 1)
        (hidden_grad,) = call(
            back,
            [shape(bf16, ROWS, WIDTH)],
            [SMEM] + [VMEM] * 3,
            2 * block * WIDTH,
            WIDTH * WIDTH * 2 + block * 8,
        )(valid_count, own_rows, rows_x, weight)
    with jax.named_scope("text"):
        keep = (jnp.arange(ROWS) < valid_count[0])[:, None]
        text_grad = jnp.where(keep, four(txt_own, txt_sends, "y"), 0.0)
    return hidden_grad, weight_grad, text_grad


def solution(mesh):
    fine = Mesh(mesh.devices.reshape(4, 2, 2, 4, 2, 2), AXES)
    blk = ("zh", "x1", "x0", "y", "c")
    by_row = P(("zl",) + blk, None)
    return jax.shard_map(
        per_device,
        mesh=fine,
        in_specs=(by_row, P(), by_row, P("zl", None), P(("zl",) + blk), P(), P()),
        out_specs=(by_row, P(blk, None), by_row),
        check_vma=False,
    )
```

time: 110 us -> 92.7 us (0.84)
  matrix products: 23.6 us -> 0 us
  waiting for transfers between devices: 22.1 us -> 38 us
  other arithmetic: 12.8 us -> 2.05 us
  Pallas kernels: 0 us -> 9.04 us
  starting transfers between devices: 41.5 us -> 36.6 us
  local copies, waits for them, and re-layouts: 6.09 us -> 3.99 us
    dot_general x7 -> x0, matrix products: 23.6 us -> none  [dot(): lax.dot_general(a, b, (((ca,), (cb,)), ((), ())), preferred_element_type=...]
    ppermute x26 -> x20, waiting for transfers between devices: 22.1 us -> 38 us  [xor(): return lax.ppermute(x, axis, [(i, i ^ step) for i in range(size)])]
    pallas_call x0 -> x6, Pallas kernels: none -> 9.04 us  [the longest x1 2.81 us: per_device(): call(project, [shape(bf16, 512, WIDTH), shape(f32, 512, WIDTH), shape(f32...]
    slice x8 -> x2, local copies, waits for them, and re-layouts: 5.29 us -> 0.07 us  [the longest x1 0.05 us: per_device(): whole = four(whole[0], [whole[k].astype(bf16) for k in (1, 2, 3)], 'y')]
    ppermute x26 -> x20, starting transfers between devices: 41.5 us -> 36.6 us  [xor(): return lax.ppermute(x, axis, [(i, i ^ step) for i in range(size)])]
    convert_element_type x2 -> x0, other arithmetic: 4.2 us -> none  [the longest x1 2.42 us: per_device(): summed_b = summed.astype(bf16)]
    unnamed x24 -> x18, local copies, waits for them, and re-layouts: 0.07 us -> 3.7 us
    select_n x2 -> x1, other arithmetic: 3.36 us -> 0.98 us  [per_device(): text_grad = jnp.where(keep, four(txt_own, txt_sends, 'y'), 0.0)]
  transfers between devices with their start and end apart: 26 -> 20, of which waited for: 12 -> 10; matrix products, arithmetic and copies ran while one was open for 28% -> 1% of each run, Pallas kernels for 0% -> 6%
where the time goes in v2:
time: 92.7 us; the launch traced here: 92.4 us
  waiting for transfers between devices  38 us (41%)
  starting transfers between devices  36.6 us (39%)
  Pallas kernels  9.04 us (10%)
  local copies, waits for them, and re-layouts  3.99 us (4%)
  between operations  2.81 us (3%)
  other arithmetic  2.05 us (2%)
    ppermute x20, waiting for transfers between devices, xor(): return lax.ppermute(x, axis, [(i, i ^ step) for i in range(size)])  38 us
    ppermute x20, starting transfers between devices, xor(): return lax.ppermute(x, axis, [(i, i ^ step) for i in range(size)])  36.6 us
    unnamed x18, local copies, waits for them, and re-layouts  3.7 us
    pallas_call x1, Pallas kernels, per_device(): call(project, [shape(bf16, 512, WIDTH), shape(f32, 512, WIDTH), shape(f32...  2.81 us
    pallas_call x1, Pallas kernels, per_device(): call(tile, [shape(bf16, 512, 512), shape(f32, 512, WIDTH), shape(bf16, 51...  2.57 us
  transfers between devices with their start and end apart: 20, of which 10 were waited for; matrix products, arithmetic and copies ran while one was open for 1% of the time, Pallas kernels for 6%

profile of v2, /device:TPU:2, one launch (start us, length us, event | category | flops | bytes accessed | tf_op | source)
XLA Modules:
  0.0 92.4 jit_solution(14045168312552267243)
XLA Ops:
  3.5 2.4 %collective-permute-start = (bf16[128,1152]{1,0:T(8,128)(2,1)S(1)}, bf16[128,1152]{1,0:T(8,128)(2,1)S(1)}, u32[]{:S(2)}, u32[]{:S(2)}) collective-permute-start(bf16[128,1152]{1,0:T(8,128)(2,1)S(1)} %get-tuple-element.22.own), channel_id=1, source_target_pairs={{0,16},{16,0},{1,17},{17,1},{2,18},{18,2},{3,19},{19,3},{4,20},{20... | collective-permute-start | bytes 884744 | tf_op jit(solution)/shard_map/gather/ppermute | solution.py:25
  5.8 6.5 %collective-permute-done.paired = bf16[128,1152]{1,0:T(8,128)(2,1)S(1)} collective-permute-done((bf16[128,1152]{1,0:T(8,128)(2,1)S(1)}, bf16[128,1152]{1,0:T(8,128)(2,1)S(1)}, u32[]{:S(2)}, u32[]{:S(2)}) %collective-permute-start) | collective-permute-done | bytes 294944 | tf_op jit(solution)/shard_map/gather/ppermute | solution.py:25
  12.5 1.7 %collective-permute-start.2 = (bf16[128,1152]{1,0:T(8,128)(2,1)S(1)}, bf16[128,1152]{1,0:T(8,128)(2,1)S(1)}, u32[]{:S(2)}, u32[]{:S(2)}) collective-permute-start(bf16[128,1152]{1,0:T(8,128)(2,1)S(1)} %get-tuple-element.26.t0), channel_id=1, source_target_pairs={{0,4},{4,0},{8,12},{12,8},{1,5},{5,1},{9,13},{13,9},{2,6},{6,2},{1... | collective-permute-start | bytes 884744 | tf_op jit(solution)/shard_map/gather/ppermute | solution.py:25
  14.1 2.9 %collective-permute-start.3 = (bf16[128,1152]{1,0:T(8,128)(2,1)S(1)}, bf16[128,1152]{1,0:T(8,128)(2,1)S(1)}, u32[]{:S(2)}, u32[]{:S(2)}) collective-permute-start(bf16[128,1152]{1,0:T(8,128)(2,1)S(1)} %get-tuple-element.26.t0), channel_id=1, source_target_pairs={{0,8},{4,12},{8,0},{12,4},{1,9},{5,13},{9,1},{13,5},{2,10},{6,14},... | collective-permute-start | bytes 884744 | tf_op jit(solution)/shard_map/gather/ppermute | solution.py:25
  18.9 1.7 %copy-done.1 = bf16[1152,1152]{1,0:T(8,128)(2,1)S(1)} copy-done((bf16[1152,1152]{1,0:T(8,128)(2,1)S(1)}, bf16[1152,1152]{1,0:T(8,128)(2,1)}, u32[]{:S(2)}) %copy-start.1) | copy-done | bytes 2654232
  20.7 2.8 %project.1 = (bf16[512,1152]{1,0:T(8,128)(2,1)S(1)}, f32[512,1152]{1,0:T(8,128)S(1)}, f32[512,1]{1,0:T(8,128)S(1)}, bf16[576,512]{1,0:T(8,128)(2,1)S(1)}) custom-call(bf16[128,1152]{1,0:T(8,128)(2,1)S(1)} %get-tuple-element.22.own, bf16[128,1152]{1,0:T(8,128)(2,1)S(1)} %collective-permute-done.paired, bf16[256,1152]{1,0:T(8,128)(2,1)S(1)} %collective-permute-done.1.cores, ...), custom_call_target="tpu_custom_call" | custom-call | flops 2038431744 | bytes 7372800 | tf_op jit(solution)/shard_map/project/pallas_call | solution.py:146
  23.5 7.3 %collective-permute-done.3.t2 = bf16[128,1152]{1,0:T(8,128)(2,1)S(1)} collective-permute-done((bf16[128,1152]{1,0:T(8,128)(2,1)S(1)}, bf16[128,1152]{1,0:T(8,128)(2,1)S(1)}, u32[]{:S(2)}, u32[]{:S(2)}) %collective-permute-start.3) | collective-permute-done | bytes 294944 | tf_op jit(solution)/shard_map/gather/ppermute | solution.py:25
  30.8 2.6 %collective-permute-done.4.t3 = bf16[128,1152]{1,0:T(8,128)(2,1)S(1)} collective-permute-done((bf16[128,1152]{1,0:T(8,128)(2,1)S(1)}, bf16[128,1152]{1,0:T(8,128)(2,1)S(1)}, u32[]{:S(2)}, u32[]{:S(2)}) %collective-permute-start.4) | collective-permute-done | bytes 294944 | tf_op jit(solution)/shard_map/gather/ppermute | solution.py:25
  33.3 2.6 %tile.1 = (bf16[512,512]{1,0:T(8,128)(2,1)S(1)}, f32[512,1152]{1,0:T(8,128)S(1)}, bf16[512,1152]{1,0:T(8,128)(2,1)S(1)}) custom-call(s32[8]{0:T(128)S(1)} %stack.41.where, f32[2]{0:T(128)S(1)} %pad_maximum_fusion.1.scalars, s32[16,128]{1,0:T(8,128)S(1)} %bitcast.14, bf16[512,1152]{1,0:T(8,128)(2,1)S(1)} %get-tuple-element.23.embed, ...), custom_call_target="tpu_custom_call" | custom-call | flops 1207959552 | bytes 8257536 | tf_op jit(solution)/shard_map/tile/pallas_call | solution.py:154
  36.0 2.8 %collective-permute-done.5.arrived = bf16[512,1152]{1,0:T(8,128)(2,1)S(1)} collective-permute-done((bf16[512,1152]{1,0:T(8,128)(2,1)S(1)}, bf16[512,1152]{1,0:T(8,128)(2,1)S(1)}, u32[]{:S(2)}, u32[]{:S(2)}) %collective-permute-start.5) | collective-permute-done | bytes 1179680 | tf_op jit(solution)/shard_map/core/ppermute | solution.py:25
  39.8 2.2 %collective-permute-start.7 = (bf16[144,1152]{1,0:T(8,128)(2,1)S(1)}, bf16[144,1152]{1,0:T(8,128)(2,1)S(1)}, u32[]{:S(2)}, u32[]{:S(2)}) collective-permute-start(bf16[144,1152]{1,0:T(8,128)(2,1)S(1)} %get-tuple-element.33), channel_id=1, source_target_pairs={{0,32},{16,48},{32,0},{48,16},{1,33},{17,49},{33,1},{49,17},{2,34}... | collective-permute-start | bytes 995336 | tf_op jit(solution)/shard_map/weight/ppermute | solution.py:25
  42.1 1.4 %collective-permute-start.8 = (bf16[144,1152]{1,0:T(8,128)(2,1)S(1)}, bf16[144,1152]{1,0:T(8,128)(2,1)S(1)}, u32[]{:S(2)}, u32[]{:S(2)}) collective-permute-start(bf16[144,1152]{1,0:T(8,128)(2,1)S(1)} %get-tuple-element.34), channel_id=1, source_target_pairs={{0,16},{16,0},{32,48},{48,32},{1,17},{17,1},{33,49},{49,33},{2,18}... | collective-permute-start | bytes 995336 | tf_op jit(solution)/shard_map/weight/ppermute | solution.py:25
  44.0 8.1 %collective-permute-done.7 = bf16[144,1152]{1,0:T(8,128)(2,1)S(1)} collective-permute-done((bf16[144,1152]{1,0:T(8,128)(2,1)S(1)}, bf16[144,1152]{1,0:T(8,128)(2,1)S(1)}, u32[]{:S(2)}, u32[]{:S(2)}) %collective-permute-start.7) | collective-permute-done | bytes 331808 | tf_op jit(solution)/shard_map/weight/ppermute | solution.py:25
  52.1 6.3 %collective-permute-done.8 = bf16[144,1152]{1,0:T(8,128)(2,1)S(1)} collective-permute-done((bf16[144,1152]{1,0:T(8,128)(2,1)S(1)}, bf16[144,1152]{1,0:T(8,128)(2,1)S(1)}, u32[]{:S(2)}, u32[]{:S(2)}) %collective-permute-start.8) | collective-permute-done | bytes 331808 | tf_op jit(solution)/shard_map/weight/ppermute | solution.py:25
  58.8 1.1 %collective-permute-start.11 = (bf16[36,1152]{1,0:T(8,128)(2,1)S(1)}, bf16[36,1152]{1,0:T(8,128)(2,1)S(1)}, u32[]{:S(2)}, u32[]{:S(2)}) collective-permute-start(bf16[36,1152]{1,0:T(8,128)(2,1)S(1)} %get-tuple-element.45), channel_id=1, source_target_pairs={{0,4},{4,0},{8,12},{12,8},{1,5},{5,1},{9,13},{13,9},{2,6},{6,2},{1... | collective-permute-start | bytes 248840 | tf_op jit(solution)/shard_map/weight/ppermute | solution.py:25
  59.9 2.9 %collective-permute-start.12 = (bf16[36,1152]{1,0:T(8,128)(2,1)S(1)}, bf16[36,1152]{1,0:T(8,128)(2,1)S(1)}, u32[]{:S(2)}, u32[]{:S(2)}) collective-permute-start(bf16[36,1152]{1,0:T(8,128)(2,1)S(1)} %get-tuple-element.44), channel_id=1, source_target_pairs={{0,12},{4,8},{8,4},{12,0},{1,13},{5,9},{9,5},{13,1},{2,14},{6,10},... | collective-permute-start | bytes 248840 | tf_op jit(solution)/shard_map/weight/ppermute | solution.py:25
  62.9 2.9 %collective-permute-done.10 = bf16[36,1152]{1,0:T(8,128)(2,1)S(1)} collective-permute-done((bf16[36,1152]{1,0:T(8,128)(2,1)S(1)}, bf16[36,1152]{1,0:T(8,128)(2,1)S(1)}, u32[]{:S(2)}, u32[]{:S(2)}) %collective-permute-start.10) | collective-permute-done | bytes 82976 | tf_op jit(solution)/shard_map/weight/ppermute | solution.py:25
  66.8 2.0 %collective-permute-start.13 = (bf16[36,1152]{1,0:T(8,128)(2,1)S(1)}, bf16[36,1152]{1,0:T(8,128)(2,1)S(1)}, u32[]{:S(2)}, u32[]{:S(2)}) collective-permute-start(bf16[36,1152]{1,0:T(8,128)(2,1)S(1)} %fusion.4), channel_id=1, source_target_pairs={{0,1},{1,0},{2,3},{3,2},{4,5},{5,4},{6,7},{7,6},{8,9},{9,8},{10,11... | collective-permute-start | bytes 248840 | tf_op jit(solution)/shard_map/weight/ppermute | solution.py:25
  70.2 2.3 %collective-permute-start.18 = (bf16[128,1152]{1,0:T(8,128)(2,1)S(1)}, bf16[128,1152]{1,0:T(8,128)(2,1)S(1)}, u32[]{:S(2)}, u32[]{:S(2)}) collective-permute-start(bf16[128,1152]{1,0:T(8,128)(2,1)S(1)} %get-tuple-element.39), channel_id=1, source_target_pairs={{0,4},{4,0},{8,12},{12,8},{1,5},{5,1},{9,13},{13,9},{2,6},{6,2},{1... | collective-permute-start | bytes 884744 | tf_op jit(solution)/shard_map/text/ppermute | solution.py:25
  72.5 1.4 %collective-permute-start.19 = (bf16[128,1152]{1,0:T(8,128)(2,1)S(1)}, bf16[128,1152]{1,0:T(8,128)(2,1)S(1)}, u32[]{:S(2)}, u32[]{:S(2)}) collective-permute-start(bf16[128,1152]{1,0:T(8,128)(2,1)S(1)} %get-tuple-element.40), channel_id=1, source_target_pairs={{0,12},{4,8},{8,4},{12,0},{1,13},{5,9},{9,5},{13,1},{2,14},{6,10},... | collective-permute-start | bytes 884744 | tf_op jit(solution)/shard_map/text/ppermute | solution.py:25
  74.5 6.4 %collective-permute-start.14 = (f32[9,1152]{1,0:T(8,128)S(1)}, f32[9,1152]{1,0:T(8,128)S(1)}, u32[]{:S(2)}, u32[]{:S(2)}) collective-permute-start(f32[9,1152]{1,0:T(8,128)S(1)} %get-tuple-element.46), channel_id=1, source_target_pairs={{0,128},{64,192},{128,0},{192,64},{1,129},{65,193},{129,1},{193,65... | collective-permute-start | bytes 124424 | tf_op jit(solution)/shard_map/weight/ppermute | solution.py:25
  81.3 3.3 %collective-permute-start.15 = (f32[9,1152]{1,0:T(8,128)S(1)}, f32[9,1152]{1,0:T(8,128)S(1)}, u32[]{:S(2)}, u32[]{:S(2)}) collective-permute-start(f32[9,1152]{1,0:T(8,128)S(1)} %get-tuple-element.48), channel_id=1, source_target_pairs={{0,64},{64,0},{128,192},{192,128},{1,65},{65,1},{129,193},{193,129... | collective-permute-start | bytes 124424 | tf_op jit(solution)/shard_map/weight/ppermute | solution.py:25
  84.6 4.5 %collective-permute-start.16 = (f32[9,1152]{1,0:T(8,128)S(1)}, f32[9,1152]{1,0:T(8,128)S(1)}, u32[]{:S(2)}, u32[]{:S(2)}) collective-permute-start(f32[9,1152]{1,0:T(8,128)S(1)} %get-tuple-element.47), channel_id=1, source_target_pairs={{0,192},{64,128},{128,64},{192,0},{1,193},{65,129},{129,65},{193,1... | collective-permute-start | bytes 124424 | tf_op jit(solution)/shard_map/weight/ppermute | solution.py:25
  90.1 1.6 %hidden.3 = bf16[128,1152]{1,0:T(8,128)(2,1)} custom-call(s32[1]{0:T(128)} %copy.15.count, f32[128,1152]{1,0:T(8,128)S(1)} %get-tuple-element.30.own, bf16[128,1152]{1,0:T(8,128)(2,1)S(1)} %collective-permute-done.6.arrived, bf16[1152,1152]{1,0:T(8,128)(2,1)S(1)} %copy-done.2), custom_call_target="tpu_custom_call" | custom-call | flops 339738624 | bytes 3833856 | tf_op jit(solution)/shard_map/hidden/pallas_call | solution.py:187
  (54 shorter events, 9.8 us)
Async XLA Ops:
  0.6 18.2 %copy-start = (s32[1,16384]{1,0:T(1,128)S(1)}, s32[1,16384]{1,0:T(1,128)}, u32[]{:S(2)}) copy-start(s32[1,16384]{1,0:T(1,128)} %param.14) | copy-start | bytes 196612
  0.6 16.6 %copy-start.5 = (s32[576]{0:T(1024)S(1)}, s32[576]{0:T(1024)}, u32[]{:S(2)}) copy-start(s32[576]{0:T(1024)} %constant.56.clone) | copy-start | bytes 6916
  0.7 16.6 %copy-start.6 = (s32[576]{0:T(1024)S(1)}, s32[576]{0:T(1024)}, u32[]{:S(2)}) copy-start(s32[576]{0:T(1024)} %constant.57.clone) | copy-start | bytes 6916
  0.7 16.6 %copy-start.7 = (s32[576]{0:T(1024)S(1)}, s32[576]{0:T(1024)}, u32[]{:S(2)}) copy-start(s32[576]{0:T(1024)} %constant.58.clone) | copy-start | bytes 6916
  3.5 8.8 %collective-permute-start = (bf16[128,1152]{1,0:T(8,128)(2,1)S(1)}, bf16[128,1152]{1,0:T(8,128)(2,1)S(1)}, u32[]{:S(2)}, u32[]{:S(2)}) collective-permute-start(bf16[128,1152]{1,0:T(8,128)(2,1)S(1)} %get-tuple-element.22.own), channel_id=1, source_target_pairs={{0,16},{16,0},{1,17},{17,1},{2,18},{18,2},{3,19},{19,3},{4,20},{20... | collective-permute-start | bytes 884744 | tf_op jit(solution)/shard_map/gather/ppermute | solution.py:25
  12.4 6.5 %collective-permute-start.1 = (bf16[256,1152]{1,0:T(8,128)(2,1)S(1)}, bf16[256,1152]{1,0:T(8,128)(2,1)S(1)}, u32[]{:S(2)}, u32[]{:S(2)}) collective-permute-start(bf16[256,1152]{1,0:T(8,128)(2,1)S(1)} %pad_maximum_fusion), channel_id=1, source_target_pairs={{0,2},{2,0},{1,3},{3,1},{4,6},{6,4},{5,7},{7,5},{8,10},{10,8},{9,1... | collective-permute-start | bytes 1769480 | tf_op jit(solution)/shard_map/gather/ppermute | solution.py:25
  12.5 11.0 %collective-permute-start.2 = (bf16[128,1152]{1,0:T(8,128)(2,1)S(1)}, bf16[128,1152]{1,0:T(8,128)(2,1)S(1)}, u32[]{:S(2)}, u32[]{:S(2)}) collective-permute-start(bf16[128,1152]{1,0:T(8,128)(2,1)S(1)} %get-tuple-element.26.t0), channel_id=1, source_target_pairs={{0,4},{4,0},{8,12},{12,8},{1,5},{5,1},{9,13},{13,9},{2,6},{6,2},{1... | collective-permute-start | bytes 884744 | tf_op jit(solution)/shard_map/gather/ppermute | solution.py:25
  14.1 16.6 %collective-permute-start.3 = (bf16[128,1152]{1,0:T(8,128)(2,1)S(1)}, bf16[128,1152]{1,0:T(8,128)(2,1)S(1)}, u32[]{:S(2)}, u32[]{:S(2)}) collective-permute-start(bf16[128,1152]{1,0:T(8,128)(2,1)S(1)} %get-tuple-element.26.t0), channel_id=1, source_target_pairs={{0,8},{4,12},{8,0},{12,4},{1,9},{5,13},{9,1},{13,5},{2,10},{6,14},... | collective-permute-start | bytes 884744 | tf_op jit(solution)/shard_map/gather/ppermute | solution.py:25
  17.0 16.3 %collective-permute-start.4 = (bf16[128,1152]{1,0:T(8,128)(2,1)S(1)}, bf16[128,1152]{1,0:T(8,128)(2,1)S(1)}, u32[]{:S(2)}, u32[]{:S(2)}) collective-permute-start(bf16[128,1152]{1,0:T(8,128)(2,1)S(1)} %get-tuple-element.26.t0), channel_id=1, source_target_pairs={{0,12},{4,8},{8,4},{12,0},{1,13},{5,9},{9,5},{13,1},{2,14},{6,10},... | collective-permute-start | bytes 884744 | tf_op jit(solution)/shard_map/gather/ppermute | solution.py:25
  35.9 2.9 %collective-permute-start.5 = (bf16[512,1152]{1,0:T(8,128)(2,1)S(1)}, bf16[512,1152]{1,0:T(8,128)(2,1)S(1)}, u32[]{:S(2)}, u32[]{:S(2)}) collective-permute-start(bf16[512,1152]{1,0:T(8,128)(2,1)S(1)} %get-tuple-element.28), channel_id=1, source_target_pairs={{0,2},{2,0},{1,3},{3,1},{4,6},{6,4},{5,7},{7,5},{8,10},{10,8},{9,1... | collective-permute-start | bytes 3538952 | tf_op jit(solution)/shard_map/core/ppermute | solution.py:25
  39.8 12.3 %collective-permute-start.7 = (bf16[144,1152]{1,0:T(8,128)(2,1)S(1)}, bf16[144,1152]{1,0:T(8,128)(2,1)S(1)}, u32[]{:S(2)}, u32[]{:S(2)}) collective-permute-start(bf16[144,1152]{1,0:T(8,128)(2,1)S(1)} %get-tuple-element.33), channel_id=1, source_target_pairs={{0,32},{16,48},{32,0},{48,16},{1,33},{17,49},{33,1},{49,17},{2,34}... | collective-permute-start | bytes 995336 | tf_op jit(solution)/shard_map/weight/ppermute | solution.py:25
  42.1 16.4 %collective-permute-start.8 = (bf16[144,1152]{1,0:T(8,128)(2,1)S(1)}, bf16[144,1152]{1,0:T(8,128)(2,1)S(1)}, u32[]{:S(2)}, u32[]{:S(2)}) collective-permute-start(bf16[144,1152]{1,0:T(8,128)(2,1)S(1)} %get-tuple-element.34), channel_id=1, source_target_pairs={{0,16},{16,0},{32,48},{48,32},{1,17},{17,1},{33,49},{49,33},{2,18}... | collective-permute-start | bytes 995336 | tf_op jit(solution)/shard_map/weight/ppermute | solution.py:25
  43.5 15.0 %collective-permute-start.9 = (bf16[144,1152]{1,0:T(8,128)(2,1)S(1)}, bf16[144,1152]{1,0:T(8,128)(2,1)S(1)}, u32[]{:S(2)}, u32[]{:S(2)}) collective-permute-start(bf16[144,1152]{1,0:T(8,128)(2,1)S(1)} %get-tuple-element.35), channel_id=1, source_target_pairs={{0,48},{16,32},{32,16},{48,0},{1,49},{17,33},{33,17},{49,1},{2,50}... | collective-permute-start | bytes 995336 | tf_op jit(solution)/shard_map/weight/ppermute | solution.py:25
  58.7 7.1 %collective-permute-start.10 = (bf16[36,1152]{1,0:T(8,128)(2,1)S(1)}, bf16[36,1152]{1,0:T(8,128)(2,1)S(1)}, u32[]{:S(2)}, u32[]{:S(2)}) collective-permute-start(bf16[36,1152]{1,0:T(8,128)(2,1)S(1)} %get-tuple-element.43), channel_id=1, source_target_pairs={{0,8},{4,12},{8,0},{12,4},{1,9},{5,13},{9,1},{13,5},{2,10},{6,14},... | collective-permute-start | bytes 248840 | tf_op jit(solution)/shard_map/weight/ppermute | solution.py:25
  58.8 7.0 %collective-permute-start.11 = (bf16[36,1152]{1,0:T(8,128)(2,1)S(1)}, bf16[36,1152]{1,0:T(8,128)(2,1)S(1)}, u32[]{:S(2)}, u32[]{:S(2)}) collective-permute-start(bf16[36,1152]{1,0:T(8,128)(2,1)S(1)} %get-tuple-element.45), channel_id=1, source_target_pairs={{0,4},{4,0},{8,12},{12,8},{1,5},{5,1},{9,13},{13,9},{2,6},{6,2},{1... | collective-permute-start | bytes 248840 | tf_op jit(solution)/shard_map/weight/ppermute | solution.py:25
  59.9 6.8 %collective-permute-start.12 = (bf16[36,1152]{1,0:T(8,128)(2,1)S(1)}, bf16[36,1152]{1,0:T(8,128)(2,1)S(1)}, u32[]{:S(2)}, u32[]{:S(2)}) collective-permute-start(bf16[36,1152]{1,0:T(8,128)(2,1)S(1)} %get-tuple-element.44), channel_id=1, source_target_pairs={{0,12},{4,8},{8,4},{12,0},{1,13},{5,9},{9,5},{13,1},{2,14},{6,10},... | collective-permute-start | bytes 248840 | tf_op jit(solution)/shard_map/weight/ppermute | solution.py:25
  66.8 7.6 %collective-permute-start.13 = (bf16[36,1152]{1,0:T(8,128)(2,1)S(1)}, bf16[36,1152]{1,0:T(8,128)(2,1)S(1)}, u32[]{:S(2)}, u32[]{:S(2)}) collective-permute-start(bf16[36,1152]{1,0:T(8,128)(2,1)S(1)} %fusion.4), channel_id=1, source_target_pairs={{0,1},{1,0},{2,3},{3,2},{4,5},{5,4},{6,7},{7,6},{8,9},{9,8},{10,11... | collective-permute-start | bytes 248840 | tf_op jit(solution)/shard_map/weight/ppermute | solution.py:25
  69.7 11.6 %collective-permute-start.17 = (bf16[128,1152]{1,0:T(8,128)(2,1)S(1)}, bf16[128,1152]{1,0:T(8,128)(2,1)S(1)}, u32[]{:S(2)}, u32[]{:S(2)}) collective-permute-start(bf16[128,1152]{1,0:T(8,128)(2,1)S(1)} %get-tuple-element.38), channel_id=1, source_target_pairs={{0,8},{4,12},{8,0},{12,4},{1,9},{5,13},{9,1},{13,5},{2,10},{6,14},... | collective-permute-start | bytes 884744 | tf_op jit(solution)/shard_map/text/ppermute | solution.py:25
  70.2 14.4 %collective-permute-start.18 = (bf16[128,1152]{1,0:T(8,128)(2,1)S(1)}, bf16[128,1152]{1,0:T(8,128)(2,1)S(1)}, u32[]{:S(2)}, u32[]{:S(2)}) collective-permute-start(bf16[128,1152]{1,0:T(8,128)(2,1)S(1)} %get-tuple-element.39), channel_id=1, source_target_pairs={{0,4},{4,0},{8,12},{12,8},{1,5},{5,1},{9,13},{13,9},{2,6},{6,2},{1... | collective-permute-start | bytes 884744 | tf_op jit(solution)/shard_map/text/ppermute | solution.py:25
  72.5 16.6 %collective-permute-start.19 = (bf16[128,1152]{1,0:T(8,128)(2,1)S(1)}, bf16[128,1152]{1,0:T(8,128)(2,1)S(1)}, u32[]{:S(2)}, u32[]{:S(2)}) collective-permute-start(bf16[128,1152]{1,0:T(8,128)(2,1)S(1)} %get-tuple-element.40), channel_id=1, source_target_pairs={{0,12},{4,8},{8,4},{12,0},{1,13},{5,9},{9,5},{13,1},{2,14},{6,10},... | collective-permute-start | bytes 884744 | tf_op jit(solution)/shard_map/text/ppermute | solution.py:25
  73.9 16.2 %collective-permute-start.6 = (bf16[128,1152]{1,0:T(8,128)(2,1)S(1)}, bf16[128,1152]{1,0:T(8,128)(2,1)S(1)}, u32[]{:S(2)}, u32[]{:S(2)}) collective-permute-start(bf16[128,1152]{1,0:T(8,128)(2,1)S(1)} %get-tuple-element.31), channel_id=1, source_target_pairs={{0,16},{16,0},{1,17},{17,1},{2,18},{18,2},{3,19},{19,3},{4,20},{20... | collective-permute-start | bytes 884744 | tf_op jit(solution)/shard_map/hidden/ppermute | solution.py:25
  74.5 17.2 %collective-permute-start.14 = (f32[9,1152]{1,0:T(8,128)S(1)}, f32[9,1152]{1,0:T(8,128)S(1)}, u32[]{:S(2)}, u32[]{:S(2)}) collective-permute-start(f32[9,1152]{1,0:T(8,128)S(1)} %get-tuple-element.46), channel_id=1, source_target_pairs={{0,128},{64,192},{128,0},{192,64},{1,129},{65,193},{129,1},{193,65... | collective-permute-start | bytes 124424 | tf_op jit(solution)/shard_map/weight/ppermute | solution.py:25
  81.3 10.4 %collective-permute-start.15 = (f32[9,1152]{1,0:T(8,128)S(1)}, f32[9,1152]{1,0:T(8,128)S(1)}, u32[]{:S(2)}, u32[]{:S(2)}) collective-permute-start(f32[9,1152]{1,0:T(8,128)S(1)} %get-tuple-element.48), channel_id=1, source_target_pairs={{0,64},{64,0},{128,192},{192,128},{1,65},{65,1},{129,193},{193,129... | collective-permute-start | bytes 124424 | tf_op jit(solution)/shard_map/weight/ppermute | solution.py:25
  84.6 7.2 %collective-permute-start.16 = (f32[9,1152]{1,0:T(8,128)S(1)}, f32[9,1152]{1,0:T(8,128)S(1)}, u32[]{:S(2)}, u32[]{:S(2)}) collective-permute-start(f32[9,1152]{1,0:T(8,128)S(1)} %get-tuple-element.47), channel_id=1, source_target_pairs={{0,192},{64,128},{128,64},{192,0},{1,193},{65,129},{129,65},{193,1... | collective-permute-start | bytes 124424 | tf_op jit(solution)/shard_map/weight/ppermute | solution.py:25
  (5 other events, 33.3 us)

commit v3 on v2

v3 whole, which is shorter than its diff:
```python
import jax
import jax.numpy as jnp
import numpy as np
from jax import lax
from jax.experimental import pallas as pl
from jax.experimental.pallas import tpu as pltpu
from jax.sharding import Mesh, PartitionSpec as P

epsilon = 1e-06
AXES = ("zh", "x1", "x0", "y", "c", "zl")
f32 = jnp.float32
bf16 = jnp.bfloat16
ROWS = 128
WIDTH = 1152
VMEM = pl.BlockSpec(memory_space=pltpu.VMEM)
SMEM = pl.BlockSpec(memory_space=pltpu.SMEM)
HBM = pl.BlockSpec(memory_space=pltpu.HBM)


def dot(a, b, ca, cb):
    return lax.dot_general(a, b, (((ca,), (cb,)), ((), ())), preferred_element_type=f32)


def xor(x, axis, step):
    size = lax.axis_size(axis)
    return lax.ppermute(x, axis, [(i, i ^ step) for i in range(size)])


def shape(dtype, *dims):
    return jax.ShapeDtypeStruct(dims, dtype)


def in_hbm(x):
    return pltpu.with_memory_space_constraint(x, pltpu.HBM)


def call(body, outs, specs, flops, moved, scratch=()):
    return pl.pallas_call(
        body,
        out_shape=outs,
        in_specs=specs,
        out_specs=[VMEM] * len(outs),
        scratch_shapes=scratch,
        compiler_params=pltpu.CompilerParams(vmem_limit_bytes=40 << 20),
        cost_estimate=pl.CostEstimate(flops=flops, bytes_accessed=moved, transcendentals=0),
    )


def prepare(count, hidden, text, hid_out, txt_out, hid_in, txt_in, sems):
    copies = [
        pltpu.make_async_copy(text, txt_in, sems.at[0]),
        pltpu.make_async_copy(hidden, hid_in, sems.at[1]),
    ]
    for copy in copies:
        copy.start()
    keep = lax.broadcasted_iota(jnp.int32, (ROWS, 1), 0) < count[0]
    copies[0].wait()
    txt = txt_in[...].astype(f32)
    txt = txt * lax.rsqrt(jnp.sum(txt * txt, axis=1, keepdims=True) + epsilon)
    txt_out[...] = jnp.where(keep, txt, 0.0).astype(bf16)
    copies[1].wait()
    hid_out[...] = jnp.where(keep, hid_in[...].astype(f32), 0.0).astype(bf16)


def join(own, paired, t1, t3, both, first, second):
    both[:ROWS] = own[...]
    both[ROWS:] = paired[...]
    first[...] = t3[: ROWS // 2]
    second[...] = t1[ROWS // 2 :]


def project(both, cores, weight, places, embed, normed, inverse, turned, held, sem):
    copy = pltpu.make_async_copy(weight, held, sem)
    copy.start()
    hid = jnp.concatenate([both[...], cores[...]], 0)
    spots = lax.broadcasted_iota(jnp.int32, (576, WIDTH), 1)
    chosen = (spots == places[...]).astype(f32).astype(bf16)
    turned[...] = dot(chosen, hid, 1, 1).astype(bf16)
    copy.wait()
    projected = dot(hid, held[...], 1, 0)
    inv = lax.rsqrt(jnp.sum(projected * projected, axis=1, keepdims=True) + epsilon)
    unit = projected * inv
    normed[...] = unit
    embed[...] = unit.astype(bf16)
    inverse[...] = inv


def tile(where, scalars, labels, embed, normed, inverse, t0, t1, t2a, t2b, t3, coef_out, part_out, part_send):
    txt = jnp.concatenate([t0[...], t1[...], t2a[...], t2b[...], t3[...]], 0)
    left = [
        jnp.transpose(jnp.broadcast_to(labels[pl.ds(where[k], 1), :], (8, ROWS)))[:, :1]
        for k in range(4)
    ]
    right = [labels[pl.ds(where[4 + k], 1), :] for k in range(4)]
    left = jnp.concatenate(left, 0)
    right = jnp.concatenate(right, 1)
    scores = scalars[0] * dot(embed[...], txt, 1, 1) + scalars[1]
    target = jnp.where(left == right, 1.0, -1.0).astype(f32)
    coef = (-target * jax.nn.sigmoid(-target * scores) * scalars[0]).astype(bf16)
    coef_out[...] = coef
    grad = dot(coef, txt, 1, 0)
    unit = normed[...]
    radial = jnp.sum(unit * grad, axis=1, keepdims=True)
    part = (grad - unit * radial) * inverse[...]
    part_out[...] = part
    part_send[...] = part.astype(bf16)


def text_terms(coef, embed, terms):
    terms[...] = dot(coef[...], embed[...], 0, 0)


def weight_terms(part, arrived, turned, terms, rows, own, s1, s2, s3, t1, t2):
    half = 2 * ROWS
    top = part[:half] + arrived[half:].astype(f32)
    low = part[half:] + arrived[:half].astype(f32)
    rows[...] = top
    summed = jnp.concatenate([top, low], 0).astype(bf16)
    grad = dot(turned[...], summed, 1, 0)
    own[...] = grad[:144]
    for k, out in enumerate((s1, s2, s3)):
        out[...] = grad[(k + 1) * 144 : (k + 2) * 144].astype(bf16)
    for k, out in enumerate((t1, t2)):
        out[...] = terms[(k + 1) * ROWS : (k + 2) * ROWS].astype(bf16)


def first_sum(own, a1, a2, a3, terms, b1, b2, rows, out, text, text_send, send):
    out[...] = own[...] + a2[...].astype(f32) + a1[...].astype(f32) + a3[...].astype(f32)
    text[...] = terms[:ROWS] + b2[...].astype(f32) + b1[...].astype(f32)
    text_send[...] = terms[3 * ROWS :].astype(bf16)
    send[...] = rows[ROWS:].astype(bf16)


def second_sum(own, a1, a2, a3, out, send):
    total = own[...] + a2[...].astype(f32) + a1[...].astype(f32) + a3[...].astype(f32)
    out[...] = total
    send[...] = total.astype(bf16)


def third_sum(count, own, a1, text, b3, rows, arrived, out, text_grad, grad):
    out[...] = own[...] + a1[...].astype(f32)
    keep = lax.broadcasted_iota(jnp.int32, (ROWS, 1), 0) < count[0]
    text_grad[...] = jnp.where(keep, text[...] + b3[...].astype(f32), 0.0)
    grad[...] = (rows[:ROWS] + arrived[...].astype(f32)).astype(bf16)


def back(count, rows, weight, out):
    grad = dot(rows[...], weight[...], 1, 1)
    keep = lax.broadcasted_iota(jnp.int32, (ROWS, 1), 0) < count[0]
    out[...] = jnp.where(keep, grad, 0.0).astype(bf16)


def four(own, sends, axis):
    got = [xor(sends[k - 1], axis, k).astype(f32) for k in (2, 1, 3)]
    return own + got[0] + got[1] + got[2]


def per_device(hidden, weight, text, pair_ids, valid_count, logit_scale, logit_bias):
    zh, x1, x0, y, c = (lax.axis_index(a) for a in ("zh", "x1", "x0", "y", "c"))
    x = x1 * 2 + x0
    X = ("x1", "x0")
    block = ROWS * WIDTH
    labels = lax.dynamic_slice_in_dim(pair_ids[0], (zh * 2 + x1) * ROWS * 16, ROWS * 16, 0)
    labels = labels.reshape(16, ROWS)
    where = [(px * 4 + y) * 2 + pc for pc, px in ((c, x0), (c, 1 - x0), (1 - c, x0), (1 - c, 1 - x0))]
    where = jnp.stack(where + [(x0 * 4 + (y ^ j)) * 2 + c for j in range(4)]).astype(jnp.int32)
    scalars = jnp.stack([logit_scale, logit_bias])
    i = np.arange(576)
    places = (
        ((zh ^ jnp.asarray(i // 9 % 4)) * 288)
        + ((x ^ jnp.asarray(i // 144)) * 72)
        + ((y ^ jnp.asarray(i // 36 % 4)) * 18)
        + (c * 9 + jnp.asarray(i % 9))
    ).astype(jnp.int32)[:, None]
    wide, tall = shape(bf16, ROWS, WIDTH), shape(f32, 512, WIDTH)
    with jax.named_scope("prepare"):
        hid, txt = call(
            prepare,
            [wide, wide],
            [SMEM, HBM, HBM],
            0,
            block,
            [pltpu.VMEM((ROWS, WIDTH), bf16)] * 2 + [pltpu.SemaphoreType.DMA((2,))],
        )(valid_count, in_hbm(hidden), in_hbm(text))
    with jax.named_scope("gather"):
        hid_x = xor(hid, "x0", 1)
        txt_1 = xor(txt, "y", 1)
        txt_3 = xor(txt, "y", 3)
        both, first, second = call(
            join,
            [shape(bf16, 256, WIDTH)] + [shape(bf16, 64, WIDTH)] * 2,
            [VMEM] * 4,
            0,
            block,
        )(hid, hid_x, txt_1, txt_3)
        txt_2a = xor(first, "y", 1)
        txt_2b = xor(second, "y", 3)
        hid_c = xor(both, "c", 1)
    with jax.named_scope("project"):
        embed, normed, inverse, turned = call(
            project,
            [shape(bf16, 512, WIDTH), tall, shape(f32, 512, 1), shape(bf16, 576, 512)],
            [VMEM, VMEM, HBM, VMEM],
            0,
            block,
            [pltpu.VMEM((WIDTH, WIDTH), bf16), pltpu.SemaphoreType.DMA],
        )(both, hid_c, in_hbm(weight), places)
    with jax.named_scope("tile"):
        coef, part, part_send = call(
            tile,
            [shape(bf16, 512, 512), tall, shape(bf16, 512, WIDTH)],
            [SMEM, SMEM] + [VMEM] * 9,
            0,
            block,
        )(where, scalars, labels, embed, normed, inverse, txt, txt_1, txt_2a, txt_2b, txt_3)
    with jax.named_scope("core"):
        arrived = xor(part_send, "c", 1)
    with jax.named_scope("text"):
        (terms,) = call(text_terms, [tall], [VMEM] * 2, 0, block)(coef, embed)
    with jax.named_scope("weight"):
        rows, own, s1, s2, s3, u1, u2 = call(
            weight_terms,
            [shape(f32, 256, WIDTH), shape(f32, 144, WIDTH)]
            + [shape(bf16, 144, WIDTH)] * 3
            + [wide] * 2,
            [VMEM] * 4,
            0,
            block,
        )(part, arrived, turned, terms)
        s2, s1, s3 = xor(s2, X, 2), xor(s1, X, 1), xor(s3, X, 3)
        u2, u1 = xor(u2, "y", 2), xor(u1, "y", 1)
        whole, text_sum, u3, rows_send = call(
            first_sum,
            [shape(f32, 144, WIDTH), shape(f32, ROWS, WIDTH), wide, wide],
            [VMEM] * 8,
            0,
            block,
        )(own, s1, s2, s3, terms, u1, u2, rows)
        whole = whole.reshape(4, 36, WIDTH)
        s2, s1, s3 = (xor(whole[k].astype(bf16), "y", k) for k in (2, 1, 3))
        rows_x = xor(rows_send, "x0", 1)
        u3 = xor(u3, "y", 3)
        small = shape(f32, 36, WIDTH)
        whole, whole_send = call(
            second_sum, [small, shape(bf16, 36, WIDTH)], [VMEM] * 4, 0, block
        )(whole[0], s1, s2, s3)
        whole, text_grad, grad = call(
            third_sum,
            [small, shape(f32, ROWS, WIDTH), wide],
            [SMEM] + [VMEM] * 6,
            0,
            block,
        )(valid_count, whole, xor(whole_send, "zl", 1), text_sum, u3, rows, rows_x)
        whole = whole.reshape(4, 9, WIDTH)
        weight_grad = four(whole[0], [whole[k] for k in (1, 2, 3)], "zh")
    with jax.named_scope("hidden"):
        (hidden_grad,) = call(
            back, [wide], [SMEM] + [VMEM] * 2, 2 * block * WIDTH, WIDTH * WIDTH * 2
        )(valid_count, grad, weight)
    return hidden_grad, weight_grad, text_grad


def solution(mesh):
    fine = Mesh(mesh.devices.reshape(4, 2, 2, 4, 2, 2), AXES)
    blk = ("zh", "x1", "x0", "y", "c")
    by_row = P(("zl",) + blk, None)
    return jax.shard_map(
        per_device,
        mesh=fine,
        in_specs=(by_row, P(), by_row, P("zl", None), P(("zl",) + blk), P(), P()),
        out_specs=(by_row, P(blk, None), by_row),
        check_vma=False,
    )
```

time: 92.7 us -> 85.5 us (0.922)
  the two profiles are of different devices: /device:TPU:2 before, /device:TPU:32 now
where the time goes in v3:
time: 85.5 us; the launch traced here: 85.3 us
  waiting for transfers between devices  39.5 us (46%)
  starting transfers between devices  28.5 us (33%)
  Pallas kernels  12.7 us (15%)
  between operations  2.76 us (3%)
  other arithmetic  1.52 us (2%)
    ppermute x21, waiting for transfers between devices, xor(): return lax.ppermute(x, axis, [(i, i ^ step) for i in range(size)])  39.5 us
    ppermute x21, starting transfers between devices, xor(): return lax.ppermute(x, axis, [(i, i ^ step) for i in range(size)])  28.5 us
    pallas_call x1, Pallas kernels, per_device(): call(project, [shape(bf16, 512, WIDTH), tall, shape(f32, 512, 1), shape(b...  4.05 us
    pallas_call x1, Pallas kernels, per_device(): call(tile, [shape(bf16, 512, 512), tall, shape(bf16, 512, WIDTH)], [SMEM,...  2.6 us
  transfers between devices with their start and end apart: 21, of which 12 were waited for; matrix products, arithmetic and copies ran while one was open for 1% of the time, Pallas kernels for 8%

profile of v3, /device:TPU:32, one launch (start us, length us, event | category | flops | bytes accessed | tf_op | source)
XLA Modules:
  0.0 85.3 jit_solution(261795796307441426)
XLA Ops:
  1.3 1.2 %prepare.1 = (bf16[128,1152]{1,0:T(8,128)(2,1)S(1)}, bf16[128,1152]{1,0:T(8,128)(2,1)S(1)}) custom-call(s32[1]{0:T(128)S(6)} %copy.15.count, bf16[128,1152]{1,0:T(8,128)(2,1)} %hidden.2, bf16[128,1152]{1,0:T(8,128)(2,1)} %text.2), custom_call_target="tpu_custom_call" | custom-call | bytes 147456 | tf_op jit(solution)/shard_map/prepare/pallas_call | solution.py:177
  2.5 1.6 %collective-permute-start = (bf16[128,1152]{1,0:T(8,128)(2,1)S(1)}, bf16[128,1152]{1,0:T(8,128)(2,1)S(1)}, u32[]{:S(2)}, u32[]{:S(2)}) collective-permute-start(bf16[128,1152]{1,0:T(8,128)(2,1)S(1)} %get-tuple-element.31.own), channel_id=1, source_target_pairs={{0,16},{16,0},{1,17},{17,1},{2,18},{18,2},{3,19},{19,3},{4,20},{20... | collective-permute-start | bytes 884744 | tf_op jit(solution)/shard_map/gather/ppermute | solution.py:26
  4.1 3.0 %collective-permute-start.2 = (bf16[128,1152]{1,0:T(8,128)(2,1)S(1)}, bf16[128,1152]{1,0:T(8,128)(2,1)S(1)}, u32[]{:S(2)}, u32[]{:S(2)}) collective-permute-start(bf16[128,1152]{1,0:T(8,128)(2,1)S(1)} %get-tuple-element.32.t0), channel_id=1, source_target_pairs={{0,12},{4,8},{8,4},{12,0},{1,13},{5,9},{9,5},{13,1},{2,14},{6,10},... | collective-permute-start | bytes 884744 | tf_op jit(solution)/shard_map/gather/ppermute | solution.py:26
  7.2 4.1 %collective-permute-done.paired = bf16[128,1152]{1,0:T(8,128)(2,1)S(1)} collective-permute-done((bf16[128,1152]{1,0:T(8,128)(2,1)S(1)}, bf16[128,1152]{1,0:T(8,128)(2,1)S(1)}, u32[]{:S(2)}, u32[]{:S(2)}) %collective-permute-start) | collective-permute-done | bytes 294944 | tf_op jit(solution)/shard_map/gather/ppermute | solution.py:26
  11.4 2.5 %collective-permute-done.2.t3 = bf16[128,1152]{1,0:T(8,128)(2,1)S(1)} collective-permute-done((bf16[128,1152]{1,0:T(8,128)(2,1)S(1)}, bf16[128,1152]{1,0:T(8,128)(2,1)S(1)}, u32[]{:S(2)}, u32[]{:S(2)}) %collective-permute-start.2) | collective-permute-done | bytes 294944 | tf_op jit(solution)/shard_map/gather/ppermute | solution.py:26
  13.8 1.5 %collective-permute-done.1.t1 = bf16[128,1152]{1,0:T(8,128)(2,1)S(1)} collective-permute-done((bf16[128,1152]{1,0:T(8,128)(2,1)S(1)}, bf16[128,1152]{1,0:T(8,128)(2,1)S(1)}, u32[]{:S(2)}, u32[]{:S(2)}) %collective-permute-start.1) | collective-permute-done | bytes 294944 | tf_op jit(solution)/shard_map/gather/ppermute | solution.py:26
  16.5 1.3 %collective-permute-start.5 = (bf16[64,1152]{1,0:T(8,128)(2,1)S(1)}, bf16[64,1152]{1,0:T(8,128)(2,1)S(1)}, u32[]{:S(2)}, u32[]{:S(2)}) collective-permute-start(bf16[64,1152]{1,0:T(8,128)(2,1)S(1)} %get-tuple-element.38), channel_id=1, source_target_pairs={{0,12},{4,8},{8,4},{12,0},{1,13},{5,9},{9,5},{13,1},{2,14},{6,10},... | collective-permute-start | bytes 442376 | tf_op jit(solution)/shard_map/gather/ppermute | solution.py:26
  19.4 4.1 %project.1 = (bf16[512,1152]{1,0:T(8,128)(2,1)S(1)}, f32[512,1152]{1,0:T(8,128)S(1)}, f32[512,1]{1,0:T(8,128)S(1)}, bf16[576,512]{1,0:T(8,128)(2,1)S(1)}) custom-call(bf16[256,1152]{1,0:T(8,128)(2,1)S(1)} %get-tuple-element.33.both, bf16[256,1152]{1,0:T(8,128)(2,1)S(1)} %collective-permute-done.3.cores, bf16[1152,1152]{1,0:T(8,128)(2,1)} %weight.11, ...), custom_call_target="tpu_custom_call" | custom-call | bytes 147456 | tf_op jit(solution)/shard_map/project/pallas_call | solution.py:200
  23.8 2.6 %tile.1 = (bf16[512,512]{1,0:T(8,128)(2,1)S(1)}, f32[512,1152]{1,0:T(8,128)S(1)}, bf16[512,1152]{1,0:T(8,128)(2,1)S(1)}) custom-call(s32[8]{0:T(128)S(1)} %stack.41.where, f32[2]{0:T(128)S(1)} %pad_maximum_fusion.scalars, s32[16,128]{1,0:T(8,128)S(1)} %bitcast.12, bf16[512,1152]{1,0:T(8,128)(2,1)S(1)} %get-tuple-element.34.embed, ...), custom_call_target="tpu_custom_call" | custom-call | bytes 147456 | tf_op jit(solution)/shard_map/tile/pallas_call | solution.py:209
  27.4 1.9 %collective-permute-done.6.arrived = bf16[512,1152]{1,0:T(8,128)(2,1)S(1)} collective-permute-done((bf16[512,1152]{1,0:T(8,128)(2,1)S(1)}, bf16[512,1152]{1,0:T(8,128)(2,1)S(1)}, u32[]{:S(2)}, u32[]{:S(2)}) %collective-permute-start.6) | collective-permute-done | bytes 1179680 | tf_op jit(solution)/shard_map/core/ppermute | solution.py:26
  30.9 3.0 %collective-permute-start.8 = (bf16[144,1152]{1,0:T(8,128)(2,1)S(1)}, bf16[144,1152]{1,0:T(8,128)(2,1)S(1)}, u32[]{:S(2)}, u32[]{:S(2)}) collective-permute-start(bf16[144,1152]{1,0:T(8,128)(2,1)S(1)} %get-tuple-element.45), channel_id=1, source_target_pairs={{0,32},{16,48},{32,0},{48,16},{1,33},{17,49},{33,1},{49,17},{2,34}... | collective-permute-start | bytes 995336 | tf_op jit(solution)/shard_map/weight/ppermute | solution.py:26
  34.0 1.1 %collective-permute-start.9 = (bf16[144,1152]{1,0:T(8,128)(2,1)S(1)}, bf16[144,1152]{1,0:T(8,128)(2,1)S(1)}, u32[]{:S(2)}, u32[]{:S(2)}) collective-permute-start(bf16[144,1152]{1,0:T(8,128)(2,1)S(1)} %get-tuple-element.46), channel_id=1, source_target_pairs={{0,48},{16,32},{32,16},{48,0},{1,49},{17,33},{33,17},{49,1},{2,50}... | collective-permute-start | bytes 995336 | tf_op jit(solution)/shard_map/weight/ppermute | solution.py:26
  35.1 1.1 %collective-permute-start.10 = (bf16[128,1152]{1,0:T(8,128)(2,1)S(1)}, bf16[128,1152]{1,0:T(8,128)(2,1)S(1)}, u32[]{:S(2)}, u32[]{:S(2)}) collective-permute-start(bf16[128,1152]{1,0:T(8,128)(2,1)S(1)} %get-tuple-element.47), channel_id=1, source_target_pairs={{0,4},{4,0},{8,12},{12,8},{1,5},{5,1},{9,13},{13,9},{2,6},{6,2},{1... | collective-permute-start | bytes 884744 | tf_op jit(solution)/shard_map/weight/ppermute | solution.py:26
  36.2 2.1 %collective-permute-start.11 = (bf16[128,1152]{1,0:T(8,128)(2,1)S(1)}, bf16[128,1152]{1,0:T(8,128)(2,1)S(1)}, u32[]{:S(2)}, u32[]{:S(2)}) collective-permute-start(bf16[128,1152]{1,0:T(8,128)(2,1)S(1)} %get-tuple-element.48), channel_id=1, source_target_pairs={{0,8},{4,12},{8,0},{12,4},{1,9},{5,13},{9,1},{13,5},{2,10},{6,14},... | collective-permute-start | bytes 884744 | tf_op jit(solution)/shard_map/weight/ppermute | solution.py:26
  38.3 6.8 %collective-permute-done.10.b1 = bf16[128,1152]{1,0:T(8,128)(2,1)S(1)} collective-permute-done((bf16[128,1152]{1,0:T(8,128)(2,1)S(1)}, bf16[128,1152]{1,0:T(8,128)(2,1)S(1)}, u32[]{:S(2)}, u32[]{:S(2)}) %collective-permute-start.10) | collective-permute-done | bytes 294944 | tf_op jit(solution)/shard_map/weight/ppermute | solution.py:26
  45.1 5.7 %collective-permute-done.11.b2 = bf16[128,1152]{1,0:T(8,128)(2,1)S(1)} collective-permute-done((bf16[128,1152]{1,0:T(8,128)(2,1)S(1)}, bf16[128,1152]{1,0:T(8,128)(2,1)S(1)}, u32[]{:S(2)}, u32[]{:S(2)}) %collective-permute-start.11) | collective-permute-done | bytes 294944 | tf_op jit(solution)/shard_map/weight/ppermute | solution.py:26
  51.9 1.8 %collective-permute-start.16 = (bf16[128,1152]{1,0:T(8,128)(2,1)S(1)}, bf16[128,1152]{1,0:T(8,128)(2,1)S(1)}, u32[]{:S(2)}, u32[]{:S(2)}) collective-permute-start(bf16[128,1152]{1,0:T(8,128)(2,1)S(1)} %get-tuple-element.54), channel_id=1, source_target_pairs={{0,12},{4,8},{8,4},{12,0},{1,13},{5,9},{9,5},{13,1},{2,14},{6,10},... | collective-permute-start | bytes 884744 | tf_op jit(solution)/shard_map/weight/ppermute | solution.py:26
  53.8 1.6 %collective-permute-start.14 = (bf16[36,1152]{1,0:T(8,128)(2,1)S(1)}, bf16[36,1152]{1,0:T(8,128)(2,1)S(1)}, u32[]{:S(2)}, u32[]{:S(2)}) collective-permute-start(bf16[36,1152]{1,0:T(8,128)(2,1)S(1)} %get-tuple-element.59), channel_id=1, source_target_pairs={{0,12},{4,8},{8,4},{12,0},{1,13},{5,9},{9,5},{13,1},{2,14},{6,10},... | collective-permute-start | bytes 248840 | tf_op jit(solution)/shard_map/weight/ppermute | solution.py:26
  56.4 1.5 %collective-permute-start.12 = (bf16[36,1152]{1,0:T(8,128)(2,1)S(1)}, bf16[36,1152]{1,0:T(8,128)(2,1)S(1)}, u32[]{:S(2)}, u32[]{:S(2)}) collective-permute-start(bf16[36,1152]{1,0:T(8,128)(2,1)S(1)} %get-tuple-element.61), channel_id=1, source_target_pairs={{0,4},{4,0},{8,12},{12,8},{1,5},{5,1},{9,13},{13,9},{2,6},{6,2},{1... | collective-permute-start | bytes 248840 | tf_op jit(solution)/shard_map/weight/ppermute | solution.py:26
  58.0 6.8 %collective-permute-done.14.a3 = bf16[36,1152]{1,0:T(8,128)(2,1)S(1)} collective-permute-done((bf16[36,1152]{1,0:T(8,128)(2,1)S(1)}, bf16[36,1152]{1,0:T(8,128)(2,1)S(1)}, u32[]{:S(2)}, u32[]{:S(2)}) %collective-permute-start.14) | collective-permute-done | bytes 82976 | tf_op jit(solution)/shard_map/weight/ppermute | solution.py:26
  65.0 4.5 %collective-permute-done.15.a1 = bf16[36,1152]{1,0:T(8,128)(2,1)S(1)} collective-permute-done((bf16[36,1152]{1,0:T(8,128)(2,1)S(1)}, bf16[36,1152]{1,0:T(8,128)(2,1)S(1)}, u32[]{:S(2)}, u32[]{:S(2)}) %collective-permute-start.15) | collective-permute-done | bytes 82976 | tf_op jit(solution)/shard_map/weight/ppermute | solution.py:26
  70.4 6.9 %collective-permute-start.18 = (f32[9,1152]{1,0:T(8,128)S(1)}, f32[9,1152]{1,0:T(8,128)S(1)}, u32[]{:S(2)}, u32[]{:S(2)}) collective-permute-start(f32[9,1152]{1,0:T(8,128)S(1)} %get-tuple-element.62), channel_id=1, source_target_pairs={{0,128},{64,192},{128,0},{192,64},{1,129},{65,193},{129,1},{193,65... | collective-permute-start | bytes 124424 | tf_op jit(solution)/shard_map/weight/ppermute | solution.py:26
  78.4 1.6 %hidden.3 = bf16[128,1152]{1,0:T(8,128)(2,1)} custom-call(s32[1]{0:T(128)S(6)} %copy.15.count, bf16[128,1152]{1,0:T(8,128)(2,1)S(1)} %get-tuple-element.56.rows, bf16[1152,1152]{1,0:T(8,128)(2,1)S(1)} %copy-done.1), custom_call_target="tpu_custom_call" | custom-call | flops 339738624 | bytes 2654208 | tf_op jit(solution)/shard_map/hidden/pallas_call | solution.py:257
  80.5 4.1 %collective-permute-done.20 = f32[9,1152]{1,0:T(8,128)S(1)} collective-permute-done((f32[9,1152]{1,0:T(8,128)S(1)}, f32[9,1152]{1,0:T(8,128)S(1)}, u32[]{:S(2)}, u32[]{:S(2)}) %collective-permute-start.20) | collective-permute-done | bytes 41504 | tf_op jit(solution)/shard_map/weight/ppermute | solution.py:26
  (42 shorter events, 10.1 us)
Async XLA Ops:
  0.6 17.2 %copy-start = (s32[1,16384]{1,0:T(1,128)S(1)}, s32[1,16384]{1,0:T(1,128)}, u32[]{:S(2)}) copy-start(s32[1,16384]{1,0:T(1,128)} %param.14) | copy-start | bytes 196612
  2.5 8.8 %collective-permute-start = (bf16[128,1152]{1,0:T(8,128)(2,1)S(1)}, bf16[128,1152]{1,0:T(8,128)(2,1)S(1)}, u32[]{:S(2)}, u32[]{:S(2)}) collective-permute-start(bf16[128,1152]{1,0:T(8,128)(2,1)S(1)} %get-tuple-element.31.own), channel_id=1, source_target_pairs={{0,16},{16,0},{1,17},{17,1},{2,18},{18,2},{3,19},{19,3},{4,20},{20... | collective-permute-start | bytes 884744 | tf_op jit(solution)/shard_map/gather/ppermute | solution.py:26
  4.1 9.7 %collective-permute-start.2 = (bf16[128,1152]{1,0:T(8,128)(2,1)S(1)}, bf16[128,1152]{1,0:T(8,128)(2,1)S(1)}, u32[]{:S(2)}, u32[]{:S(2)}) collective-permute-start(bf16[128,1152]{1,0:T(8,128)(2,1)S(1)} %get-tuple-element.32.t0), channel_id=1, source_target_pairs={{0,12},{4,8},{8,4},{12,0},{1,13},{5,9},{9,5},{13,1},{2,14},{6,10},... | collective-permute-start | bytes 884744 | tf_op jit(solution)/shard_map/gather/ppermute | solution.py:26
  7.1 8.2 %collective-permute-start.1 = (bf16[128,1152]{1,0:T(8,128)(2,1)S(1)}, bf16[128,1152]{1,0:T(8,128)(2,1)S(1)}, u32[]{:S(2)}, u32[]{:S(2)}) collective-permute-start(bf16[128,1152]{1,0:T(8,128)(2,1)S(1)} %get-tuple-element.32.t0), channel_id=1, source_target_pairs={{0,4},{4,0},{8,12},{12,8},{1,5},{5,1},{9,13},{13,9},{2,6},{6,2},{1... | collective-permute-start | bytes 884744 | tf_op jit(solution)/shard_map/gather/ppermute | solution.py:26
  15.4 4.1 %collective-permute-start.3 = (bf16[256,1152]{1,0:T(8,128)(2,1)S(1)}, bf16[256,1152]{1,0:T(8,128)(2,1)S(1)}, u32[]{:S(2)}, u32[]{:S(2)}) collective-permute-start(bf16[256,1152]{1,0:T(8,128)(2,1)S(1)} %get-tuple-element.33.both), channel_id=1, source_target_pairs={{0,2},{2,0},{1,3},{3,1},{4,6},{6,4},{5,7},{7,5},{8,10},{10,8},{9,1... | collective-permute-start | bytes 1769480 | tf_op jit(solution)/shard_map/gather/ppermute | solution.py:26
  16.2 7.3 %collective-permute-start.4 = (bf16[64,1152]{1,0:T(8,128)(2,1)S(1)}, bf16[64,1152]{1,0:T(8,128)(2,1)S(1)}, u32[]{:S(2)}, u32[]{:S(2)}) collective-permute-start(bf16[64,1152]{1,0:T(8,128)(2,1)S(1)} %get-tuple-element.37), channel_id=1, source_target_pairs={{0,4},{4,0},{8,12},{12,8},{1,5},{5,1},{9,13},{13,9},{2,6},{6,2},{1... | collective-permute-start | bytes 442376 | tf_op jit(solution)/shard_map/gather/ppermute | solution.py:26
  16.5 7.2 %collective-permute-start.5 = (bf16[64,1152]{1,0:T(8,128)(2,1)S(1)}, bf16[64,1152]{1,0:T(8,128)(2,1)S(1)}, u32[]{:S(2)}, u32[]{:S(2)}) collective-permute-start(bf16[64,1152]{1,0:T(8,128)(2,1)S(1)} %get-tuple-element.38), channel_id=1, source_target_pairs={{0,12},{4,8},{8,4},{12,0},{1,13},{5,9},{9,5},{13,1},{2,14},{6,10},... | collective-permute-start | bytes 442376 | tf_op jit(solution)/shard_map/gather/ppermute | solution.py:26
  26.4 2.9 %collective-permute-start.6 = (bf16[512,1152]{1,0:T(8,128)(2,1)S(1)}, bf16[512,1152]{1,0:T(8,128)(2,1)S(1)}, u32[]{:S(2)}, u32[]{:S(2)}) collective-permute-start(bf16[512,1152]{1,0:T(8,128)(2,1)S(1)} %get-tuple-element.40), channel_id=1, source_target_pairs={{0,2},{2,0},{1,3},{3,1},{4,6},{6,4},{5,7},{7,5},{8,10},{10,8},{9,1... | collective-permute-start | bytes 3538952 | tf_op jit(solution)/shard_map/core/ppermute | solution.py:26
  30.3 20.4 %collective-permute-start.7 = (bf16[144,1152]{1,0:T(8,128)(2,1)S(1)}, bf16[144,1152]{1,0:T(8,128)(2,1)S(1)}, u32[]{:S(2)}, u32[]{:S(2)}) collective-permute-start(bf16[144,1152]{1,0:T(8,128)(2,1)S(1)} %get-tuple-element.44), channel_id=1, source_target_pairs={{0,16},{16,0},{32,48},{48,32},{1,17},{17,1},{33,49},{49,33},{2,18}... | collective-permute-start | bytes 995336 | tf_op jit(solution)/shard_map/weight/ppermute | solution.py:26
  30.9 19.8 %collective-permute-start.8 = (bf16[144,1152]{1,0:T(8,128)(2,1)S(1)}, bf16[144,1152]{1,0:T(8,128)(2,1)S(1)}, u32[]{:S(2)}, u32[]{:S(2)}) collective-permute-start(bf16[144,1152]{1,0:T(8,128)(2,1)S(1)} %get-tuple-element.45), channel_id=1, source_target_pairs={{0,32},{16,48},{32,0},{48,16},{1,33},{17,49},{33,1},{49,17},{2,34}... | collective-permute-start | bytes 995336 | tf_op jit(solution)/shard_map/weight/ppermute | solution.py:26
  34.0 17.6 %collective-permute-start.9 = (bf16[144,1152]{1,0:T(8,128)(2,1)S(1)}, bf16[144,1152]{1,0:T(8,128)(2,1)S(1)}, u32[]{:S(2)}, u32[]{:S(2)}) collective-permute-start(bf16[144,1152]{1,0:T(8,128)(2,1)S(1)} %get-tuple-element.46), channel_id=1, source_target_pairs={{0,48},{16,32},{32,16},{48,0},{1,49},{17,33},{33,17},{49,1},{2,50}... | collective-permute-start | bytes 995336 | tf_op jit(solution)/shard_map/weight/ppermute | solution.py:26
  35.1 9.9 %collective-permute-start.10 = (bf16[128,1152]{1,0:T(8,128)(2,1)S(1)}, bf16[128,1152]{1,0:T(8,128)(2,1)S(1)}, u32[]{:S(2)}, u32[]{:S(2)}) collective-permute-start(bf16[128,1152]{1,0:T(8,128)(2,1)S(1)} %get-tuple-element.47), channel_id=1, source_target_pairs={{0,4},{4,0},{8,12},{12,8},{1,5},{5,1},{9,13},{13,9},{2,6},{6,2},{1... | collective-permute-start | bytes 884744 | tf_op jit(solution)/shard_map/weight/ppermute | solution.py:26
  36.2 14.6 %collective-permute-start.11 = (bf16[128,1152]{1,0:T(8,128)(2,1)S(1)}, bf16[128,1152]{1,0:T(8,128)(2,1)S(1)}, u32[]{:S(2)}, u32[]{:S(2)}) collective-permute-start(bf16[128,1152]{1,0:T(8,128)(2,1)S(1)} %get-tuple-element.48), channel_id=1, source_target_pairs={{0,8},{4,12},{8,0},{12,4},{1,9},{5,13},{9,1},{13,5},{2,10},{6,14},... | collective-permute-start | bytes 884744 | tf_op jit(solution)/shard_map/weight/ppermute | solution.py:26
  51.9 26.4 %copy-start.1 = (bf16[1152,1152]{1,0:T(8,128)(2,1)S(1)}, bf16[1152,1152]{1,0:T(8,128)(2,1)}, u32[]{:S(2)}) copy-start(bf16[1152,1152]{1,0:T(8,128)(2,1)} %weight.11) | copy-start | bytes 7962628
  51.9 17.5 %collective-permute-start.16 = (bf16[128,1152]{1,0:T(8,128)(2,1)S(1)}, bf16[128,1152]{1,0:T(8,128)(2,1)S(1)}, u32[]{:S(2)}, u32[]{:S(2)}) collective-permute-start(bf16[128,1152]{1,0:T(8,128)(2,1)S(1)} %get-tuple-element.54), channel_id=1, source_target_pairs={{0,12},{4,8},{8,4},{12,0},{1,13},{5,9},{9,5},{13,1},{2,14},{6,10},... | collective-permute-start | bytes 884744 | tf_op jit(solution)/shard_map/weight/ppermute | solution.py:26
  53.7 15.8 %collective-permute-start.17 = (bf16[128,1152]{1,0:T(8,128)(2,1)S(1)}, bf16[128,1152]{1,0:T(8,128)(2,1)S(1)}, u32[]{:S(2)}, u32[]{:S(2)}) collective-permute-start(bf16[128,1152]{1,0:T(8,128)(2,1)S(1)} %get-tuple-element.55), channel_id=1, source_target_pairs={{0,16},{16,0},{1,17},{17,1},{2,18},{18,2},{3,19},{19,3},{4,20},{20... | collective-permute-start | bytes 884744 | tf_op jit(solution)/shard_map/weight/ppermute | solution.py:26
  53.8 11.0 %collective-permute-start.14 = (bf16[36,1152]{1,0:T(8,128)(2,1)S(1)}, bf16[36,1152]{1,0:T(8,128)(2,1)S(1)}, u32[]{:S(2)}, u32[]{:S(2)}) collective-permute-start(bf16[36,1152]{1,0:T(8,128)(2,1)S(1)} %get-tuple-element.59), channel_id=1, source_target_pairs={{0,12},{4,8},{8,4},{12,0},{1,13},{5,9},{9,5},{13,1},{2,14},{6,10},... | collective-permute-start | bytes 248840 | tf_op jit(solution)/shard_map/weight/ppermute | solution.py:26
  55.4 9.4 %collective-permute-start.13 = (bf16[36,1152]{1,0:T(8,128)(2,1)S(1)}, bf16[36,1152]{1,0:T(8,128)(2,1)S(1)}, u32[]{:S(2)}, u32[]{:S(2)}) collective-permute-start(bf16[36,1152]{1,0:T(8,128)(2,1)S(1)} %get-tuple-element.60), channel_id=1, source_target_pairs={{0,8},{4,12},{8,0},{12,4},{1,9},{5,13},{9,1},{13,5},{2,10},{6,14},... | collective-permute-start | bytes 248840 | tf_op jit(solution)/shard_map/weight/ppermute | solution.py:26
  56.4 8.3 %collective-permute-start.12 = (bf16[36,1152]{1,0:T(8,128)(2,1)S(1)}, bf16[36,1152]{1,0:T(8,128)(2,1)S(1)}, u32[]{:S(2)}, u32[]{:S(2)}) collective-permute-start(bf16[36,1152]{1,0:T(8,128)(2,1)S(1)} %get-tuple-element.61), channel_id=1, source_target_pairs={{0,4},{4,0},{8,12},{12,8},{1,5},{5,1},{9,13},{13,9},{2,6},{6,2},{1... | collective-permute-start | bytes 248840 | tf_op jit(solution)/shard_map/weight/ppermute | solution.py:26
  64.8 4.6 %collective-permute-start.15 = (bf16[36,1152]{1,0:T(8,128)(2,1)S(1)}, bf16[36,1152]{1,0:T(8,128)(2,1)S(1)}, u32[]{:S(2)}, u32[]{:S(2)}) collective-permute-start(bf16[36,1152]{1,0:T(8,128)(2,1)S(1)} %get-tuple-element.52), channel_id=1, source_target_pairs={{0,1},{1,0},{2,3},{3,2},{4,5},{5,4},{6,7},{7,6},{8,9},{9,8},{10,11... | collective-permute-start | bytes 248840 | tf_op jit(solution)/shard_map/weight/ppermute | solution.py:26
  70.4 10.1 %collective-permute-start.18 = (f32[9,1152]{1,0:T(8,128)S(1)}, f32[9,1152]{1,0:T(8,128)S(1)}, u32[]{:S(2)}, u32[]{:S(2)}) collective-permute-start(f32[9,1152]{1,0:T(8,128)S(1)} %get-tuple-element.62), channel_id=1, source_target_pairs={{0,128},{64,192},{128,0},{192,64},{1,129},{65,193},{129,1},{193,65... | collective-permute-start | bytes 124424 | tf_op jit(solution)/shard_map/weight/ppermute | solution.py:26
  77.4 7.3 %collective-permute-start.20 = (f32[9,1152]{1,0:T(8,128)S(1)}, f32[9,1152]{1,0:T(8,128)S(1)}, u32[]{:S(2)}, u32[]{:S(2)}) collective-permute-start(f32[9,1152]{1,0:T(8,128)S(1)} %get-tuple-element.63), channel_id=1, source_target_pairs={{0,192},{64,128},{128,64},{192,0},{1,193},{65,129},{129,65},{193,1... | collective-permute-start | bytes 124424 | tf_op jit(solution)/shard_map/weight/ppermute | solution.py:26
  77.4 7.3 %collective-permute-start.19 = (f32[9,1152]{1,0:T(8,128)S(1)}, f32[9,1152]{1,0:T(8,128)S(1)}, u32[]{:S(2)}, u32[]{:S(2)}) collective-permute-start(f32[9,1152]{1,0:T(8,128)S(1)} %get-tuple-element.64), channel_id=1, source_target_pairs={{0,64},{64,0},{128,192},{192,128},{1,65},{65,1},{129,193},{193,129... | collective-permute-start | bytes 124424 | tf_op jit(solution)/shard_map/weight/ppermute | solution.py:26

commit v4 on v3

v4 whole, which is shorter than its diff:
```python
import jax
import jax.numpy as jnp
from jax import lax
from jax.experimental import pallas as pl
from jax.experimental.pallas import tpu as pltpu
from jax.sharding import Mesh, PartitionSpec as P

epsilon = 1e-06
AXES = ("zh", "x1", "x0", "y", "c", "zl")
f32 = jnp.float32
bf16 = jnp.bfloat16
ROWS = 128
WIDTH = 1152
VMEM = pl.BlockSpec(memory_space=pltpu.VMEM)
SMEM = pl.BlockSpec(memory_space=pltpu.SMEM)
ANY = pl.BlockSpec(memory_space=pl.ANY)
HBM = pl.BlockSpec(memory_space=pltpu.HBM)


def dot(a, b, ca, cb):
    return lax.dot_general(a, b, (((ca,), (cb,)), ((), ())), preferred_element_type=f32)


def xor(x, axis, step):
    size = lax.axis_size(axis)
    return lax.ppermute(x, axis, [(i, i ^ step) for i in range(size)])


def shape(dtype, *dims):
    return jax.ShapeDtypeStruct(dims, dtype)


def in_hbm(x):
    return pltpu.with_memory_space_constraint(x, pltpu.HBM)


def call(body, outs, specs, flops, moved, scratch=()):
    return pl.pallas_call(
        body,
        out_shape=outs,
        in_specs=specs,
        out_specs=[VMEM] * len(outs),
        scratch_shapes=scratch,
        compiler_params=pltpu.CompilerParams(vmem_limit_bytes=40 << 20),
        cost_estimate=pl.CostEstimate(flops=flops, bytes_accessed=moved, transcendentals=0),
    )


def prepare(count, hidden, text, hid_out, txt_out, hid_in, txt_in, sems):
    copies = [
        pltpu.make_async_copy(text, txt_in, sems.at[0]),
        pltpu.make_async_copy(hidden, hid_in, sems.at[1]),
    ]
    for copy in copies:
        copy.start()
    keep = lax.broadcasted_iota(jnp.int32, (ROWS, 1), 0) < count[0]
    copies[0].wait()
    txt = txt_in[...].astype(f32)
    txt = txt * lax.rsqrt(jnp.sum(txt * txt, axis=1, keepdims=True) + epsilon)
    txt_out[...] = jnp.where(keep, txt, 0.0).astype(bf16)
    copies[1].wait()
    hid_out[...] = jnp.where(keep, hid_in[...].astype(f32), 0.0).astype(bf16)


def join(after, own, paired, t1, t3, both, first, second):
    both[:ROWS] = own[...]
    both[ROWS:] = paired[...]
    first[...] = t3[: ROWS // 2]
    second[...] = t1[ROWS // 2 :]


def ahead(after, pair_ids, weight, held, chosen, left, right, sem):
    copy = pltpu.make_async_copy(weight, held, sem)
    copy.start()
    zh, x1, x0, y, c, zl = (lax.axis_index(a) for a in AXES)
    row = lax.broadcasted_iota(jnp.int32, (576, 1), 0)
    k, row = row // 144, row % 144
    j, row = row // 36, row % 36
    m, r = row // 9, row % 9
    turn = jnp.where(zl == 0, 4 - m, m)
    owner = (zh + turn) % 4
    place = owner * 288 + (k ^ (x1 * 2 + x0)) * 72 + (j ^ y) * 18 + c * 9 + r
    spots = lax.broadcasted_iota(jnp.int32, (576, WIDTH), 1)
    chosen[...] = (spots == place).astype(f32).astype(bf16)
    base = (zh * 2 + x1) * 16

    def label(px, py, pc):
        start = pl.multiple_of((base + (px * 4 + py) * 2 + pc) * ROWS, ROWS)
        return pair_ids[:, pl.ds(start, ROWS)]

    for k, (px, pc) in enumerate(((x0, c), (1 - x0, c), (x0, 1 - c), (1 - x0, 1 - c))):
        tall = jnp.transpose(jnp.broadcast_to(label(px, y, pc), (8, ROWS)))
        left[k * ROWS : (k + 1) * ROWS, :] = tall[:, :1]
    for j in range(4):
        right[:, j * ROWS : (j + 1) * ROWS] = label(x0, y ^ j, c)
    copy.wait()


def project(hid, weight, chosen, embed, normed, inverse, turned):
    projected = dot(hid[...], weight[...], 1, 0)
    turned[...] = dot(chosen[...], hid[...], 1, 1).astype(bf16)
    inv = lax.rsqrt(jnp.sum(projected * projected, axis=1, keepdims=True) + epsilon)
    unit = projected * inv
    normed[...] = unit
    embed[...] = unit.astype(bf16)
    inverse[...] = inv


def tile(scale, bias, left, right, e0, e1, n0, n1, i0, i1, t0, t1, t2a, t2b, t3, coef_out, part_out, part_send):
    txt = jnp.concatenate([t0[...], t1[...], t2a[...], t2b[...], t3[...]], 0)
    embed = jnp.concatenate([e0[...], e1[...]], 0)
    scores = scale[0] * dot(embed, txt, 1, 1) + bias[0]
    target = jnp.where(left[...] == right[...], 1.0, -1.0).astype(f32)
    coef = (-target * jax.nn.sigmoid(-target * scores) * scale[0]).astype(bf16)
    coef_out[...] = coef
    grad = dot(coef, txt, 1, 0)
    for k, (unit, inverse) in enumerate(((n0, i0), (n1, i1))):
        half = slice(k * 256, (k + 1) * 256)
        radial = jnp.sum(unit[...] * grad[half], axis=1, keepdims=True)
        part = (grad[half] - unit[...] * radial) * inverse[...]
        part_out[half, :] = part
        part_send[half, :] = part.astype(bf16)


def text_terms(coef, e0, e1, terms):
    terms[...] = dot(coef[:256], e0[...], 0, 0) + dot(coef[256:], e1[...], 0, 0)


def weight_terms(part, arrived, h0, h1, terms, rows, own, s1, s2, s3, t1, t2, t3):
    half = 2 * ROWS
    top = part[:half] + arrived[half:].astype(f32)
    low = part[half:] + arrived[:half].astype(f32)
    rows[...] = top
    grad = dot(h0[...], top.astype(bf16), 1, 0) + dot(h1[...], low.astype(bf16), 1, 0)
    own[...] = grad[:144]
    for k, out in enumerate((s1, s2, s3)):
        out[...] = grad[(k + 1) * 144 : (k + 2) * 144].astype(bf16)
    for k, out in enumerate((t1, t2, t3)):
        out[...] = terms[(k + 1) * ROWS : (k + 2) * ROWS].astype(bf16)


def first_sum(own, a1, a2, a3, b1, b2, b3, out, s1, s2, s3, held):
    held[...] = own[...] + a2[...].astype(f32) + a1[...].astype(f32) + a3[...].astype(f32)
    out[...] = held[:36]
    for k, send in enumerate((s1, s2, s3)):
        send[...] = held[(k + 1) * 36 : (k + 2) * 36].astype(bf16)


def second_sum(own, a1, a2, a3, rows, send, rows_send):
    total = own[...] + a2[...].astype(f32) + a1[...].astype(f32) + a3[...].astype(f32)
    send[...] = total.astype(bf16)
    rows_send[...] = rows[ROWS:].astype(bf16)


def third_sum(own, arrived, out, near, far, mine, held):
    mine[...] = own[...].astype(f32)
    held[...] = arrived[...].astype(f32)
    out[...] = mine[:9] + held[:9]
    near[...] = mine[9:18] + held[27:36]
    far[...] = mine[18:27] + held[18:27]


def last_sum(after, own, a1, a2, a3, out):
    out[...] = own[...] + (a1[...] + a2[...]) + a3[...]


def text_sum(after, count, terms, b1, b2, b3, out):
    keep = lax.broadcasted_iota(jnp.int32, (ROWS, 1), 0) < count[0]
    total = terms[:ROWS] + b2[...].astype(f32) + b1[...].astype(f32) + b3[...].astype(f32)
    out[...] = jnp.where(keep, total, 0.0)


def back(count, rows, arrived, weight, out, done):
    total = (rows[:ROWS] + arrived[...].astype(f32)).astype(bf16)
    grad = dot(total, weight[...], 1, 1)
    keep = lax.broadcasted_iota(jnp.int32, (ROWS, 1), 0) < count[0]
    out[...] = jnp.where(keep, grad, 0.0).astype(bf16)
    done[...] = jnp.zeros((8, ROWS), f32)


def per_device(hidden, weight, text, pair_ids, valid_count, logit_scale, logit_bias):
    X = ("x1", "x0")
    block = ROWS * WIDTH
    wide, tall = shape(bf16, ROWS, WIDTH), shape(f32, 512, WIDTH)
    with jax.named_scope("prepare"):
        hid, txt = call(
            prepare,
            [wide, wide],
            [SMEM, HBM, HBM],
            0,
            block,
            [pltpu.VMEM((ROWS, WIDTH), bf16)] * 2 + [pltpu.SemaphoreType.DMA((2,))],
        )(valid_count, in_hbm(hidden), in_hbm(text))
    with jax.named_scope("gather"):
        hid_x = xor(hid, "x0", 1)
        txt_1 = xor(txt, "y", 1)
        txt_3 = xor(txt, "y", 3)
        held, chosen, left, right = call(
            ahead,
            [
                shape(bf16, WIDTH, WIDTH),
                shape(bf16, 576, WIDTH),
                shape(jnp.int32, 512, 1),
                shape(jnp.int32, 1, 512),
            ],
            [ANY, VMEM, HBM],
            block * 1000,
            block,
            [pltpu.SemaphoreType.DMA],
        )(hid, pair_ids, in_hbm(weight))
        both, first, second = call(
            join,
            [shape(bf16, 256, WIDTH)] + [shape(bf16, 64, WIDTH)] * 2,
            [ANY] + [VMEM] * 4,
            0,
            block,
        )(chosen, hid, hid_x, txt_1, txt_3)
        txt_2a = xor(first, "y", 1)
        txt_2b = xor(second, "y", 3)
        hid_c = xor(both, "c", 1)
    with jax.named_scope("project"):
        outs = [shape(bf16, 256, WIDTH), shape(f32, 256, WIDTH), shape(f32, 256, 1), shape(bf16, 576, 256)]
        run = call(project, outs, [VMEM] * 3, 0, block)
        e0, n0, i0, h0 = run(both, held, chosen)
        e1, n1, i1, h1 = run(hid_c, held, chosen)
    with jax.named_scope("tile"):
        coef, part, part_send = call(
            tile,
            [shape(bf16, 512, 512), tall, shape(bf16, 512, WIDTH)],
            [SMEM, SMEM] + [VMEM] * 13,
            0,
            block,
        )(
            logit_scale.reshape(1), logit_bias.reshape(1), left, right,
            e0, e1, n0, n1, i0, i1, txt, txt_1, txt_2a, txt_2b, txt_3,
        )
    with jax.named_scope("core"):
        arrived = xor(part_send, "c", 1)
    with jax.named_scope("text"):
        (terms,) = call(text_terms, [tall], [VMEM] * 3, 0, block)(coef, e0, e1)
    with jax.named_scope("weight"):
        rows, own, s1, s2, s3, u1, u2, u3 = call(
            weight_terms,
            [shape(f32, 256, WIDTH), shape(f32, 144, WIDTH)]
            + [shape(bf16, 144, WIDTH)] * 3
            + [wide] * 3,
            [VMEM] * 5,
            0,
            block,
        )(part, arrived, h0, h1, terms)
        s2, s1, s3 = xor(s2, X, 2), xor(s1, X, 1), xor(s3, X, 3)
        u1, u3, u2 = xor(u1, "y", 1), xor(u3, "y", 3), xor(u2, "y", 2)
        small, small_b = shape(f32, 36, WIDTH), shape(bf16, 36, WIDTH)
        whole, s1, s2, s3 = call(
            first_sum,
            [small] + [small_b] * 3,
            [VMEM] * 4 + [ANY] * 3,
            0,
            block,
            [pltpu.VMEM((144, WIDTH), f32)],
        )(own, s1, s2, s3, u1, u2, u3)
        s2, s1, s3 = xor(s2, "y", 2), xor(s1, "y", 1), xor(s3, "y", 3)
        whole_send, rows_send = call(second_sum, [small_b, wide], [VMEM] * 5, 0, block)(
            whole, s1, s2, s3, rows
        )
        arrived = xor(whole_send, "zl", 1)
        whole, near, far = call(
            third_sum,
            [shape(f32, 9, WIDTH)] * 3,
            [VMEM] * 2,
            0,
            block,
            [pltpu.VMEM((36, WIDTH), f32)] * 2,
        )(whole_send, arrived)
        Z = ("zh", "zl")
        steps = (near, 1), (near, 2), (far, 3)
        got = [
            lax.ppermute(x, Z, [(p, (p + (hop if p % 2 else -hop)) % 8) for p in range(8)])
            for x, hop in steps
        ]
    with jax.named_scope("hidden"):
        rows_x = xor(rows_send, "x0", 1)
        hidden_grad, done = call(
            back, [wide, shape(f32, 8, ROWS)], [SMEM] + [VMEM] * 3, 2 * block * WIDTH, WIDTH * WIDTH * 2
        )(valid_count, rows, rows_x, held)
    with jax.named_scope("weight"):
        (weight_grad,) = call(last_sum, [shape(f32, 9, WIDTH)], [ANY] + [VMEM] * 4, 0, block)(
            done, whole, *got
        )
    with jax.named_scope("text"):
        (text_grad,) = call(
            text_sum, [shape(f32, ROWS, WIDTH)], [ANY, SMEM] + [VMEM] * 4, 0, block * 16
        )(whole_send, valid_count, terms, u1, u2, u3)
    return hidden_grad, weight_grad, text_grad


def solution(mesh):
    fine = Mesh(mesh.devices.reshape(4, 2, 2, 4, 2, 2), AXES)
    blk = ("zh", "x1", "x0", "y", "c")
    by_row = P(("zl",) + blk, None)
    return jax.shard_map(
        per_device,
        mesh=fine,
        in_specs=(by_row, P(), by_row, P("zl", None), P(("zl",) + blk), P(), P()),
        out_specs=(by_row, P(blk, None), by_row),
        check_vma=False,
    )
```

time: 85.5 us -> 86.4 us (1.011)
  the two profiles are of different devices: /device:TPU:32 before, /device:TPU:2 now
where the time goes in v4:
time: 86.4 us; the launch traced here: 86.1 us
  starting transfers between devices  33.8 us (39%)
  waiting for transfers between devices  28.8 us (33%)
  Pallas kernels  17.6 us (20%)
  local copies, waits for them, and re-layouts  3.25 us (4%)
  between operations  2.72 us (3%)
    ppermute x18, waiting for transfers between devices, xor(): return lax.ppermute(x, axis, [(i, i ^ step) for i in range(size)])  28.3 us
    ppermute x18, starting transfers between devices, xor(): return lax.ppermute(x, axis, [(i, i ^ step) for i in range(size)])  23.3 us
    ppermute x3, starting transfers between devices, per_device(): lax.ppermute(x, Z, [(p, (p + (hop if p % 2 else -hop)) % 8) for p in rang...  10.5 us
    unnamed x10, local copies, waits for them, and re-layouts  3.25 us
    pallas_call x1, Pallas kernels, per_device(): call(tile, [shape(bf16, 512, 512), tall, shape(bf16, 512, WIDTH)], [SMEM,...  3.01 us
    pallas_call x1, Pallas kernels, per_device(): e1, n1, i1, h1 = run(hid_c, held, chosen)  2.55 us
    pallas_call x1, Pallas kernels, per_device(): e0, n0, i0, h0 = run(both, held, chosen)  2.51 us
    pallas_call x1, Pallas kernels, per_device(): call(ahead, [shape(bf16, WIDTH, WIDTH), shape(bf16, 576, WIDTH), shape(jn...  1.78 us
  transfers between devices with their start and end apart: 21, of which 12 were waited for; matrix products, arithmetic and copies ran while one was open for 0% of the time, Pallas kernels for 12%

profile of v4, /device:TPU:2, one launch (start us, length us, event | category | flops | bytes accessed | tf_op | source)
XLA Modules:
  0.0 86.1 jit_solution(1550363834253639659)
XLA Ops:
  2.5 2.4 %collective-permute-start = (bf16[128,1152]{1,0:T(8,128)(2,1)S(1)}, bf16[128,1152]{1,0:T(8,128)(2,1)S(1)}, u32[]{:S(2)}, u32[]{:S(2)}) collective-permute-start(bf16[128,1152]{1,0:T(8,128)(2,1)S(1)} %get-tuple-element.42.after.own), channel_id=1, source_target_pairs={{0,16},{16,0},{1,17},{17,1},{2,18},{18,2},{3,19},{19,3},{4,20},{20... | collective-permute-start | bytes 884744 | tf_op jit(solution)/shard_map/gather/ppermute | solution.py:26
  7.1 1.8 %gather.2 = (bf16[1152,1152]{1,0:T(8,128)(2,1)S(1)}, bf16[576,1152]{1,0:T(8,128)(2,1)S(1)}, s32[512,1]{1,0:T(8,128)S(1)}, s32[1,512]{1,0:T(1,128)S(1)}) custom-call(bf16[128,1152]{1,0:T(8,128)(2,1)S(1)} %get-tuple-element.42.after.own, s32[1,16384]{1,0:T(1,128)S(1)} %copy-done.4, bf16[1152,1152]{1,0:T(8,128)(2,1)} %weight.6), custom_call_target="tpu_custom_call" | custom-call | flops 147456000 | bytes 147456 | tf_op jit(solution)/shard_map/gather/pallas_call | solution.py:198
  8.9 2.4 %collective-permute-done.paired = bf16[128,1152]{1,0:T(8,128)(2,1)S(1)} collective-permute-done((bf16[128,1152]{1,0:T(8,128)(2,1)S(1)}, bf16[128,1152]{1,0:T(8,128)(2,1)S(1)}, u32[]{:S(2)}, u32[]{:S(2)}) %collective-permute-start) | collective-permute-done | bytes 294944 | tf_op jit(solution)/shard_map/gather/ppermute | solution.py:26
  20.5 2.5 %project.2 = (bf16[256,1152]{1,0:T(8,128)(2,1)S(1)}, f32[256,1152]{1,0:T(8,128)S(1)}, f32[256,1]{1,0:T(8,128)S(1)}, bf16[576,256]{1,0:T(8,128)(2,1)S(1)}) custom-call(bf16[256,1152]{1,0:T(8,128)(2,1)} %get-tuple-element.47.hid, bf16[1152,1152]{1,0:T(8,128)(2,1)S(1)} %get-tuple-element.48.weight, bf16[576,1152]{1,0:T(8,128)(2,1)S(1)} %copy-done.1), custom_call_target="tpu_custom_call" | custom-call | bytes 147456 | tf_op jit(solution)/shard_map/project/pallas_call | solution.py:224
  23.0 2.6 %project.3 = (bf16[256,1152]{1,0:T(8,128)(2,1)S(1)}, f32[256,1152]{1,0:T(8,128)S(1)}, f32[256,1]{1,0:T(8,128)S(1)}, bf16[576,256]{1,0:T(8,128)(2,1)S(1)}) custom-call(bf16[256,1152]{1,0:T(8,128)(2,1)} %collective-permute-done.3.hid, bf16[1152,1152]{1,0:T(8,128)(2,1)S(1)} %get-tuple-element.48.weight, bf16[576,1152]{1,0:T(8,128)(2,1)S(1)} %copy-done.1), custom_call_target="tpu_custom_call" | custom-call | bytes 147456 | tf_op jit(solution)/shard_map/project/pallas_call | solution.py:225
  25.6 3.0 %tile.1 = (bf16[512,512]{1,0:T(8,128)(2,1)S(1)}, f32[512,1152]{1,0:T(8,128)S(1)}, bf16[512,1152]{1,0:T(8,128)(2,1)S(1)}) custom-call(f32[1]{0:T(128)} %bitcast.2.scale, f32[1]{0:T(128)} %bitcast.3.bias, s32[512,1]{1,0:T(8,128)S(1)} %copy-done.3, s32[1,512]{1,0:T(1,128)S(1)} %get-tuple-element.44.right, bf16[256,1152]{1,0:T(8,128)(2,1)S(1)} %get-tuple-element.49.e0, ...), custom_call_target="tpu_custom_call" | custom-call | bytes 147456 | tf_op jit(solution)/shard_map/tile/pallas_call | solution.py:227
  29.8 1.7 %collective-permute-done.6.arrived = bf16[512,1152]{1,0:T(8,128)(2,1)S(1)} collective-permute-done((bf16[512,1152]{1,0:T(8,128)(2,1)S(1)}, bf16[512,1152]{1,0:T(8,128)(2,1)S(1)}, u32[]{:S(2)}, u32[]{:S(2)}) %collective-permute-start.6) | collective-permute-done | bytes 1179680 | tf_op jit(solution)/shard_map/core/ppermute | solution.py:26
  32.6 1.7 %collective-permute-start.10 = (bf16[128,1152]{1,0:T(8,128)(2,1)S(1)}, bf16[128,1152]{1,0:T(8,128)(2,1)S(1)}, u32[]{:S(2)}, u32[]{:S(2)}) collective-permute-start(bf16[128,1152]{1,0:T(8,128)(2,1)S(1)} %get-tuple-element.67), channel_id=1, source_target_pairs={{0,4},{4,0},{8,12},{12,8},{1,5},{5,1},{9,13},{13,9},{2,6},{6,2},{1... | collective-permute-start | bytes 884744 | tf_op jit(solution)/shard_map/weight/ppermute | solution.py:26
  35.8 2.1 %collective-permute-start.8 = (bf16[144,1152]{1,0:T(8,128)(2,1)S(1)}, bf16[144,1152]{1,0:T(8,128)(2,1)S(1)}, u32[]{:S(2)}, u32[]{:S(2)}) collective-permute-start(bf16[144,1152]{1,0:T(8,128)(2,1)S(1)} %get-tuple-element.65), channel_id=1, source_target_pairs={{0,32},{16,48},{32,0},{48,16},{1,33},{17,49},{33,1},{49,17},{2,34}... | collective-permute-start | bytes 995336 | tf_op jit(solution)/shard_map/weight/ppermute | solution.py:26
  37.9 2.1 %collective-permute-start.11 = (bf16[128,1152]{1,0:T(8,128)(2,1)S(1)}, bf16[128,1152]{1,0:T(8,128)(2,1)S(1)}, u32[]{:S(2)}, u32[]{:S(2)}) collective-permute-start(bf16[128,1152]{1,0:T(8,128)(2,1)S(1)} %get-tuple-element.68), channel_id=1, source_target_pairs={{0,8},{4,12},{8,0},{12,4},{1,9},{5,13},{9,1},{13,5},{2,10},{6,14},... | collective-permute-start | bytes 884744 | tf_op jit(solution)/shard_map/weight/ppermute | solution.py:26
  40.0 2.7 %collective-permute-done.10.b1 = bf16[128,1152]{1,0:T(8,128)(2,1)S(1)} collective-permute-done((bf16[128,1152]{1,0:T(8,128)(2,1)S(1)}, bf16[128,1152]{1,0:T(8,128)(2,1)S(1)}, u32[]{:S(2)}, u32[]{:S(2)}) %collective-permute-start.10) | collective-permute-done | bytes 294944 | tf_op jit(solution)/shard_map/weight/ppermute | solution.py:26
  42.7 2.0 %collective-permute-start.12 = (bf16[128,1152]{1,0:T(8,128)(2,1)S(1)}, bf16[128,1152]{1,0:T(8,128)(2,1)S(1)}, u32[]{:S(2)}, u32[]{:S(2)}) collective-permute-start(bf16[128,1152]{1,0:T(8,128)(2,1)S(1)} %get-tuple-element.69), channel_id=1, source_target_pairs={{0,12},{4,8},{8,4},{12,0},{1,13},{5,9},{9,5},{13,1},{2,14},{6,10},... | collective-permute-start | bytes 884744 | tf_op jit(solution)/shard_map/weight/ppermute | solution.py:26
  44.7 5.1 %collective-permute-done.11.b2 = bf16[128,1152]{1,0:T(8,128)(2,1)S(1)} collective-permute-done((bf16[128,1152]{1,0:T(8,128)(2,1)S(1)}, bf16[128,1152]{1,0:T(8,128)(2,1)S(1)}, u32[]{:S(2)}, u32[]{:S(2)}) %collective-permute-start.11) | collective-permute-done | bytes 294944 | tf_op jit(solution)/shard_map/weight/ppermute | solution.py:26
  49.8 6.2 %collective-permute-done.12.b3 = bf16[128,1152]{1,0:T(8,128)(2,1)S(1)} collective-permute-done((bf16[128,1152]{1,0:T(8,128)(2,1)S(1)}, bf16[128,1152]{1,0:T(8,128)(2,1)S(1)}, u32[]{:S(2)}, u32[]{:S(2)}) %collective-permute-start.12) | collective-permute-done | bytes 294944 | tf_op jit(solution)/shard_map/weight/ppermute | solution.py:26
  56.9 2.2 %collective-permute-start.14 = (bf16[36,1152]{1,0:T(8,128)(2,1)S(1)}, bf16[36,1152]{1,0:T(8,128)(2,1)S(1)}, u32[]{:S(2)}, u32[]{:S(2)}) collective-permute-start(bf16[36,1152]{1,0:T(8,128)(2,1)S(1)} %get-tuple-element.72), channel_id=1, source_target_pairs={{0,8},{4,12},{8,0},{12,4},{1,9},{5,13},{9,1},{13,5},{2,10},{6,14},... | collective-permute-start | bytes 248840 | tf_op jit(solution)/shard_map/weight/ppermute | solution.py:26
  59.1 1.9 %collective-permute-start.15 = (bf16[36,1152]{1,0:T(8,128)(2,1)S(1)}, bf16[36,1152]{1,0:T(8,128)(2,1)S(1)}, u32[]{:S(2)}, u32[]{:S(2)}) collective-permute-start(bf16[36,1152]{1,0:T(8,128)(2,1)S(1)} %get-tuple-element.73), channel_id=1, source_target_pairs={{0,12},{4,8},{8,4},{12,0},{1,13},{5,9},{9,5},{13,1},{2,14},{6,10},... | collective-permute-start | bytes 248840 | tf_op jit(solution)/shard_map/weight/ppermute | solution.py:26
  61.9 1.9 %collective-permute-done.14.a2 = bf16[36,1152]{1,0:T(8,128)(2,1)S(1)} collective-permute-done((bf16[36,1152]{1,0:T(8,128)(2,1)S(1)}, bf16[36,1152]{1,0:T(8,128)(2,1)S(1)}, u32[]{:S(2)}, u32[]{:S(2)}) %collective-permute-start.14) | collective-permute-done | bytes 82976 | tf_op jit(solution)/shard_map/weight/ppermute | solution.py:26
  63.8 1.7 %collective-permute-done.15.a3 = bf16[36,1152]{1,0:T(8,128)(2,1)S(1)} collective-permute-done((bf16[36,1152]{1,0:T(8,128)(2,1)S(1)}, bf16[36,1152]{1,0:T(8,128)(2,1)S(1)}, u32[]{:S(2)}, u32[]{:S(2)}) %collective-permute-start.15) | collective-permute-done | bytes 82976 | tf_op jit(solution)/shard_map/weight/ppermute | solution.py:26
  65.6 1.6 %collective-permute-start.16 = (bf16[128,1152]{1,0:T(8,128)(2,1)S(1)}, bf16[128,1152]{1,0:T(8,128)(2,1)S(1)}, u32[]{:S(2)}, u32[]{:S(2)}) collective-permute-start(bf16[128,1152]{1,0:T(8,128)(2,1)S(1)} %get-tuple-element.74), channel_id=1, source_target_pairs={{0,16},{16,0},{1,17},{17,1},{2,18},{18,2},{3,19},{19,3},{4,20},{20... | collective-permute-start | bytes 884744 | tf_op jit(solution)/shard_map/hidden/ppermute | solution.py:26
  67.2 1.9 %collective-permute-start.17 = (bf16[36,1152]{1,0:T(8,128)(2,1)S(1)}, bf16[36,1152]{1,0:T(8,128)(2,1)S(1)}, u32[]{:S(2)}, u32[]{:S(2)}) collective-permute-start(bf16[36,1152]{1,0:T(8,128)(2,1)S(1)} %get-tuple-element.77.own.after), channel_id=1, source_target_pairs={{0,1},{1,0},{2,3},{3,2},{4,5},{5,4},{6,7},{7,6},{8,9},{9,8},{10,11... | collective-permute-start | bytes 248840 | tf_op jit(solution)/shard_map/weight/ppermute | solution.py:26
  69.1 2.6 %collective-permute-done.17.arrived = bf16[36,1152]{1,0:T(8,128)(2,1)S(1)} collective-permute-done((bf16[36,1152]{1,0:T(8,128)(2,1)S(1)}, bf16[36,1152]{1,0:T(8,128)(2,1)S(1)}, u32[]{:S(2)}, u32[]{:S(2)}) %collective-permute-start.17) | collective-permute-done | bytes 82976 | tf_op jit(solution)/shard_map/weight/ppermute | solution.py:26
  71.8 6.8 %collective-permute-start.20 = (f32[9,1152]{1,0:T(8,128)S(1)}, f32[9,1152]{1,0:T(8,128)S(1)}, u32[]{:S(2)}, u32[]{:S(2)}) collective-permute-start(f32[9,1152]{1,0:T(8,128)S(1)} %get-tuple-element.80), channel_id=1, source_target_pairs={{0,129},{1,128},{64,193},{65,192},{128,1},{129,0},{192,65},{193,64... | collective-permute-start | bytes 124424 | tf_op jit(solution)/shard_map/weight/ppermute | solution.py:278
  79.2 3.1 %collective-permute-start.18 = (f32[9,1152]{1,0:T(8,128)S(1)}, f32[9,1152]{1,0:T(8,128)S(1)}, u32[]{:S(2)}, u32[]{:S(2)}) collective-permute-start(f32[9,1152]{1,0:T(8,128)S(1)} %get-tuple-element.79), channel_id=1, source_target_pairs={{0,193},{1,64},{64,1},{65,128},{128,65},{129,192},{192,129},{193,0... | collective-permute-start | bytes 124424 | tf_op jit(solution)/shard_map/weight/ppermute | solution.py:278
  83.3 1.6 %hidden.3 = (bf16[128,1152]{1,0:T(8,128)(2,1)}, f32[8,128]{1,0:T(8,128)S(1)}) custom-call(s32[1]{0:T(128)S(6)} %copy.10.count, f32[256,1152]{1,0:T(8,128)S(1)} %get-tuple-element.62.rows, bf16[128,1152]{1,0:T(8,128)(2,1)S(1)} %collective-permute-done.16.arrived, bf16[1152,1152]{1,0:T(8,128)(2,1)S(1)} %get-tuple-element.48.weight), custom_call_target="tpu_custom_call" | custom-call | flops 339738624 | bytes 2654208 | tf_op jit(solution)/shard_map/hidden/pallas_call | solution.py:283
  (42 shorter events, 19.5 us)
Async XLA Ops:
  2.5 8.8 %collective-permute-start = (bf16[128,1152]{1,0:T(8,128)(2,1)S(1)}, bf16[128,1152]{1,0:T(8,128)(2,1)S(1)}, u32[]{:S(2)}, u32[]{:S(2)}) collective-permute-start(bf16[128,1152]{1,0:T(8,128)(2,1)S(1)} %get-tuple-element.42.after.own), channel_id=1, source_target_pairs={{0,16},{16,0},{1,17},{17,1},{2,18},{18,2},{3,19},{19,3},{4,20},{20... | collective-permute-start | bytes 884744 | tf_op jit(solution)/shard_map/gather/ppermute | solution.py:26
  4.8 8.0 %collective-permute-start.2 = (bf16[128,1152]{1,0:T(8,128)(2,1)S(1)}, bf16[128,1152]{1,0:T(8,128)(2,1)S(1)}, u32[]{:S(2)}, u32[]{:S(2)}) collective-permute-start(bf16[128,1152]{1,0:T(8,128)(2,1)S(1)} %get-tuple-element.46.t0), channel_id=1, source_target_pairs={{0,12},{4,8},{8,4},{12,0},{1,13},{5,9},{9,5},{13,1},{2,14},{6,10},... | collective-permute-start | bytes 884744 | tf_op jit(solution)/shard_map/gather/ppermute | solution.py:26
  6.1 8.2 %collective-permute-start.1 = (bf16[128,1152]{1,0:T(8,128)(2,1)S(1)}, bf16[128,1152]{1,0:T(8,128)(2,1)S(1)}, u32[]{:S(2)}, u32[]{:S(2)}) collective-permute-start(bf16[128,1152]{1,0:T(8,128)(2,1)S(1)} %get-tuple-element.46.t0), channel_id=1, source_target_pairs={{0,4},{4,0},{8,12},{12,8},{1,5},{5,1},{9,13},{13,9},{2,6},{6,2},{1... | collective-permute-start | bytes 884744 | tf_op jit(solution)/shard_map/gather/ppermute | solution.py:26
  8.9 6.4 %copy-start.2 = (s32[512,1]{1,0:T(8,128)}, s32[512,1]{1,0:T(8,128)S(1)}, u32[]{:S(2)}) copy-start(s32[512,1]{1,0:T(8,128)S(1)} %get-tuple-element.43.left) | copy-start | bytes 6148
  16.3 6.7 %collective-permute-start.3 = (bf16[256,1152]{1,0:T(8,128)(2,1)}, bf16[256,1152]{1,0:T(8,128)(2,1)}, u32[]{:S(2)}, u32[]{:S(2)}) collective-permute-start(bf16[256,1152]{1,0:T(8,128)(2,1)} %get-tuple-element.47.hid), channel_id=1, source_target_pairs={{0,2},{2,0},{1,3},{3,1},{4,6},{6,4},{5,7},{7,5},{8,10},{10,8},{9,1... | collective-permute-start | bytes 1769480 | tf_op jit(solution)/shard_map/gather/ppermute | solution.py:26
  16.3 9.2 %collective-permute-start.4 = (bf16[64,1152]{1,0:T(8,128)(2,1)}, bf16[64,1152]{1,0:T(8,128)(2,1)}, u32[]{:S(2)}, u32[]{:S(2)}) collective-permute-start(bf16[64,1152]{1,0:T(8,128)(2,1)} %get-tuple-element.55), channel_id=1, source_target_pairs={{0,4},{4,0},{8,12},{12,8},{1,5},{5,1},{9,13},{13,9},{2,6},{6,2},{1... | collective-permute-start | bytes 442376 | tf_op jit(solution)/shard_map/gather/ppermute | solution.py:26
  16.6 8.9 %collective-permute-start.5 = (bf16[64,1152]{1,0:T(8,128)(2,1)}, bf16[64,1152]{1,0:T(8,128)(2,1)}, u32[]{:S(2)}, u32[]{:S(2)}) collective-permute-start(bf16[64,1152]{1,0:T(8,128)(2,1)} %get-tuple-element.56), channel_id=1, source_target_pairs={{0,12},{4,8},{8,4},{12,0},{1,13},{5,9},{9,5},{13,1},{2,14},{6,10},... | collective-permute-start | bytes 442376 | tf_op jit(solution)/shard_map/gather/ppermute | solution.py:26
  19.1 1.3 %copy-start.1 = (bf16[576,1152]{1,0:T(8,128)(2,1)S(1)}, bf16[576,1152]{1,0:T(8,128)(2,1)}, u32[]{:S(2)}) copy-start(bf16[576,1152]{1,0:T(8,128)(2,1)} %copy-done) | copy-start | bytes 3981316
  23.0 2.6 %copy-start.3 = (s32[512,1]{1,0:T(8,128)S(1)}, s32[512,1]{1,0:T(8,128)}, u32[]{:S(2)}) copy-start(s32[512,1]{1,0:T(8,128)} %copy-done.2) | copy-start | bytes 6148
  28.6 2.9 %collective-permute-start.6 = (bf16[512,1152]{1,0:T(8,128)(2,1)S(1)}, bf16[512,1152]{1,0:T(8,128)(2,1)S(1)}, u32[]{:S(2)}, u32[]{:S(2)}) collective-permute-start(bf16[512,1152]{1,0:T(8,128)(2,1)S(1)} %get-tuple-element.58), channel_id=1, source_target_pairs={{0,2},{2,0},{1,3},{3,1},{4,6},{6,4},{5,7},{7,5},{8,10},{10,8},{9,1... | collective-permute-start | bytes 3538952 | tf_op jit(solution)/shard_map/core/ppermute | solution.py:26
  32.6 10.1 %collective-permute-start.10 = (bf16[128,1152]{1,0:T(8,128)(2,1)S(1)}, bf16[128,1152]{1,0:T(8,128)(2,1)S(1)}, u32[]{:S(2)}, u32[]{:S(2)}) collective-permute-start(bf16[128,1152]{1,0:T(8,128)(2,1)S(1)} %get-tuple-element.67), channel_id=1, source_target_pairs={{0,4},{4,0},{8,12},{12,8},{1,5},{5,1},{9,13},{13,9},{2,6},{6,2},{1... | collective-permute-start | bytes 884744 | tf_op jit(solution)/shard_map/weight/ppermute | solution.py:26
  34.3 21.7 %collective-permute-start.7 = (bf16[144,1152]{1,0:T(8,128)(2,1)S(1)}, bf16[144,1152]{1,0:T(8,128)(2,1)S(1)}, u32[]{:S(2)}, u32[]{:S(2)}) collective-permute-start(bf16[144,1152]{1,0:T(8,128)(2,1)S(1)} %get-tuple-element.64), channel_id=1, source_target_pairs={{0,16},{16,0},{32,48},{48,32},{1,17},{17,1},{33,49},{49,33},{2,18}... | collective-permute-start | bytes 995336 | tf_op jit(solution)/shard_map/weight/ppermute | solution.py:26
  35.8 20.2 %collective-permute-start.8 = (bf16[144,1152]{1,0:T(8,128)(2,1)S(1)}, bf16[144,1152]{1,0:T(8,128)(2,1)S(1)}, u32[]{:S(2)}, u32[]{:S(2)}) collective-permute-start(bf16[144,1152]{1,0:T(8,128)(2,1)S(1)} %get-tuple-element.65), channel_id=1, source_target_pairs={{0,32},{16,48},{32,0},{48,16},{1,33},{17,49},{33,1},{49,17},{2,34}... | collective-permute-start | bytes 995336 | tf_op jit(solution)/shard_map/weight/ppermute | solution.py:26
  37.9 18.1 %collective-permute-start.9 = (bf16[144,1152]{1,0:T(8,128)(2,1)S(1)}, bf16[144,1152]{1,0:T(8,128)(2,1)S(1)}, u32[]{:S(2)}, u32[]{:S(2)}) collective-permute-start(bf16[144,1152]{1,0:T(8,128)(2,1)S(1)} %get-tuple-element.66), channel_id=1, source_target_pairs={{0,48},{16,32},{32,16},{48,0},{1,49},{17,33},{33,17},{49,1},{2,50}... | collective-permute-start | bytes 995336 | tf_op jit(solution)/shard_map/weight/ppermute | solution.py:26
  37.9 11.9 %collective-permute-start.11 = (bf16[128,1152]{1,0:T(8,128)(2,1)S(1)}, bf16[128,1152]{1,0:T(8,128)(2,1)S(1)}, u32[]{:S(2)}, u32[]{:S(2)}) collective-permute-start(bf16[128,1152]{1,0:T(8,128)(2,1)S(1)} %get-tuple-element.68), channel_id=1, source_target_pairs={{0,8},{4,12},{8,0},{12,4},{1,9},{5,13},{9,1},{13,5},{2,10},{6,14},... | collective-permute-start | bytes 884744 | tf_op jit(solution)/shard_map/weight/ppermute | solution.py:26
  42.7 13.3 %collective-permute-start.12 = (bf16[128,1152]{1,0:T(8,128)(2,1)S(1)}, bf16[128,1152]{1,0:T(8,128)(2,1)S(1)}, u32[]{:S(2)}, u32[]{:S(2)}) collective-permute-start(bf16[128,1152]{1,0:T(8,128)(2,1)S(1)} %get-tuple-element.69), channel_id=1, source_target_pairs={{0,12},{4,8},{8,4},{12,0},{1,13},{5,9},{9,5},{13,1},{2,14},{6,10},... | collective-permute-start | bytes 884744 | tf_op jit(solution)/shard_map/weight/ppermute | solution.py:26
  56.3 5.6 %collective-permute-start.13 = (bf16[36,1152]{1,0:T(8,128)(2,1)S(1)}, bf16[36,1152]{1,0:T(8,128)(2,1)S(1)}, u32[]{:S(2)}, u32[]{:S(2)}) collective-permute-start(bf16[36,1152]{1,0:T(8,128)(2,1)S(1)} %get-tuple-element.71), channel_id=1, source_target_pairs={{0,4},{4,0},{8,12},{12,8},{1,5},{5,1},{9,13},{13,9},{2,6},{6,2},{1... | collective-permute-start | bytes 248840 | tf_op jit(solution)/shard_map/weight/ppermute | solution.py:26
  56.9 6.9 %collective-permute-start.14 = (bf16[36,1152]{1,0:T(8,128)(2,1)S(1)}, bf16[36,1152]{1,0:T(8,128)(2,1)S(1)}, u32[]{:S(2)}, u32[]{:S(2)}) collective-permute-start(bf16[36,1152]{1,0:T(8,128)(2,1)S(1)} %get-tuple-element.72), channel_id=1, source_target_pairs={{0,8},{4,12},{8,0},{12,4},{1,9},{5,13},{9,1},{13,5},{2,10},{6,14},... | collective-permute-start | bytes 248840 | tf_op jit(solution)/shard_map/weight/ppermute | solution.py:26
  59.1 6.4 %collective-permute-start.15 = (bf16[36,1152]{1,0:T(8,128)(2,1)S(1)}, bf16[36,1152]{1,0:T(8,128)(2,1)S(1)}, u32[]{:S(2)}, u32[]{:S(2)}) collective-permute-start(bf16[36,1152]{1,0:T(8,128)(2,1)S(1)} %get-tuple-element.73), channel_id=1, source_target_pairs={{0,12},{4,8},{8,4},{12,0},{1,13},{5,9},{9,5},{13,1},{2,14},{6,10},... | collective-permute-start | bytes 248840 | tf_op jit(solution)/shard_map/weight/ppermute | solution.py:26
  65.6 17.7 %collective-permute-start.16 = (bf16[128,1152]{1,0:T(8,128)(2,1)S(1)}, bf16[128,1152]{1,0:T(8,128)(2,1)S(1)}, u32[]{:S(2)}, u32[]{:S(2)}) collective-permute-start(bf16[128,1152]{1,0:T(8,128)(2,1)S(1)} %get-tuple-element.74), channel_id=1, source_target_pairs={{0,16},{16,0},{1,17},{17,1},{2,18},{18,2},{3,19},{19,3},{4,20},{20... | collective-permute-start | bytes 884744 | tf_op jit(solution)/shard_map/hidden/ppermute | solution.py:26
  67.2 4.6 %collective-permute-start.17 = (bf16[36,1152]{1,0:T(8,128)(2,1)S(1)}, bf16[36,1152]{1,0:T(8,128)(2,1)S(1)}, u32[]{:S(2)}, u32[]{:S(2)}) collective-permute-start(bf16[36,1152]{1,0:T(8,128)(2,1)S(1)} %get-tuple-element.77.own.after), channel_id=1, source_target_pairs={{0,1},{1,0},{2,3},{3,2},{4,5},{5,4},{6,7},{7,6},{8,9},{9,8},{10,11... | collective-permute-start | bytes 248840 | tf_op jit(solution)/shard_map/weight/ppermute | solution.py:26
  71.8 13.1 %collective-permute-start.20 = (f32[9,1152]{1,0:T(8,128)S(1)}, f32[9,1152]{1,0:T(8,128)S(1)}, u32[]{:S(2)}, u32[]{:S(2)}) collective-permute-start(f32[9,1152]{1,0:T(8,128)S(1)} %get-tuple-element.80), channel_id=1, source_target_pairs={{0,129},{1,128},{64,193},{65,192},{128,1},{129,0},{192,65},{193,64... | collective-permute-start | bytes 124424 | tf_op jit(solution)/shard_map/weight/ppermute | solution.py:278
  78.6 6.3 %collective-permute-start.19 = (f32[9,1152]{1,0:T(8,128)S(1)}, f32[9,1152]{1,0:T(8,128)S(1)}, u32[]{:S(2)}, u32[]{:S(2)}) collective-permute-start(f32[9,1152]{1,0:T(8,128)S(1)} %get-tuple-element.79), channel_id=1, source_target_pairs={{0,192},{1,65},{64,0},{65,129},{128,64},{129,193},{192,128},{193,1... | collective-permute-start | bytes 124424 | tf_op jit(solution)/shard_map/weight/ppermute | solution.py:278
  79.2 6.3 %collective-permute-start.18 = (f32[9,1152]{1,0:T(8,128)S(1)}, f32[9,1152]{1,0:T(8,128)S(1)}, u32[]{:S(2)}, u32[]{:S(2)}) collective-permute-start(f32[9,1152]{1,0:T(8,128)S(1)} %get-tuple-element.79), channel_id=1, source_target_pairs={{0,193},{1,64},{64,1},{65,128},{128,65},{129,192},{192,129},{193,0... | collective-permute-start | bytes 124424 | tf_op jit(solution)/shard_map/weight/ppermute | solution.py:278
  (2 other events, 1.9 us)

commit v5 on v4

--- a/solution.py
+++ b/solution.py
@@ -34,14 +34,14 @@
     return pltpu.with_memory_space_constraint(x, pltpu.HBM)
 
 
-def call(body, outs, specs, flops, moved, scratch=()):
+def call(body, outs, specs, flops, moved, scratch=(), vmem=8):
     return pl.pallas_call(
         body,
         out_shape=outs,
         in_specs=specs,
         out_specs=[VMEM] * len(outs),
         scratch_shapes=scratch,
-        compiler_params=pltpu.CompilerParams(vmem_limit_bytes=40 << 20),
+        compiler_params=pltpu.CompilerParams(vmem_limit_bytes=vmem << 20),
         cost_estimate=pl.CostEstimate(flops=flops, bytes_accessed=moved, transcendentals=0),
     )
 
@@ -96,9 +96,10 @@
     copy.wait()
 
 
-def project(hid, weight, chosen, embed, normed, inverse, turned):
-    projected = dot(hid[...], weight[...], 1, 0)
-    turned[...] = dot(chosen[...], hid[...], 1, 1).astype(bf16)
+def project(both, cores, weight, chosen, embed, normed, inverse, turned):
+    hid = jnp.concatenate([both[...], cores[...]], 0)
+    projected = dot(hid, weight[...], 1, 0)
+    turned[...] = dot(chosen[...], hid, 1, 1).astype(bf16)
     inv = lax.rsqrt(jnp.sum(projected * projected, axis=1, keepdims=True) + epsilon)
     unit = projected * inv
     normed[...] = unit
@@ -106,50 +107,49 @@
     inverse[...] = inv
 
 
-def tile(scale, bias, left, right, e0, e1, n0, n1, i0, i1, t0, t1, t2a, t2b, t3, coef_out, part_out, part_send):
+def tile(scale, bias, left, right, embed, normed, inverse, t0, t1, t2a, t2b, t3, coef_out, part_out, part_send):
     txt = jnp.concatenate([t0[...], t1[...], t2a[...], t2b[...], t3[...]], 0)
-    embed = jnp.concatenate([e0[...], e1[...]], 0)
-    scores = scale[0] * dot(embed, txt, 1, 1) + bias[0]
+    scores = scale[0] * dot(embed[...], txt, 1, 1) + bias[0]
     target = jnp.where(left[...] == right[...], 1.0, -1.0).astype(f32)
     coef = (-target * jax.nn.sigmoid(-target * scores) * scale[0]).astype(bf16)
     coef_out[...] = coef
     grad = dot(coef, txt, 1, 0)
-    for k, (unit, inverse) in enumerate(((n0, i0), (n1, i1))):
-        half = slice(k * 256, (k + 1) * 256)
-        radial = jnp.sum(unit[...] * grad[half], axis=1, keepdims=True)
-        part = (grad[half] - unit[...] * radial) * inverse[...]
-        part_out[half, :] = part
-        part_send[half, :] = part.astype(bf16)
-
-
-def text_terms(coef, e0, e1, terms):
-    terms[...] = dot(coef[:256], e0[...], 0, 0) + dot(coef[256:], e1[...], 0, 0)
-
-
-def weight_terms(part, arrived, h0, h1, terms, rows, own, s1, s2, s3, t1, t2, t3):
+    unit = normed[...]
+    radial = jnp.sum(unit * grad, axis=1, keepdims=True)
+    part = (grad - unit * radial) * inverse[...]
+    part_out[...] = part
+    part_send[...] = part.astype(bf16)
+
+
+def text_terms(coef, embed, terms):
+    terms[...] = dot(coef[...], embed[...], 0, 0)
+
+
+def weight_terms(part, arrived, turned, terms, rows, own, s1, s2, s3, t1, t2):
     half = 2 * ROWS
     top = part[:half] + arrived[half:].astype(f32)
     low = part[half:] + arrived[:half].astype(f32)
     rows[...] = top
-    grad = dot(h0[...], top.astype(bf16), 1, 0) + dot(h1[...], low.astype(bf16), 1, 0)
+    grad = dot(turned[...], jnp.concatenate([top, low], 0).astype(bf16), 1, 0)
     own[...] = grad[:144]
     for k, out in enumerate((s1, s2, s3)):
         out[...] = grad[(k + 1) * 144 : (k + 2) * 144].astype(bf16)
-    for k, out in enumerate((t1, t2, t3)):
+    for k, out in enumerate((t1, t2)):
         out[...] = terms[(k + 1) * ROWS : (k + 2) * ROWS].astype(bf16)
 
 
-def first_sum(own, a1, a2, a3, b1, b2, b3, out, s1, s2, s3, held):
+def first_sum(own, a1, a2, a3, b1, b2, out, s1, s2, s3, held):
     held[...] = own[...] + a2[...].astype(f32) + a1[...].astype(f32) + a3[...].astype(f32)
     out[...] = held[:36]
     for k, send in enumerate((s1, s2, s3)):
         send[...] = held[(k + 1) * 36 : (k + 2) * 36].astype(bf16)
 
 
-def second_sum(own, a1, a2, a3, rows, send, rows_send):
+def second_sum(own, a1, a2, a3, rows, terms, send, rows_send, t3):
     total = own[...] + a2[...].astype(f32) + a1[...].astype(f32) + a3[...].astype(f32)
     send[...] = total.astype(bf16)
     rows_send[...] = rows[ROWS:].astype(bf16)
+    t3[...] = terms[3 * ROWS :].astype(bf16)
 
 
 def third_sum(own, arrived, out, near, far, mine, held):
@@ -215,54 +215,61 @@
             0,
             block,
         )(chosen, hid, hid_x, txt_1, txt_3)
+        hid_c = xor(both, "c", 1)
         txt_2a = xor(first, "y", 1)
         txt_2b = xor(second, "y", 3)
-        hid_c = xor(both, "c", 1)
     with jax.named_scope("project"):
-        outs = [shape(bf16, 256, WIDTH), shape(f32, 256, WIDTH), shape(f32, 256, 1), shape(bf16, 576, 256)]
-        run = call(project, outs, [VMEM] * 3, 0, block)
-        e0, n0, i0, h0 = run(both, held, chosen)
-        e1, n1, i1, h1 = run(hid_c, held, chosen)
+        embed, normed, inverse, turned = call(
+            project,
+            [shape(bf16, 512, WIDTH), tall, shape(f32, 512, 1), shape(bf16, 576, 512)],
+            [VMEM] * 4,
+            0,
+            block,
+            vmem=16,
+        )(both, hid_c, held, chosen)
     with jax.named_scope("tile"):
         coef, part, part_send = call(
             tile,
             [shape(bf16, 512, 512), tall, shape(bf16, 512, WIDTH)],
-            [SMEM, SMEM] + [VMEM] * 13,
-            0,
-            block,
+            [SMEM, SMEM] + [VMEM] * 10,
+            0,
+            block,
+            vmem=16,
         )(
             logit_scale.reshape(1), logit_bias.reshape(1), left, right,
-            e0, e1, n0, n1, i0, i1, txt, txt_1, txt_2a, txt_2b, txt_3,
+            embed, normed, inverse, txt, txt_1, txt_2a, txt_2b, txt_3,
         )
     with jax.named_scope("core"):
         arrived = xor(part_send, "c", 1)
     with jax.named_scope("text"):
-        (terms,) = call(text_terms, [tall], [VMEM] * 3, 0, block)(coef, e0, e1)
+        (terms,) = call(text_terms, [tall], [VMEM] * 2, 0, block)(coef, embed)
     with jax.named_scope("weight"):
-        rows, own, s1, s2, s3, u1, u2, u3 = call(
+        rows, own, s1, s2, s3, u1, u2 = call(
             weight_terms,
             [shape(f32, 256, WIDTH), shape(f32, 144, WIDTH)]
             + [shape(bf16, 144, WIDTH)] * 3
-            + [wide] * 3,
-            [VMEM] * 5,
-            0,
-            block,
-        )(part, arrived, h0, h1, terms)
+            + [wide] * 2,
+            [VMEM] * 4,
+            0,
+            block,
+            vmem=16,
+        )(part, arrived, turned, terms)
         s2, s1, s3 = xor(s2, X, 2), xor(s1, X, 1), xor(s3, X, 3)
-        u1, u3, u2 = xor(u1, "y", 1), xor(u3, "y", 3), xor(u2, "y", 2)
+        u2, u1 = xor(u2, "y", 2), xor(u1, "y", 1)
         small, small_b = shape(f32, 36, WIDTH), shape(bf16, 36, WIDTH)
         whole, s1, s2, s3 = call(
             first_sum,
             [small] + [small_b] * 3,
-            [VMEM] * 4 + [ANY] * 3,
+            [VMEM] * 4 + [ANY] * 2,
             0,
             block,
             [pltpu.VMEM((144, WIDTH), f32)],
-        )(own, s1, s2, s3, u1, u2, u3)
+        )(own, s1, s2, s3, u1, u2)
         s2, s1, s3 = xor(s2, "y", 2), xor(s1, "y", 1), xor(s3, "y", 3)
-        whole_send, rows_send = call(second_sum, [small_b, wide], [VMEM] * 5, 0, block)(
-            whole, s1, s2, s3, rows
-        )
+        whole_send, rows_send, u3 = call(
+            second_sum, [small_b, wide, wide], [VMEM] * 6, 0, block
+        )(whole, s1, s2, s3, rows, terms)
+        u3 = xor(u3, "y", 3)
         arrived = xor(whole_send, "zl", 1)
         whole, near, far = call(
             third_sum,

time: 86.4 us -> 85.7 us (level)
  starting transfers between devices: 33.8 us -> 35.2 us
  Pallas kernels: 17.6 us -> 16.5 us
  waiting for transfers between devices: 28.8 us -> 27.7 us
    ppermute x3, starting transfers between devices: 10.5 us -> 11.7 us  [per_device(): lax.ppermute(x, Z, [(p, (p + (hop if p % 2 else -hop)) % 8) for p in rang...]
    pallas_call x5 -> x4, Pallas kernels: 6.29 us -> 5.22 us  [the longest x1 3.97 us: per_device(): call(project, [shape(bf16, 512, WIDTH), tall, shape(f32, 512, 1), shape(b...]
    ppermute x18, waiting for transfers between devices: 28.3 us -> 27.2 us  [xor(): return lax.ppermute(x, axis, [(i, i ^ step) for i in range(size)])]
  transfers between devices with their start and end apart: 21 -> 21, of which waited for: 12 -> 11; matrix products, arithmetic and copies ran while one was open for 0% -> 0% of each run, Pallas kernels for 12% -> 11%
where the time goes in v5:
time: 85.7 us; the launch traced here: 85.4 us
  starting transfers between devices  35.2 us (41%)
  waiting for transfers between devices  27.7 us (32%)
  Pallas kernels  16.5 us (19%)
  local copies, waits for them, and re-layouts  3.25 us (4%)
  between operations  2.7 us (3%)
    ppermute x18, waiting for transfers between devices, xor(): return lax.ppermute(x, axis, [(i, i ^ step) for i in range(size)])  27.2 us
    ppermute x18, starting transfers between devices, xor(): return lax.ppermute(x, axis, [(i, i ^ step) for i in range(size)])  23.5 us
    ppermute x3, starting transfers between devices, per_device(): lax.ppermute(x, Z, [(p, (p + (hop if p % 2 else -hop)) % 8) for p in rang...  11.7 us
    pallas_call x1, Pallas kernels, per_device(): call(project, [shape(bf16, 512, WIDTH), tall, shape(f32, 512, 1), shape(b...  3.97 us
    unnamed x10, local copies, waits for them, and re-layouts  3.25 us
    pallas_call x1, Pallas kernels, per_device(): call(tile, [shape(bf16, 512, 512), tall, shape(bf16, 512, WIDTH)], [SMEM,...  3.06 us
    pallas_call x1, Pallas kernels, per_device(): call(ahead, [shape(bf16, WIDTH, WIDTH), shape(bf16, 576, WIDTH), shape(jn...  1.78 us
  transfers between devices with their start and end apart: 21, of which 11 were waited for; matrix products, arithmetic and copies ran while one was open for 0% of the time, Pallas kernels for 11%

profile of v5, /device:TPU:2, one launch (start us, length us, event | category | flops | bytes accessed | tf_op | source)
XLA Modules:
  0.0 85.4 jit_solution(11232413288476286963)
XLA Ops:
  2.5 2.4 %collective-permute-start = (bf16[128,1152]{1,0:T(8,128)(2,1)S(1)}, bf16[128,1152]{1,0:T(8,128)(2,1)S(1)}, u32[]{:S(2)}, u32[]{:S(2)}) collective-permute-start(bf16[128,1152]{1,0:T(8,128)(2,1)S(1)} %get-tuple-element.38.after.own), channel_id=1, source_target_pairs={{0,16},{16,0},{1,17},{17,1},{2,18},{18,2},{3,19},{19,3},{4,20},{20... | collective-permute-start | bytes 884744 | tf_op jit(solution)/shard_map/gather/ppermute | solution.py:26
  7.1 1.8 %gather.2 = (bf16[1152,1152]{1,0:T(8,128)(2,1)S(1)}, bf16[576,1152]{1,0:T(8,128)(2,1)S(1)}, s32[512,1]{1,0:T(8,128)S(1)}, s32[1,512]{1,0:T(1,128)S(1)}) custom-call(bf16[128,1152]{1,0:T(8,128)(2,1)S(1)} %get-tuple-element.38.after.own, s32[1,16384]{1,0:T(1,128)S(1)} %copy-done.4, bf16[1152,1152]{1,0:T(8,128)(2,1)} %weight.6), custom_call_target="tpu_custom_call" | custom-call | flops 147456000 | bytes 147456 | tf_op jit(solution)/shard_map/gather/pallas_call | solution.py:198
  8.9 2.4 %collective-permute-done.paired = bf16[128,1152]{1,0:T(8,128)(2,1)S(1)} collective-permute-done((bf16[128,1152]{1,0:T(8,128)(2,1)S(1)}, bf16[128,1152]{1,0:T(8,128)(2,1)S(1)}, u32[]{:S(2)}, u32[]{:S(2)}) %collective-permute-start) | collective-permute-done | bytes 294944 | tf_op jit(solution)/shard_map/gather/ppermute | solution.py:26
  11.3 1.5 %collective-permute-done.2.t3 = bf16[128,1152]{1,0:T(8,128)(2,1)S(1)} collective-permute-done((bf16[128,1152]{1,0:T(8,128)(2,1)S(1)}, bf16[128,1152]{1,0:T(8,128)(2,1)S(1)}, u32[]{:S(2)}, u32[]{:S(2)}) %collective-permute-start.2) | collective-permute-done | bytes 294944 | tf_op jit(solution)/shard_map/gather/ppermute | solution.py:26
  12.8 1.5 %collective-permute-done.1.t1 = bf16[128,1152]{1,0:T(8,128)(2,1)S(1)} collective-permute-done((bf16[128,1152]{1,0:T(8,128)(2,1)S(1)}, bf16[128,1152]{1,0:T(8,128)(2,1)S(1)}, u32[]{:S(2)}, u32[]{:S(2)}) %collective-permute-start.1) | collective-permute-done | bytes 294944 | tf_op jit(solution)/shard_map/gather/ppermute | solution.py:26
  20.5 4.0 %project.1 = (bf16[512,1152]{1,0:T(8,128)(2,1)S(1)}, f32[512,1152]{1,0:T(8,128)S(1)}, f32[512,1]{1,0:T(8,128)S(1)}, bf16[576,512]{1,0:T(8,128)(2,1)S(1)}) custom-call(bf16[256,1152]{1,0:T(8,128)(2,1)} %get-tuple-element.43.both, bf16[256,1152]{1,0:T(8,128)(2,1)} %collective-permute-done.3.cores, bf16[1152,1152]{1,0:T(8,128)(2,1)S(1)} %get-tuple-element.44.weight, ...), custom_call_target="tpu_custom_call" | custom-call | bytes 147456 | tf_op jit(solution)/shard_map/project/pallas_call | solution.py:222
  24.5 3.1 %tile.1 = (bf16[512,512]{1,0:T(8,128)(2,1)S(1)}, f32[512,1152]{1,0:T(8,128)S(1)}, bf16[512,1152]{1,0:T(8,128)(2,1)S(1)}) custom-call(f32[1]{0:T(128)} %bitcast.2.scale, f32[1]{0:T(128)} %bitcast.3.bias, s32[512,1]{1,0:T(8,128)S(1)} %copy-done.3, s32[1,512]{1,0:T(1,128)S(1)} %get-tuple-element.40.right, bf16[512,1152]{1,0:T(8,128)(2,1)S(1)} %get-tuple-element.45.embed, ...), custom_call_target="tpu_custom_call" | custom-call | bytes 147456 | tf_op jit(solution)/shard_map/tile/pallas_call | solution.py:231
  28.8 1.7 %collective-permute-done.6.arrived = bf16[512,1152]{1,0:T(8,128)(2,1)S(1)} collective-permute-done((bf16[512,1152]{1,0:T(8,128)(2,1)S(1)}, bf16[512,1152]{1,0:T(8,128)(2,1)S(1)}, u32[]{:S(2)}, u32[]{:S(2)}) %collective-permute-start.6) | collective-permute-done | bytes 1179680 | tf_op jit(solution)/shard_map/core/ppermute | solution.py:26
  31.4 1.6 %collective-permute-start.7 = (bf16[144,1152]{1,0:T(8,128)(2,1)S(1)}, bf16[144,1152]{1,0:T(8,128)(2,1)S(1)}, u32[]{:S(2)}, u32[]{:S(2)}) collective-permute-start(bf16[144,1152]{1,0:T(8,128)(2,1)S(1)} %get-tuple-element.56), channel_id=1, source_target_pairs={{0,16},{16,0},{32,48},{48,32},{1,17},{17,1},{33,49},{49,33},{2,18}... | collective-permute-start | bytes 995336 | tf_op jit(solution)/shard_map/weight/ppermute | solution.py:26
  33.0 2.1 %collective-permute-start.8 = (bf16[144,1152]{1,0:T(8,128)(2,1)S(1)}, bf16[144,1152]{1,0:T(8,128)(2,1)S(1)}, u32[]{:S(2)}, u32[]{:S(2)}) collective-permute-start(bf16[144,1152]{1,0:T(8,128)(2,1)S(1)} %get-tuple-element.57), channel_id=1, source_target_pairs={{0,32},{16,48},{32,0},{48,16},{1,33},{17,49},{33,1},{49,17},{2,34}... | collective-permute-start | bytes 995336 | tf_op jit(solution)/shard_map/weight/ppermute | solution.py:26
  35.2 1.4 %collective-permute-start.10 = (bf16[128,1152]{1,0:T(8,128)(2,1)S(1)}, bf16[128,1152]{1,0:T(8,128)(2,1)S(1)}, u32[]{:S(2)}, u32[]{:S(2)}) collective-permute-start(bf16[128,1152]{1,0:T(8,128)(2,1)S(1)} %get-tuple-element.59), channel_id=1, source_target_pairs={{0,4},{4,0},{8,12},{12,8},{1,5},{5,1},{9,13},{13,9},{2,6},{6,2},{1... | collective-permute-start | bytes 884744 | tf_op jit(solution)/shard_map/weight/ppermute | solution.py:26
  36.6 2.1 %collective-permute-start.11 = (bf16[128,1152]{1,0:T(8,128)(2,1)S(1)}, bf16[128,1152]{1,0:T(8,128)(2,1)S(1)}, u32[]{:S(2)}, u32[]{:S(2)}) collective-permute-start(bf16[128,1152]{1,0:T(8,128)(2,1)S(1)} %get-tuple-element.60), channel_id=1, source_target_pairs={{0,8},{4,12},{8,0},{12,4},{1,9},{5,13},{9,1},{13,5},{2,10},{6,14},... | collective-permute-start | bytes 884744 | tf_op jit(solution)/shard_map/weight/ppermute | solution.py:26
  38.6 6.4 %collective-permute-done.10.b1 = bf16[128,1152]{1,0:T(8,128)(2,1)S(1)} collective-permute-done((bf16[128,1152]{1,0:T(8,128)(2,1)S(1)}, bf16[128,1152]{1,0:T(8,128)(2,1)S(1)}, u32[]{:S(2)}, u32[]{:S(2)}) %collective-permute-start.10) | collective-permute-done | bytes 294944 | tf_op jit(solution)/shard_map/weight/ppermute | solution.py:26
  45.1 6.3 %collective-permute-done.11.b2 = bf16[128,1152]{1,0:T(8,128)(2,1)S(1)} collective-permute-done((bf16[128,1152]{1,0:T(8,128)(2,1)S(1)}, bf16[128,1152]{1,0:T(8,128)(2,1)S(1)}, u32[]{:S(2)}, u32[]{:S(2)}) %collective-permute-start.11) | collective-permute-done | bytes 294944 | tf_op jit(solution)/shard_map/weight/ppermute | solution.py:26
  51.9 1.4 %collective-permute-start.12 = (bf16[36,1152]{1,0:T(8,128)(2,1)S(1)}, bf16[36,1152]{1,0:T(8,128)(2,1)S(1)}, u32[]{:S(2)}, u32[]{:S(2)}) collective-permute-start(bf16[36,1152]{1,0:T(8,128)(2,1)S(1)} %get-tuple-element.62), channel_id=1, source_target_pairs={{0,4},{4,0},{8,12},{12,8},{1,5},{5,1},{9,13},{13,9},{2,6},{6,2},{1... | collective-permute-start | bytes 248840 | tf_op jit(solution)/shard_map/weight/ppermute | solution.py:26
  53.3 2.1 %collective-permute-start.13 = (bf16[36,1152]{1,0:T(8,128)(2,1)S(1)}, bf16[36,1152]{1,0:T(8,128)(2,1)S(1)}, u32[]{:S(2)}, u32[]{:S(2)}) collective-permute-start(bf16[36,1152]{1,0:T(8,128)(2,1)S(1)} %get-tuple-element.63), channel_id=1, source_target_pairs={{0,8},{4,12},{8,0},{12,4},{1,9},{5,13},{9,1},{13,5},{2,10},{6,14},... | collective-permute-start | bytes 248840 | tf_op jit(solution)/shard_map/weight/ppermute | solution.py:26
  56.7 2.7 %collective-permute-done.13.a2 = bf16[36,1152]{1,0:T(8,128)(2,1)S(1)} collective-permute-done((bf16[36,1152]{1,0:T(8,128)(2,1)S(1)}, bf16[36,1152]{1,0:T(8,128)(2,1)S(1)}, u32[]{:S(2)}, u32[]{:S(2)}) %collective-permute-start.13) | collective-permute-done | bytes 82976 | tf_op jit(solution)/shard_map/weight/ppermute | solution.py:26
  59.4 1.8 %collective-permute-done.14.a3 = bf16[36,1152]{1,0:T(8,128)(2,1)S(1)} collective-permute-done((bf16[36,1152]{1,0:T(8,128)(2,1)S(1)}, bf16[36,1152]{1,0:T(8,128)(2,1)S(1)}, u32[]{:S(2)}, u32[]{:S(2)}) %collective-permute-start.14) | collective-permute-done | bytes 82976 | tf_op jit(solution)/shard_map/weight/ppermute | solution.py:26
  62.6 2.7 %collective-permute-start.15 = (bf16[128,1152]{1,0:T(8,128)(2,1)S(1)}, bf16[128,1152]{1,0:T(8,128)(2,1)S(1)}, u32[]{:S(2)}, u32[]{:S(2)}) collective-permute-start(bf16[128,1152]{1,0:T(8,128)(2,1)S(1)} %get-tuple-element.65), channel_id=1, source_target_pairs={{0,16},{16,0},{1,17},{17,1},{2,18},{18,2},{3,19},{19,3},{4,20},{20... | collective-permute-start | bytes 884744 | tf_op jit(solution)/shard_map/hidden/ppermute | solution.py:26
  65.3 1.9 %collective-permute-start.16 = (bf16[36,1152]{1,0:T(8,128)(2,1)S(1)}, bf16[36,1152]{1,0:T(8,128)(2,1)S(1)}, u32[]{:S(2)}, u32[]{:S(2)}) collective-permute-start(bf16[36,1152]{1,0:T(8,128)(2,1)S(1)} %get-tuple-element.68.own.after), channel_id=1, source_target_pairs={{0,1},{1,0},{2,3},{3,2},{4,5},{5,4},{6,7},{7,6},{8,9},{9,8},{10,11... | collective-permute-start | bytes 248840 | tf_op jit(solution)/shard_map/weight/ppermute | solution.py:26
  67.2 2.6 %collective-permute-done.16.arrived = bf16[36,1152]{1,0:T(8,128)(2,1)S(1)} collective-permute-done((bf16[36,1152]{1,0:T(8,128)(2,1)S(1)}, bf16[36,1152]{1,0:T(8,128)(2,1)S(1)}, u32[]{:S(2)}, u32[]{:S(2)}) %collective-permute-start.16) | collective-permute-done | bytes 82976 | tf_op jit(solution)/shard_map/weight/ppermute | solution.py:26
  69.9 6.8 %collective-permute-start.19 = (f32[9,1152]{1,0:T(8,128)S(1)}, f32[9,1152]{1,0:T(8,128)S(1)}, u32[]{:S(2)}, u32[]{:S(2)}) collective-permute-start(f32[9,1152]{1,0:T(8,128)S(1)} %get-tuple-element.71), channel_id=1, source_target_pairs={{0,129},{1,128},{64,193},{65,192},{128,1},{129,0},{192,65},{193,64... | collective-permute-start | bytes 124424 | tf_op jit(solution)/shard_map/weight/ppermute | solution.py:285
  77.3 4.3 %collective-permute-start.17 = (f32[9,1152]{1,0:T(8,128)S(1)}, f32[9,1152]{1,0:T(8,128)S(1)}, u32[]{:S(2)}, u32[]{:S(2)}) collective-permute-start(f32[9,1152]{1,0:T(8,128)S(1)} %get-tuple-element.70), channel_id=1, source_target_pairs={{0,193},{1,64},{64,1},{65,128},{128,65},{129,192},{192,129},{193,0... | collective-permute-start | bytes 124424 | tf_op jit(solution)/shard_map/weight/ppermute | solution.py:285
  82.6 1.6 %hidden.3 = (bf16[128,1152]{1,0:T(8,128)(2,1)}, f32[8,128]{1,0:T(8,128)S(1)}) custom-call(s32[1]{0:T(128)S(6)} %copy.10.count, f32[256,1152]{1,0:T(8,128)S(1)} %get-tuple-element.54.rows, bf16[128,1152]{1,0:T(8,128)(2,1)S(1)} %collective-permute-done.15.arrived, bf16[1152,1152]{1,0:T(8,128)(2,1)S(1)} %get-tuple-element.44.weight), custom_call_target="tpu_custom_call" | custom-call | flops 339738624 | bytes 2654208 | tf_op jit(solution)/shard_map/hidden/pallas_call | solution.py:290
  (41 shorter events, 16.5 us)
Async XLA Ops:
  2.5 8.8 %collective-permute-start = (bf16[128,1152]{1,0:T(8,128)(2,1)S(1)}, bf16[128,1152]{1,0:T(8,128)(2,1)S(1)}, u32[]{:S(2)}, u32[]{:S(2)}) collective-permute-start(bf16[128,1152]{1,0:T(8,128)(2,1)S(1)} %get-tuple-element.38.after.own), channel_id=1, source_target_pairs={{0,16},{16,0},{1,17},{17,1},{2,18},{18,2},{3,19},{19,3},{4,20},{20... | collective-permute-start | bytes 884744 | tf_op jit(solution)/shard_map/gather/ppermute | solution.py:26
  4.8 8.0 %collective-permute-start.2 = (bf16[128,1152]{1,0:T(8,128)(2,1)S(1)}, bf16[128,1152]{1,0:T(8,128)(2,1)S(1)}, u32[]{:S(2)}, u32[]{:S(2)}) collective-permute-start(bf16[128,1152]{1,0:T(8,128)(2,1)S(1)} %get-tuple-element.42.t0), channel_id=1, source_target_pairs={{0,12},{4,8},{8,4},{12,0},{1,13},{5,9},{9,5},{13,1},{2,14},{6,10},... | collective-permute-start | bytes 884744 | tf_op jit(solution)/shard_map/gather/ppermute | solution.py:26
  6.1 8.2 %collective-permute-start.1 = (bf16[128,1152]{1,0:T(8,128)(2,1)S(1)}, bf16[128,1152]{1,0:T(8,128)(2,1)S(1)}, u32[]{:S(2)}, u32[]{:S(2)}) collective-permute-start(bf16[128,1152]{1,0:T(8,128)(2,1)S(1)} %get-tuple-element.42.t0), channel_id=1, source_target_pairs={{0,4},{4,0},{8,12},{12,8},{1,5},{5,1},{9,13},{13,9},{2,6},{6,2},{1... | collective-permute-start | bytes 884744 | tf_op jit(solution)/shard_map/gather/ppermute | solution.py:26
  8.9 6.4 %copy-start.2 = (s32[512,1]{1,0:T(8,128)}, s32[512,1]{1,0:T(8,128)S(1)}, u32[]{:S(2)}) copy-start(s32[512,1]{1,0:T(8,128)S(1)} %get-tuple-element.39.left) | copy-start | bytes 6148
  16.4 2.8 %collective-permute-start.3 = (bf16[256,1152]{1,0:T(8,128)(2,1)}, bf16[256,1152]{1,0:T(8,128)(2,1)}, u32[]{:S(2)}, u32[]{:S(2)}) collective-permute-start(bf16[256,1152]{1,0:T(8,128)(2,1)} %get-tuple-element.43.both), channel_id=1, source_target_pairs={{0,2},{2,0},{1,3},{3,1},{4,6},{6,4},{5,7},{7,5},{8,10},{10,8},{9,1... | collective-permute-start | bytes 1769480 | tf_op jit(solution)/shard_map/gather/ppermute | solution.py:26
  16.4 8.1 %collective-permute-start.4 = (bf16[64,1152]{1,0:T(8,128)(2,1)}, bf16[64,1152]{1,0:T(8,128)(2,1)}, u32[]{:S(2)}, u32[]{:S(2)}) collective-permute-start(bf16[64,1152]{1,0:T(8,128)(2,1)} %get-tuple-element.48), channel_id=1, source_target_pairs={{0,4},{4,0},{8,12},{12,8},{1,5},{5,1},{9,13},{13,9},{2,6},{6,2},{1... | collective-permute-start | bytes 442376 | tf_op jit(solution)/shard_map/gather/ppermute | solution.py:26
  16.6 7.8 %collective-permute-start.5 = (bf16[64,1152]{1,0:T(8,128)(2,1)}, bf16[64,1152]{1,0:T(8,128)(2,1)}, u32[]{:S(2)}, u32[]{:S(2)}) collective-permute-start(bf16[64,1152]{1,0:T(8,128)(2,1)} %get-tuple-element.49), channel_id=1, source_target_pairs={{0,12},{4,8},{8,4},{12,0},{1,13},{5,9},{9,5},{13,1},{2,14},{6,10},... | collective-permute-start | bytes 442376 | tf_op jit(solution)/shard_map/gather/ppermute | solution.py:26
  19.2 1.3 %copy-start.1 = (bf16[576,1152]{1,0:T(8,128)(2,1)S(1)}, bf16[576,1152]{1,0:T(8,128)(2,1)}, u32[]{:S(2)}) copy-start(bf16[576,1152]{1,0:T(8,128)(2,1)} %copy-done) | copy-start | bytes 3981316
  20.5 4.0 %copy-start.3 = (s32[512,1]{1,0:T(8,128)S(1)}, s32[512,1]{1,0:T(8,128)}, u32[]{:S(2)}) copy-start(s32[512,1]{1,0:T(8,128)} %copy-done.2) | copy-start | bytes 6148
  27.6 2.9 %collective-permute-start.6 = (bf16[512,1152]{1,0:T(8,128)(2,1)S(1)}, bf16[512,1152]{1,0:T(8,128)(2,1)S(1)}, u32[]{:S(2)}, u32[]{:S(2)}) collective-permute-start(bf16[512,1152]{1,0:T(8,128)(2,1)S(1)} %get-tuple-element.51), channel_id=1, source_target_pairs={{0,2},{2,0},{1,3},{3,1},{4,6},{6,4},{5,7},{7,5},{8,10},{10,8},{9,1... | collective-permute-start | bytes 3538952 | tf_op jit(solution)/shard_map/core/ppermute | solution.py:26
  31.4 20.0 %collective-permute-start.7 = (bf16[144,1152]{1,0:T(8,128)(2,1)S(1)}, bf16[144,1152]{1,0:T(8,128)(2,1)S(1)}, u32[]{:S(2)}, u32[]{:S(2)}) collective-permute-start(bf16[144,1152]{1,0:T(8,128)(2,1)S(1)} %get-tuple-element.56), channel_id=1, source_target_pairs={{0,16},{16,0},{32,48},{48,32},{1,17},{17,1},{33,49},{49,33},{2,18}... | collective-permute-start | bytes 995336 | tf_op jit(solution)/shard_map/weight/ppermute | solution.py:26
  33.0 18.4 %collective-permute-start.8 = (bf16[144,1152]{1,0:T(8,128)(2,1)S(1)}, bf16[144,1152]{1,0:T(8,128)(2,1)S(1)}, u32[]{:S(2)}, u32[]{:S(2)}) collective-permute-start(bf16[144,1152]{1,0:T(8,128)(2,1)S(1)} %get-tuple-element.57), channel_id=1, source_target_pairs={{0,32},{16,48},{32,0},{48,16},{1,33},{17,49},{33,1},{49,17},{2,34}... | collective-permute-start | bytes 995336 | tf_op jit(solution)/shard_map/weight/ppermute | solution.py:26
  35.2 16.5 %collective-permute-start.9 = (bf16[144,1152]{1,0:T(8,128)(2,1)S(1)}, bf16[144,1152]{1,0:T(8,128)(2,1)S(1)}, u32[]{:S(2)}, u32[]{:S(2)}) collective-permute-start(bf16[144,1152]{1,0:T(8,128)(2,1)S(1)} %get-tuple-element.58), channel_id=1, source_target_pairs={{0,48},{16,32},{32,16},{48,0},{1,49},{17,33},{33,17},{49,1},{2,50}... | collective-permute-start | bytes 995336 | tf_op jit(solution)/shard_map/weight/ppermute | solution.py:26
  35.2 9.9 %collective-permute-start.10 = (bf16[128,1152]{1,0:T(8,128)(2,1)S(1)}, bf16[128,1152]{1,0:T(8,128)(2,1)S(1)}, u32[]{:S(2)}, u32[]{:S(2)}) collective-permute-start(bf16[128,1152]{1,0:T(8,128)(2,1)S(1)} %get-tuple-element.59), channel_id=1, source_target_pairs={{0,4},{4,0},{8,12},{12,8},{1,5},{5,1},{9,13},{13,9},{2,6},{6,2},{1... | collective-permute-start | bytes 884744 | tf_op jit(solution)/shard_map/weight/ppermute | solution.py:26
  36.6 14.9 %collective-permute-start.11 = (bf16[128,1152]{1,0:T(8,128)(2,1)S(1)}, bf16[128,1152]{1,0:T(8,128)(2,1)S(1)}, u32[]{:S(2)}, u32[]{:S(2)}) collective-permute-start(bf16[128,1152]{1,0:T(8,128)(2,1)S(1)} %get-tuple-element.60), channel_id=1, source_target_pairs={{0,8},{4,12},{8,0},{12,4},{1,9},{5,13},{9,1},{13,5},{2,10},{6,14},... | collective-permute-start | bytes 884744 | tf_op jit(solution)/shard_map/weight/ppermute | solution.py:26
  51.9 4.8 %collective-permute-start.12 = (bf16[36,1152]{1,0:T(8,128)(2,1)S(1)}, bf16[36,1152]{1,0:T(8,128)(2,1)S(1)}, u32[]{:S(2)}, u32[]{:S(2)}) collective-permute-start(bf16[36,1152]{1,0:T(8,128)(2,1)S(1)} %get-tuple-element.62), channel_id=1, source_target_pairs={{0,4},{4,0},{8,12},{12,8},{1,5},{5,1},{9,13},{13,9},{2,6},{6,2},{1... | collective-permute-start | bytes 248840 | tf_op jit(solution)/shard_map/weight/ppermute | solution.py:26
  53.3 6.1 %collective-permute-start.13 = (bf16[36,1152]{1,0:T(8,128)(2,1)S(1)}, bf16[36,1152]{1,0:T(8,128)(2,1)S(1)}, u32[]{:S(2)}, u32[]{:S(2)}) collective-permute-start(bf16[36,1152]{1,0:T(8,128)(2,1)S(1)} %get-tuple-element.63), channel_id=1, source_target_pairs={{0,8},{4,12},{8,0},{12,4},{1,9},{5,13},{9,1},{13,5},{2,10},{6,14},... | collective-permute-start | bytes 248840 | tf_op jit(solution)/shard_map/weight/ppermute | solution.py:26
  55.4 5.8 %collective-permute-start.14 = (bf16[36,1152]{1,0:T(8,128)(2,1)S(1)}, bf16[36,1152]{1,0:T(8,128)(2,1)S(1)}, u32[]{:S(2)}, u32[]{:S(2)}) collective-permute-start(bf16[36,1152]{1,0:T(8,128)(2,1)S(1)} %get-tuple-element.64), channel_id=1, source_target_pairs={{0,12},{4,8},{8,4},{12,0},{1,13},{5,9},{9,5},{13,1},{2,14},{6,10},... | collective-permute-start | bytes 248840 | tf_op jit(solution)/shard_map/weight/ppermute | solution.py:26
  61.3 20.3 %collective-permute-start.20 = (bf16[128,1152]{1,0:T(8,128)(2,1)S(1)}, bf16[128,1152]{1,0:T(8,128)(2,1)S(1)}, u32[]{:S(2)}, u32[]{:S(2)}) collective-permute-start(bf16[128,1152]{1,0:T(8,128)(2,1)S(1)} %get-tuple-element.72), channel_id=1, source_target_pairs={{0,12},{4,8},{8,4},{12,0},{1,13},{5,9},{9,5},{13,1},{2,14},{6,10},... | collective-permute-start | bytes 884744 | tf_op jit(solution)/shard_map/weight/ppermute | solution.py:26
  62.6 19.9 %collective-permute-start.15 = (bf16[128,1152]{1,0:T(8,128)(2,1)S(1)}, bf16[128,1152]{1,0:T(8,128)(2,1)S(1)}, u32[]{:S(2)}, u32[]{:S(2)}) collective-permute-start(bf16[128,1152]{1,0:T(8,128)(2,1)S(1)} %get-tuple-element.65), channel_id=1, source_target_pairs={{0,16},{16,0},{1,17},{17,1},{2,18},{18,2},{3,19},{19,3},{4,20},{20... | collective-permute-start | bytes 884744 | tf_op jit(solution)/shard_map/hidden/ppermute | solution.py:26
  65.3 4.6 %collective-permute-start.16 = (bf16[36,1152]{1,0:T(8,128)(2,1)S(1)}, bf16[36,1152]{1,0:T(8,128)(2,1)S(1)}, u32[]{:S(2)}, u32[]{:S(2)}) collective-permute-start(bf16[36,1152]{1,0:T(8,128)(2,1)S(1)} %get-tuple-element.68.own.after), channel_id=1, source_target_pairs={{0,1},{1,0},{2,3},{3,2},{4,5},{5,4},{6,7},{7,6},{8,9},{9,8},{10,11... | collective-permute-start | bytes 248840 | tf_op jit(solution)/shard_map/weight/ppermute | solution.py:26
  69.9 14.3 %collective-permute-start.19 = (f32[9,1152]{1,0:T(8,128)S(1)}, f32[9,1152]{1,0:T(8,128)S(1)}, u32[]{:S(2)}, u32[]{:S(2)}) collective-permute-start(f32[9,1152]{1,0:T(8,128)S(1)} %get-tuple-element.71), channel_id=1, source_target_pairs={{0,129},{1,128},{64,193},{65,192},{128,1},{129,0},{192,65},{193,64... | collective-permute-start | bytes 124424 | tf_op jit(solution)/shard_map/weight/ppermute | solution.py:285
  76.7 7.5 %collective-permute-start.18 = (f32[9,1152]{1,0:T(8,128)S(1)}, f32[9,1152]{1,0:T(8,128)S(1)}, u32[]{:S(2)}, u32[]{:S(2)}) collective-permute-start(f32[9,1152]{1,0:T(8,128)S(1)} %get-tuple-element.70), channel_id=1, source_target_pairs={{0,192},{1,65},{64,0},{65,129},{128,64},{129,193},{192,128},{193,1... | collective-permute-start | bytes 124424 | tf_op jit(solution)/shard_map/weight/ppermute | solution.py:285
  77.3 7.4 %collective-permute-start.17 = (f32[9,1152]{1,0:T(8,128)S(1)}, f32[9,1152]{1,0:T(8,128)S(1)}, u32[]{:S(2)}, u32[]{:S(2)}) collective-permute-start(f32[9,1152]{1,0:T(8,128)S(1)} %get-tuple-element.70), channel_id=1, source_target_pairs={{0,193},{1,64},{64,1},{65,128},{128,65},{129,192},{192,129},{193,0... | collective-permute-start | bytes 124424 | tf_op jit(solution)/shard_map/weight/ppermute | solution.py:285
  (2 other events, 1.9 us)

commit v6 on v5

--- a/solution.py
+++ b/solution.py
@@ -69,9 +69,11 @@
     second[...] = t1[ROWS // 2 :]
 
 
-def ahead(after, pair_ids, weight, held, chosen, left, right, sem):
+def ahead(after, scale, bias, pair_ids, weight, held, chosen, left, right, settings, sem):
     copy = pltpu.make_async_copy(weight, held, sem)
     copy.start()
+    settings[0:1, :] = jnp.full((1, ROWS), scale[0], f32)
+    settings[1:2, :] = jnp.full((1, ROWS), bias[0], f32)
     zh, x1, x0, y, c, zl = (lax.axis_index(a) for a in AXES)
     row = lax.broadcasted_iota(jnp.int32, (576, 1), 0)
     k, row = row // 144, row % 144
@@ -79,7 +81,8 @@
     m, r = row // 9, row % 9
     turn = jnp.where(zl == 0, 4 - m, m)
     owner = (zh + turn) % 4
-    place = owner * 288 + (k ^ (x1 * 2 + x0)) * 72 + (j ^ y) * 18 + c * 9 + r
+    core = (c + owner + zh) % 2
+    place = owner * 288 + (k ^ (x1 * 2 + x0)) * 72 + (j ^ y) * 18 + core * 9 + r
     spots = lax.broadcasted_iota(jnp.int32, (576, WIDTH), 1)
     chosen[...] = (spots == place).astype(f32).astype(bf16)
     base = (zh * 2 + x1) * 16
@@ -107,11 +110,12 @@
     inverse[...] = inv
 
 
-def tile(scale, bias, left, right, embed, normed, inverse, t0, t1, t2a, t2b, t3, coef_out, part_out, part_send):
+def tile(settings, left, right, embed, normed, inverse, t0, t1, t2a, t2b, t3, coef_out, part_out, part_send):
     txt = jnp.concatenate([t0[...], t1[...], t2a[...], t2b[...], t3[...]], 0)
-    scores = scale[0] * dot(embed[...], txt, 1, 1) + bias[0]
+    scale, bias = settings[0:1, 0:1], settings[1:2, 0:1]
+    scores = scale * dot(embed[...], txt, 1, 1) + bias
     target = jnp.where(left[...] == right[...], 1.0, -1.0).astype(f32)
-    coef = (-target * jax.nn.sigmoid(-target * scores) * scale[0]).astype(bf16)
+    coef = (-target * jax.nn.sigmoid(-target * scores) * scale).astype(bf16)
     coef_out[...] = coef
     grad = dot(coef, txt, 1, 0)
     unit = normed[...]
@@ -121,11 +125,13 @@
     part_send[...] = part.astype(bf16)
 
 
-def text_terms(coef, embed, terms):
-    terms[...] = dot(coef[...], embed[...], 0, 0)
-
-
-def weight_terms(part, arrived, turned, terms, rows, own, s1, s2, s3, t1, t2):
+def text_terms(coef, embed, terms, t2):
+    grad = dot(coef[...], embed[...], 0, 0)
+    terms[...] = grad
+    t2[...] = grad[2 * ROWS : 3 * ROWS].astype(bf16)
+
+
+def weight_terms(part, arrived, turned, terms, rows, own, s1, s2, s3, t1, t3):
     half = 2 * ROWS
     top = part[:half] + arrived[half:].astype(f32)
     low = part[half:] + arrived[:half].astype(f32)
@@ -134,22 +140,21 @@
     own[...] = grad[:144]
     for k, out in enumerate((s1, s2, s3)):
         out[...] = grad[(k + 1) * 144 : (k + 2) * 144].astype(bf16)
-    for k, out in enumerate((t1, t2)):
-        out[...] = terms[(k + 1) * ROWS : (k + 2) * ROWS].astype(bf16)
-
-
-def first_sum(own, a1, a2, a3, b1, b2, out, s1, s2, s3, held):
+    t1[...] = terms[ROWS : 2 * ROWS].astype(bf16)
+    t3[...] = terms[3 * ROWS :].astype(bf16)
+
+
+def first_sum(own, a1, a2, a3, b1, b2, b3, out, s1, s2, s3, held):
     held[...] = own[...] + a2[...].astype(f32) + a1[...].astype(f32) + a3[...].astype(f32)
     out[...] = held[:36]
     for k, send in enumerate((s1, s2, s3)):
         send[...] = held[(k + 1) * 36 : (k + 2) * 36].astype(bf16)
 
 
-def second_sum(own, a1, a2, a3, rows, terms, send, rows_send, t3):
+def second_sum(own, a1, a2, a3, rows, send, rows_send):
     total = own[...] + a2[...].astype(f32) + a1[...].astype(f32) + a3[...].astype(f32)
     send[...] = total.astype(bf16)
     rows_send[...] = rows[ROWS:].astype(bf16)
-    t3[...] = terms[3 * ROWS :].astype(bf16)
 
 
 def third_sum(own, arrived, out, near, far, mine, held):
@@ -176,6 +181,15 @@
     keep = lax.broadcasted_iota(jnp.int32, (ROWS, 1), 0) < count[0]
     out[...] = jnp.where(keep, grad, 0.0).astype(bf16)
     done[...] = jnp.zeros((8, ROWS), f32)
+
+
+def along_z(x, hop, cross):
+    pairs = []
+    for z in range(8):
+        to = (z + (hop if z % 2 else -hop)) % 8
+        for c in range(2):
+            pairs.append((z // 2 * 4 + c * 2 + z % 2, to // 2 * 4 + (c ^ cross) * 2 + to % 2))
+    return lax.ppermute(x, ("zh", "c", "zl"), pairs)
 
 
 def per_device(hidden, weight, text, pair_ids, valid_count, logit_scale, logit_bias):
@@ -195,19 +209,20 @@
         hid_x = xor(hid, "x0", 1)
         txt_1 = xor(txt, "y", 1)
         txt_3 = xor(txt, "y", 3)
-        held, chosen, left, right = call(
+        held, chosen, left, right, settings = call(
             ahead,
             [
                 shape(bf16, WIDTH, WIDTH),
                 shape(bf16, 576, WIDTH),
                 shape(jnp.int32, 512, 1),
                 shape(jnp.int32, 1, 512),
+                shape(f32, 2, ROWS),
             ],
-            [ANY, VMEM, HBM],
+            [ANY, SMEM, SMEM, VMEM, HBM],
             block * 1000,
             block,
             [pltpu.SemaphoreType.DMA],
-        )(hid, pair_ids, in_hbm(weight))
+        )(hid, logit_scale.reshape(1), logit_bias.reshape(1), pair_ids, in_hbm(weight))
         both, first, second = call(
             join,
             [shape(bf16, 256, WIDTH)] + [shape(bf16, 64, WIDTH)] * 2,
@@ -231,20 +246,20 @@
         coef, part, part_send = call(
             tile,
             [shape(bf16, 512, 512), tall, shape(bf16, 512, WIDTH)],
-            [SMEM, SMEM] + [VMEM] * 10,
+            [VMEM] * 11,
             0,
             block,
             vmem=16,
         )(
-            logit_scale.reshape(1), logit_bias.reshape(1), left, right,
-            embed, normed, inverse, txt, txt_1, txt_2a, txt_2b, txt_3,
+            settings, left, right, embed, normed, inverse, txt, txt_1, txt_2a, txt_2b, txt_3,
         )
     with jax.named_scope("core"):
         arrived = xor(part_send, "c", 1)
     with jax.named_scope("text"):
-        (terms,) = call(text_terms, [tall], [VMEM] * 2, 0, block)(coef, embed)
+        terms, u2 = call(text_terms, [tall, wide], [VMEM] * 2, 0, block)(coef, embed)
+        u2 = xor(u2, "y", 2)
     with jax.named_scope("weight"):
-        rows, own, s1, s2, s3, u1, u2 = call(
+        rows, own, s1, s2, s3, u1, u3 = call(
             weight_terms,
             [shape(f32, 256, WIDTH), shape(f32, 144, WIDTH)]
             + [shape(bf16, 144, WIDTH)] * 3
@@ -255,21 +270,20 @@
             vmem=16,
         )(part, arrived, turned, terms)
         s2, s1, s3 = xor(s2, X, 2), xor(s1, X, 1), xor(s3, X, 3)
-        u2, u1 = xor(u2, "y", 2), xor(u1, "y", 1)
+        u1, u3 = xor(u1, "y", 1), xor(u3, "y", 3)
         small, small_b = shape(f32, 36, WIDTH), shape(bf16, 36, WIDTH)
         whole, s1, s2, s3 = call(
             first_sum,
             [small] + [small_b] * 3,
-            [VMEM] * 4 + [ANY] * 2,
+            [VMEM] * 4 + [ANY] * 3,
             0,
             block,
             [pltpu.VMEM((144, WIDTH), f32)],
-        )(own, s1, s2, s3, u1, u2)
+        )(own, s1, s2, s3, u1, u2, u3)
         s2, s1, s3 = xor(s2, "y", 2), xor(s1, "y", 1), xor(s3, "y", 3)
-        whole_send, rows_send, u3 = call(
-            second_sum, [small_b, wide, wide], [VMEM] * 6, 0, block
-        )(whole, s1, s2, s3, rows, terms)
-        u3 = xor(u3, "y", 3)
+        whole_send, rows_send = call(second_sum, [small_b, wide], [VMEM] * 5, 0, block)(
+            whole, s1, s2, s3, rows
+        )
         arrived = xor(whole_send, "zl", 1)
         whole, near, far = call(
             third_sum,
@@ -279,12 +293,7 @@
             block,
             [pltpu.VMEM((36, WIDTH), f32)] * 2,
         )(whole_send, arrived)
-        Z = ("zh", "zl")
-        steps = (near, 1), (near, 2), (far, 3)
-        got = [
-            lax.ppermute(x, Z, [(p, (p + (hop if p % 2 else -hop)) % 8) for p in range(8)])
-            for x, hop in steps
-        ]
+        got = [along_z(near, 1, 1), along_z(near, 2, 1), along_z(far, 3, 0)]
     with jax.named_scope("hidden"):
         rows_x = xor(rows_send, "x0", 1)
         hidden_grad, done = call(

time: 85.7 us -> 79.9 us (0.932)
  the two profiles are of different devices: /device:TPU:2 before, /device:TPU:1 now
where the time goes in v6:
time: 79.9 us; the launch traced here: 79.7 us
  starting transfers between devices  32.8 us (41%)
  waiting for transfers between devices  30.1 us (38%)
  Pallas kernels  13.4 us (17%)
  between operations  2.68 us (3%)
  local copies, waits for them, and re-layouts  0.83 us (1%)
    ppermute x18, waiting for transfers between devices, xor(): return lax.ppermute(x, axis, [(i, i ^ step) for i in range(size)])  26.4 us
    ppermute x18, starting transfers between devices, xor(): return lax.ppermute(x, axis, [(i, i ^ step) for i in range(size)])  22.4 us
    ppermute x3, starting transfers between devices, along_z(): return lax.ppermute(x, ('zh', 'c', 'zl'), pairs)  10.3 us
    ppermute x3, waiting for transfers between devices, along_z(): return lax.ppermute(x, ('zh', 'c', 'zl'), pairs)  3.7 us
    pallas_call x1, Pallas kernels, per_device(): call(project, [shape(bf16, 512, WIDTH), tall, shape(f32, 512, 1), shape(b...  2.7 us
    pallas_call x1, Pallas kernels, per_device(): call(tile, [shape(bf16, 512, 512), tall, shape(bf16, 512, WIDTH)], [VMEM]...  2.09 us
    pallas_call x1, Pallas kernels, per_device(): call(ahead, [shape(bf16, WIDTH, WIDTH), shape(bf16, 576, WIDTH), shape(jn...  1.78 us
    pallas_call x1, Pallas kernels, per_device(): call(back, [wide, shape(f32, 8, ROWS)], [SMEM] + [VMEM] * 3, 2 * block *...  1.64 us
  transfers between devices with their start and end apart: 21, of which 15 were waited for; matrix products, arithmetic and copies ran while one was open for 0% of the time, Pallas kernels for 11%

profile of v6, /device:TPU:1, one launch (start us, length us, event | category | flops | bytes accessed | tf_op | source)
XLA Modules:
  0.0 79.7 jit_solution(13619910216883001053)
XLA Ops:
  2.5 2.1 %collective-permute-start = (bf16[128,1152]{1,0:T(8,128)(2,1)S(1)}, bf16[128,1152]{1,0:T(8,128)(2,1)S(1)}, u32[]{:S(2)}, u32[]{:S(2)}) collective-permute-start(bf16[128,1152]{1,0:T(8,128)(2,1)S(1)} %get-tuple-element.40.after.own), channel_id=1, source_target_pairs={{0,16},{16,0},{1,17},{17,1},{2,18},{18,2},{3,19},{19,3},{4,20},{20... | collective-permute-start | bytes 884744 | tf_op jit(solution)/shard_map/gather/ppermute | solution.py:26
  4.6 2.7 %collective-permute-start.2 = (bf16[128,1152]{1,0:T(8,128)(2,1)S(1)}, bf16[128,1152]{1,0:T(8,128)(2,1)S(1)}, u32[]{:S(2)}, u32[]{:S(2)}) collective-permute-start(bf16[128,1152]{1,0:T(8,128)(2,1)S(1)} %get-tuple-element.45.t0), channel_id=1, source_target_pairs={{0,12},{4,8},{8,4},{12,0},{1,13},{5,9},{9,5},{13,1},{2,14},{6,10},... | collective-permute-start | bytes 884744 | tf_op jit(solution)/shard_map/gather/ppermute | solution.py:26
  9.5 1.8 %gather.2 = (bf16[1152,1152]{1,0:T(8,128)(2,1)S(1)}, bf16[576,1152]{1,0:T(8,128)(2,1)S(1)}, s32[512,1]{1,0:T(8,128)S(1)}, s32[1,512]{1,0:T(1,128)S(1)}, f32[2,128]{1,0:T(2,128)S(1)}) custom-call(bf16[128,1152]{1,0:T(8,128)(2,1)S(1)} %get-tuple-element.40.after.own, f32[1]{0:T(128)} %bitcast.2.scale, f32[1]{0:T(128)} %bitcast.3.bias, s32[1,16384]{1,0:T(1,128)S(1)} %copy-done, ...), custom_call_target="tpu_custom_call" | custom-call | flops 147456000 | bytes 147456 | tf_op jit(solution)/shard_map/gather/pallas_call | solution.py:212
  11.3 1.9 %collective-permute-done.2.t3 = bf16[128,1152]{1,0:T(8,128)(2,1)S(1)} collective-permute-done((bf16[128,1152]{1,0:T(8,128)(2,1)S(1)}, bf16[128,1152]{1,0:T(8,128)(2,1)S(1)}, u32[]{:S(2)}, u32[]{:S(2)}) %collective-permute-start.2) | collective-permute-done | bytes 294944 | tf_op jit(solution)/shard_map/gather/ppermute | solution.py:26
  13.1 1.5 %collective-permute-done.1.t1 = bf16[128,1152]{1,0:T(8,128)(2,1)S(1)} collective-permute-done((bf16[128,1152]{1,0:T(8,128)(2,1)S(1)}, bf16[128,1152]{1,0:T(8,128)(2,1)S(1)}, u32[]{:S(2)}, u32[]{:S(2)}) %collective-permute-start.1) | collective-permute-done | bytes 294944 | tf_op jit(solution)/shard_map/gather/ppermute | solution.py:26
  14.7 2.2 %collective-permute-start.3 = (bf16[256,1152]{1,0:T(8,128)(2,1)S(1)}, bf16[256,1152]{1,0:T(8,128)(2,1)S(1)}, u32[]{:S(2)}, u32[]{:S(2)}) collective-permute-start(bf16[256,1152]{1,0:T(8,128)(2,1)S(1)} %get-tuple-element.46.both), channel_id=1, source_target_pairs={{0,2},{2,0},{1,3},{3,1},{4,6},{6,4},{5,7},{7,5},{8,10},{10,8},{9,1... | collective-permute-start | bytes 1769480 | tf_op jit(solution)/shard_map/gather/ppermute | solution.py:26
  18.5 2.7 %project.1 = (bf16[512,1152]{1,0:T(8,128)(2,1)S(1)}, f32[512,1152]{1,0:T(8,128)S(1)}, f32[512,1]{1,0:T(8,128)S(1)}, bf16[576,512]{1,0:T(8,128)(2,1)S(1)}) custom-call(bf16[256,1152]{1,0:T(8,128)(2,1)S(1)} %get-tuple-element.46.both, bf16[256,1152]{1,0:T(8,128)(2,1)S(1)} %collective-permute-done.3.cores, bf16[1152,1152]{1,0:T(8,128)(2,1)S(1)} %get-tuple-element.47.weight, ...), custom_call_target="tpu_custom_call" | custom-call | bytes 147456 | tf_op jit(solution)/shard_map/project/pallas_call | solution.py:237
  23.2 2.1 %tile.1 = (bf16[512,512]{1,0:T(8,128)(2,1)S(1)}, f32[512,1152]{1,0:T(8,128)S(1)}, bf16[512,1152]{1,0:T(8,128)(2,1)S(1)}) custom-call(f32[2,128]{1,0:T(2,128)S(1)} %get-tuple-element.41.settings, s32[512,1]{1,0:T(8,128)S(1)} %get-tuple-element.42.left, s32[1,512]{1,0:T(1,128)S(1)} %get-tuple-element.43.right, bf16[512,1152]{1,0:T(8,128)(2,1)S(1)} %get-tuple-element.48.embed, ...), custom_call_target="tpu_custom_call" | custom-call | bytes 147456 | tf_op jit(solution)/shard_map/tile/pallas_call | solution.py:246
  27.5 1.4 %collective-permute-start.11 = (bf16[128,1152]{1,0:T(8,128)(2,1)S(1)}, bf16[128,1152]{1,0:T(8,128)(2,1)S(1)}, u32[]{:S(2)}, u32[]{:S(2)}) collective-permute-start(bf16[128,1152]{1,0:T(8,128)(2,1)S(1)} %get-tuple-element.64), channel_id=1, source_target_pairs={{0,8},{4,12},{8,0},{12,4},{1,9},{5,13},{9,1},{13,5},{2,10},{6,14},... | collective-permute-start | bytes 884744 | tf_op jit(solution)/shard_map/text/ppermute | solution.py:26
  30.4 2.7 %collective-permute-start.8 = (bf16[144,1152]{1,0:T(8,128)(2,1)S(1)}, bf16[144,1152]{1,0:T(8,128)(2,1)S(1)}, u32[]{:S(2)}, u32[]{:S(2)}) collective-permute-start(bf16[144,1152]{1,0:T(8,128)(2,1)S(1)} %get-tuple-element.61), channel_id=1, source_target_pairs={{0,32},{16,48},{32,0},{48,16},{1,33},{17,49},{33,1},{49,17},{2,34}... | collective-permute-start | bytes 995336 | tf_op jit(solution)/shard_map/weight/ppermute | solution.py:26
  34.5 3.4 %collective-permute-done.11.b2 = bf16[128,1152]{1,0:T(8,128)(2,1)S(1)} collective-permute-done((bf16[128,1152]{1,0:T(8,128)(2,1)S(1)}, bf16[128,1152]{1,0:T(8,128)(2,1)S(1)}, u32[]{:S(2)}, u32[]{:S(2)}) %collective-permute-start.11) | collective-permute-done | bytes 294944 | tf_op jit(solution)/shard_map/text/ppermute | solution.py:26
  39.1 2.9 %collective-permute-done.10.b1 = bf16[128,1152]{1,0:T(8,128)(2,1)S(1)} collective-permute-done((bf16[128,1152]{1,0:T(8,128)(2,1)S(1)}, bf16[128,1152]{1,0:T(8,128)(2,1)S(1)}, u32[]{:S(2)}, u32[]{:S(2)}) %collective-permute-start.10) | collective-permute-done | bytes 294944 | tf_op jit(solution)/shard_map/weight/ppermute | solution.py:26
  42.0 4.4 %collective-permute-done.12.b3 = bf16[128,1152]{1,0:T(8,128)(2,1)S(1)} collective-permute-done((bf16[128,1152]{1,0:T(8,128)(2,1)S(1)}, bf16[128,1152]{1,0:T(8,128)(2,1)S(1)}, u32[]{:S(2)}, u32[]{:S(2)}) %collective-permute-start.12) | collective-permute-done | bytes 294944 | tf_op jit(solution)/shard_map/weight/ppermute | solution.py:26
  46.4 1.4 %collective-permute-done.8.a2 = bf16[144,1152]{1,0:T(8,128)(2,1)S(1)} collective-permute-done((bf16[144,1152]{1,0:T(8,128)(2,1)S(1)}, bf16[144,1152]{1,0:T(8,128)(2,1)S(1)}, u32[]{:S(2)}, u32[]{:S(2)}) %collective-permute-start.8) | collective-permute-done | bytes 331808 | tf_op jit(solution)/shard_map/weight/ppermute | solution.py:26
  47.9 2.0 %collective-permute-done.9.a3 = bf16[144,1152]{1,0:T(8,128)(2,1)S(1)} collective-permute-done((bf16[144,1152]{1,0:T(8,128)(2,1)S(1)}, bf16[144,1152]{1,0:T(8,128)(2,1)S(1)}, u32[]{:S(2)}, u32[]{:S(2)}) %collective-permute-start.9) | collective-permute-done | bytes 331808 | tf_op jit(solution)/shard_map/weight/ppermute | solution.py:26
  50.8 2.1 %collective-permute-start.14 = (bf16[36,1152]{1,0:T(8,128)(2,1)S(1)}, bf16[36,1152]{1,0:T(8,128)(2,1)S(1)}, u32[]{:S(2)}, u32[]{:S(2)}) collective-permute-start(bf16[36,1152]{1,0:T(8,128)(2,1)S(1)} %get-tuple-element.68), channel_id=1, source_target_pairs={{0,8},{4,12},{8,0},{12,4},{1,9},{5,13},{9,1},{13,5},{2,10},{6,14},... | collective-permute-start | bytes 248840 | tf_op jit(solution)/shard_map/weight/ppermute | solution.py:26
  54.1 1.7 %collective-permute-done.14.a2 = bf16[36,1152]{1,0:T(8,128)(2,1)S(1)} collective-permute-done((bf16[36,1152]{1,0:T(8,128)(2,1)S(1)}, bf16[36,1152]{1,0:T(8,128)(2,1)S(1)}, u32[]{:S(2)}, u32[]{:S(2)}) %collective-permute-start.14) | collective-permute-done | bytes 82976 | tf_op jit(solution)/shard_map/weight/ppermute | solution.py:26
  55.8 2.8 %collective-permute-done.15.a3 = bf16[36,1152]{1,0:T(8,128)(2,1)S(1)} collective-permute-done((bf16[36,1152]{1,0:T(8,128)(2,1)S(1)}, bf16[36,1152]{1,0:T(8,128)(2,1)S(1)}, u32[]{:S(2)}, u32[]{:S(2)}) %collective-permute-start.15) | collective-permute-done | bytes 82976 | tf_op jit(solution)/shard_map/weight/ppermute | solution.py:26
  58.7 1.7 %collective-permute-start.17 = (bf16[36,1152]{1,0:T(8,128)(2,1)S(1)}, bf16[36,1152]{1,0:T(8,128)(2,1)S(1)}, u32[]{:S(2)}, u32[]{:S(2)}) collective-permute-start(bf16[36,1152]{1,0:T(8,128)(2,1)S(1)} %get-tuple-element.73.own.after), channel_id=1, source_target_pairs={{0,1},{1,0},{2,3},{3,2},{4,5},{5,4},{6,7},{7,6},{8,9},{9,8},{10,11... | collective-permute-start | bytes 248840 | tf_op jit(solution)/shard_map/weight/ppermute | solution.py:26
  60.4 1.9 %collective-permute-done.17.arrived = bf16[36,1152]{1,0:T(8,128)(2,1)S(1)} collective-permute-done((bf16[36,1152]{1,0:T(8,128)(2,1)S(1)}, bf16[36,1152]{1,0:T(8,128)(2,1)S(1)}, u32[]{:S(2)}, u32[]{:S(2)}) %collective-permute-start.17) | collective-permute-done | bytes 82976 | tf_op jit(solution)/shard_map/weight/ppermute | solution.py:26
  62.4 6.4 %collective-permute-start.20 = (f32[9,1152]{1,0:T(8,128)S(1)}, f32[9,1152]{1,0:T(8,128)S(1)}, u32[]{:S(2)}, u32[]{:S(2)}) collective-permute-start(f32[9,1152]{1,0:T(8,128)S(1)} %get-tuple-element.76), channel_id=1, source_target_pairs={{0,129},{2,131},{1,128},{3,130},{64,193},{66,195},{65,192},{67,194... | collective-permute-start | bytes 124424 | tf_op jit(solution)/shard_map/weight/ppermute | solution.py:192
  68.8 4.0 %collective-permute-start.19 = (f32[9,1152]{1,0:T(8,128)S(1)}, f32[9,1152]{1,0:T(8,128)S(1)}, u32[]{:S(2)}, u32[]{:S(2)}) collective-permute-start(f32[9,1152]{1,0:T(8,128)S(1)} %get-tuple-element.75), channel_id=1, source_target_pairs={{0,194},{2,192},{1,67},{3,65},{64,2},{66,0},{65,131},{67,129},{128... | collective-permute-start | bytes 124424 | tf_op jit(solution)/shard_map/weight/ppermute | solution.py:192
  73.7 1.6 %hidden.3 = (bf16[128,1152]{1,0:T(8,128)(2,1)}, f32[8,128]{1,0:T(8,128)S(1)}) custom-call(s32[1]{0:T(128)S(6)} %copy.10.count, f32[256,1152]{1,0:T(8,128)S(1)} %get-tuple-element.58.rows, bf16[128,1152]{1,0:T(8,128)(2,1)S(1)} %collective-permute-done.16.arrived, bf16[1152,1152]{1,0:T(8,128)(2,1)S(1)} %get-tuple-element.47.weight), custom_call_target="tpu_custom_call" | custom-call | flops 339738624 | bytes 2654208 | tf_op jit(solution)/shard_map/hidden/pallas_call | solution.py:299
  75.4 3.7 %collective-permute-done.19.a2 = f32[9,1152]{1,0:T(8,128)S(1)} collective-permute-done((f32[9,1152]{1,0:T(8,128)S(1)}, f32[9,1152]{1,0:T(8,128)S(1)}, u32[]{:S(2)}, u32[]{:S(2)}) %collective-permute-start.19) | collective-permute-done | bytes 41504 | tf_op jit(solution)/shard_map/weight/ppermute | solution.py:192
  (33 shorter events, 15.9 us)
Async XLA Ops:
  2.5 8.8 %collective-permute-start = (bf16[128,1152]{1,0:T(8,128)(2,1)S(1)}, bf16[128,1152]{1,0:T(8,128)(2,1)S(1)}, u32[]{:S(2)}, u32[]{:S(2)}) collective-permute-start(bf16[128,1152]{1,0:T(8,128)(2,1)S(1)} %get-tuple-element.40.after.own), channel_id=1, source_target_pairs={{0,16},{16,0},{1,17},{17,1},{2,18},{18,2},{3,19},{19,3},{4,20},{20... | collective-permute-start | bytes 884744 | tf_op jit(solution)/shard_map/gather/ppermute | solution.py:26
  4.6 8.5 %collective-permute-start.2 = (bf16[128,1152]{1,0:T(8,128)(2,1)S(1)}, bf16[128,1152]{1,0:T(8,128)(2,1)S(1)}, u32[]{:S(2)}, u32[]{:S(2)}) collective-permute-start(bf16[128,1152]{1,0:T(8,128)(2,1)S(1)} %get-tuple-element.45.t0), channel_id=1, source_target_pairs={{0,12},{4,8},{8,4},{12,0},{1,13},{5,9},{9,5},{13,1},{2,14},{6,10},... | collective-permute-start | bytes 884744 | tf_op jit(solution)/shard_map/gather/ppermute | solution.py:26
  7.3 7.3 %collective-permute-start.1 = (bf16[128,1152]{1,0:T(8,128)(2,1)S(1)}, bf16[128,1152]{1,0:T(8,128)(2,1)S(1)}, u32[]{:S(2)}, u32[]{:S(2)}) collective-permute-start(bf16[128,1152]{1,0:T(8,128)(2,1)S(1)} %get-tuple-element.45.t0), channel_id=1, source_target_pairs={{0,4},{4,0},{8,12},{12,8},{1,5},{5,1},{9,13},{13,9},{2,6},{6,2},{1... | collective-permute-start | bytes 884744 | tf_op jit(solution)/shard_map/gather/ppermute | solution.py:26
  8.6 0.8 %copy-start = (s32[1,16384]{1,0:T(1,128)S(1)}, s32[1,16384]{1,0:T(1,128)}, u32[]{:S(2)}) copy-start(s32[1,16384]{1,0:T(1,128)} %pair_ids.1) | copy-start | bytes 196612
  14.7 3.9 %collective-permute-start.3 = (bf16[256,1152]{1,0:T(8,128)(2,1)S(1)}, bf16[256,1152]{1,0:T(8,128)(2,1)S(1)}, u32[]{:S(2)}, u32[]{:S(2)}) collective-permute-start(bf16[256,1152]{1,0:T(8,128)(2,1)S(1)} %get-tuple-element.46.both), channel_id=1, source_target_pairs={{0,2},{2,0},{1,3},{3,1},{4,6},{6,4},{5,7},{7,5},{8,10},{10,8},{9,1... | collective-permute-start | bytes 1769480 | tf_op jit(solution)/shard_map/gather/ppermute | solution.py:26
  16.9 5.4 %collective-permute-start.4 = (bf16[64,1152]{1,0:T(8,128)(2,1)S(1)}, bf16[64,1152]{1,0:T(8,128)(2,1)S(1)}, u32[]{:S(2)}, u32[]{:S(2)}) collective-permute-start(bf16[64,1152]{1,0:T(8,128)(2,1)S(1)} %get-tuple-element.51), channel_id=1, source_target_pairs={{0,4},{4,0},{8,12},{12,8},{1,5},{5,1},{9,13},{13,9},{2,6},{6,2},{1... | collective-permute-start | bytes 442376 | tf_op jit(solution)/shard_map/gather/ppermute | solution.py:26
  16.9 6.3 %collective-permute-start.5 = (bf16[64,1152]{1,0:T(8,128)(2,1)S(1)}, bf16[64,1152]{1,0:T(8,128)(2,1)S(1)}, u32[]{:S(2)}, u32[]{:S(2)}) collective-permute-start(bf16[64,1152]{1,0:T(8,128)(2,1)S(1)} %get-tuple-element.52), channel_id=1, source_target_pairs={{0,12},{4,8},{8,4},{12,0},{1,13},{5,9},{9,5},{13,1},{2,14},{6,10},... | collective-permute-start | bytes 442376 | tf_op jit(solution)/shard_map/gather/ppermute | solution.py:26
  25.3 3.8 %collective-permute-start.6 = (bf16[512,1152]{1,0:T(8,128)(2,1)S(1)}, bf16[512,1152]{1,0:T(8,128)(2,1)S(1)}, u32[]{:S(2)}, u32[]{:S(2)}) collective-permute-start(bf16[512,1152]{1,0:T(8,128)(2,1)S(1)} %get-tuple-element.54), channel_id=1, source_target_pairs={{0,2},{2,0},{1,3},{3,1},{4,6},{6,4},{5,7},{7,5},{8,10},{10,8},{9,1... | collective-permute-start | bytes 3538952 | tf_op jit(solution)/shard_map/core/ppermute | solution.py:26
  27.5 10.4 %collective-permute-start.11 = (bf16[128,1152]{1,0:T(8,128)(2,1)S(1)}, bf16[128,1152]{1,0:T(8,128)(2,1)S(1)}, u32[]{:S(2)}, u32[]{:S(2)}) collective-permute-start(bf16[128,1152]{1,0:T(8,128)(2,1)S(1)} %get-tuple-element.64), channel_id=1, source_target_pairs={{0,8},{4,12},{8,0},{12,4},{1,9},{5,13},{9,1},{13,5},{2,10},{6,14},... | collective-permute-start | bytes 884744 | tf_op jit(solution)/shard_map/text/ppermute | solution.py:26
  30.1 16.3 %collective-permute-start.7 = (bf16[144,1152]{1,0:T(8,128)(2,1)S(1)}, bf16[144,1152]{1,0:T(8,128)(2,1)S(1)}, u32[]{:S(2)}, u32[]{:S(2)}) collective-permute-start(bf16[144,1152]{1,0:T(8,128)(2,1)S(1)} %get-tuple-element.60), channel_id=1, source_target_pairs={{0,16},{16,0},{32,48},{48,32},{1,17},{17,1},{33,49},{49,33},{2,18}... | collective-permute-start | bytes 995336 | tf_op jit(solution)/shard_map/weight/ppermute | solution.py:26
  30.4 17.4 %collective-permute-start.8 = (bf16[144,1152]{1,0:T(8,128)(2,1)S(1)}, bf16[144,1152]{1,0:T(8,128)(2,1)S(1)}, u32[]{:S(2)}, u32[]{:S(2)}) collective-permute-start(bf16[144,1152]{1,0:T(8,128)(2,1)S(1)} %get-tuple-element.61), channel_id=1, source_target_pairs={{0,32},{16,48},{32,0},{48,16},{1,33},{17,49},{33,1},{49,17},{2,34}... | collective-permute-start | bytes 995336 | tf_op jit(solution)/shard_map/weight/ppermute | solution.py:26
  33.2 16.7 %collective-permute-start.9 = (bf16[144,1152]{1,0:T(8,128)(2,1)S(1)}, bf16[144,1152]{1,0:T(8,128)(2,1)S(1)}, u32[]{:S(2)}, u32[]{:S(2)}) collective-permute-start(bf16[144,1152]{1,0:T(8,128)(2,1)S(1)} %get-tuple-element.62), channel_id=1, source_target_pairs={{0,48},{16,32},{32,16},{48,0},{1,49},{17,33},{33,17},{49,1},{2,50}... | collective-permute-start | bytes 995336 | tf_op jit(solution)/shard_map/weight/ppermute | solution.py:26
  34.0 8.0 %collective-permute-start.10 = (bf16[128,1152]{1,0:T(8,128)(2,1)S(1)}, bf16[128,1152]{1,0:T(8,128)(2,1)S(1)}, u32[]{:S(2)}, u32[]{:S(2)}) collective-permute-start(bf16[128,1152]{1,0:T(8,128)(2,1)S(1)} %get-tuple-element.63), channel_id=1, source_target_pairs={{0,4},{4,0},{8,12},{12,8},{1,5},{5,1},{9,13},{13,9},{2,6},{6,2},{1... | collective-permute-start | bytes 884744 | tf_op jit(solution)/shard_map/weight/ppermute | solution.py:26
  37.9 8.5 %collective-permute-start.12 = (bf16[128,1152]{1,0:T(8,128)(2,1)S(1)}, bf16[128,1152]{1,0:T(8,128)(2,1)S(1)}, u32[]{:S(2)}, u32[]{:S(2)}) collective-permute-start(bf16[128,1152]{1,0:T(8,128)(2,1)S(1)} %get-tuple-element.65), channel_id=1, source_target_pairs={{0,12},{4,8},{8,4},{12,0},{1,13},{5,9},{9,5},{13,1},{2,14},{6,10},... | collective-permute-start | bytes 884744 | tf_op jit(solution)/shard_map/weight/ppermute | solution.py:26
  50.1 3.9 %collective-permute-start.13 = (bf16[36,1152]{1,0:T(8,128)(2,1)S(1)}, bf16[36,1152]{1,0:T(8,128)(2,1)S(1)}, u32[]{:S(2)}, u32[]{:S(2)}) collective-permute-start(bf16[36,1152]{1,0:T(8,128)(2,1)S(1)} %get-tuple-element.67), channel_id=1, source_target_pairs={{0,4},{4,0},{8,12},{12,8},{1,5},{5,1},{9,13},{13,9},{2,6},{6,2},{1... | collective-permute-start | bytes 248840 | tf_op jit(solution)/shard_map/weight/ppermute | solution.py:26
  50.8 5.0 %collective-permute-start.14 = (bf16[36,1152]{1,0:T(8,128)(2,1)S(1)}, bf16[36,1152]{1,0:T(8,128)(2,1)S(1)}, u32[]{:S(2)}, u32[]{:S(2)}) collective-permute-start(bf16[36,1152]{1,0:T(8,128)(2,1)S(1)} %get-tuple-element.68), channel_id=1, source_target_pairs={{0,8},{4,12},{8,0},{12,4},{1,9},{5,13},{9,1},{13,5},{2,10},{6,14},... | collective-permute-start | bytes 248840 | tf_op jit(solution)/shard_map/weight/ppermute | solution.py:26
  52.8 5.7 %collective-permute-start.15 = (bf16[36,1152]{1,0:T(8,128)(2,1)S(1)}, bf16[36,1152]{1,0:T(8,128)(2,1)S(1)}, u32[]{:S(2)}, u32[]{:S(2)}) collective-permute-start(bf16[36,1152]{1,0:T(8,128)(2,1)S(1)} %get-tuple-element.69), channel_id=1, source_target_pairs={{0,12},{4,8},{8,4},{12,0},{1,13},{5,9},{9,5},{13,1},{2,14},{6,10},... | collective-permute-start | bytes 248840 | tf_op jit(solution)/shard_map/weight/ppermute | solution.py:26
  58.6 15.1 %collective-permute-start.16 = (bf16[128,1152]{1,0:T(8,128)(2,1)S(1)}, bf16[128,1152]{1,0:T(8,128)(2,1)S(1)}, u32[]{:S(2)}, u32[]{:S(2)}) collective-permute-start(bf16[128,1152]{1,0:T(8,128)(2,1)S(1)} %get-tuple-element.70), channel_id=1, source_target_pairs={{0,16},{16,0},{1,17},{17,1},{2,18},{18,2},{3,19},{19,3},{4,20},{20... | collective-permute-start | bytes 884744 | tf_op jit(solution)/shard_map/hidden/ppermute | solution.py:26
  58.7 3.7 %collective-permute-start.17 = (bf16[36,1152]{1,0:T(8,128)(2,1)S(1)}, bf16[36,1152]{1,0:T(8,128)(2,1)S(1)}, u32[]{:S(2)}, u32[]{:S(2)}) collective-permute-start(bf16[36,1152]{1,0:T(8,128)(2,1)S(1)} %get-tuple-element.73.own.after), channel_id=1, source_target_pairs={{0,1},{1,0},{2,3},{3,2},{4,5},{5,4},{6,7},{7,6},{8,9},{9,8},{10,11... | collective-permute-start | bytes 248840 | tf_op jit(solution)/shard_map/weight/ppermute | solution.py:26
  62.4 13.0 %collective-permute-start.20 = (f32[9,1152]{1,0:T(8,128)S(1)}, f32[9,1152]{1,0:T(8,128)S(1)}, u32[]{:S(2)}, u32[]{:S(2)}) collective-permute-start(f32[9,1152]{1,0:T(8,128)S(1)} %get-tuple-element.76), channel_id=1, source_target_pairs={{0,129},{2,131},{1,128},{3,130},{64,193},{66,195},{65,192},{67,194... | collective-permute-start | bytes 124424 | tf_op jit(solution)/shard_map/weight/ppermute | solution.py:192
  68.8 10.3 %collective-permute-start.19 = (f32[9,1152]{1,0:T(8,128)S(1)}, f32[9,1152]{1,0:T(8,128)S(1)}, u32[]{:S(2)}, u32[]{:S(2)}) collective-permute-start(f32[9,1152]{1,0:T(8,128)S(1)} %get-tuple-element.75), channel_id=1, source_target_pairs={{0,194},{2,192},{1,67},{3,65},{64,2},{66,0},{65,131},{67,129},{128... | collective-permute-start | bytes 124424 | tf_op jit(solution)/shard_map/weight/ppermute | solution.py:192
  72.8 6.3 %collective-permute-start.18 = (f32[9,1152]{1,0:T(8,128)S(1)}, f32[9,1152]{1,0:T(8,128)S(1)}, u32[]{:S(2)}, u32[]{:S(2)}) collective-permute-start(f32[9,1152]{1,0:T(8,128)S(1)} %get-tuple-element.75), channel_id=1, source_target_pairs={{0,195},{2,193},{1,66},{3,64},{64,3},{66,1},{65,130},{67,128},{128... | collective-permute-start | bytes 124424 | tf_op jit(solution)/shard_map/weight/ppermute | solution.py:192

commit v7 on v6

--- a/solution.py
+++ b/solution.py
@@ -144,29 +144,32 @@
     t3[...] = terms[3 * ROWS :].astype(bf16)
 
 
-def first_sum(own, a1, a2, a3, b1, b2, b3, out, s1, s2, s3, held):
+def first_sum(own, a2, a1, a3, b1, b2, b3, out, s1, s2, s3, held):
     held[...] = own[...] + a2[...].astype(f32) + a1[...].astype(f32) + a3[...].astype(f32)
     out[...] = held[:36]
     for k, send in enumerate((s1, s2, s3)):
         send[...] = held[(k + 1) * 36 : (k + 2) * 36].astype(bf16)
 
 
-def second_sum(own, a1, a2, a3, rows, send, rows_send):
+def second_sum(own, a2, a1, a3, rows, keep, send, rows_send, held):
     total = own[...] + a2[...].astype(f32) + a1[...].astype(f32) + a3[...].astype(f32)
-    send[...] = total.astype(bf16)
+    total = total.astype(bf16).astype(f32)
+    held[...] = total
+    keep[...] = total
+    send[...] = jnp.concatenate([held[:9], held[18:]], 0).astype(bf16)
     rows_send[...] = rows[ROWS:].astype(bf16)
 
 
-def third_sum(own, arrived, out, near, far, mine, held):
-    mine[...] = own[...].astype(f32)
+def third_sum(own, arrived, out, near, far, held):
     held[...] = arrived[...].astype(f32)
-    out[...] = mine[:9] + held[:9]
-    near[...] = mine[9:18] + held[27:36]
-    far[...] = mine[18:27] + held[18:27]
-
-
-def last_sum(after, own, a1, a2, a3, out):
-    out[...] = own[...] + (a1[...] + a2[...]) + a3[...]
+    out[...] = own[:9] + held[:9]
+    near[...] = (own[9:18] + held[18:]).astype(bf16)
+    far[...] = (own[18:27] + held[9:18]).astype(bf16)
+
+
+def last_sum(after, own, a1, a3, a2, out):
+    sides = a1[...].astype(f32) + a2[...].astype(f32)
+    out[...] = own[...] + sides + a3[...].astype(f32)
 
 
 def text_sum(after, count, terms, b1, b2, b3, out):
@@ -279,21 +282,26 @@
             0,
             block,
             [pltpu.VMEM((144, WIDTH), f32)],
-        )(own, s1, s2, s3, u1, u2, u3)
+        )(own, s2, s1, s3, u1, u2, u3)
         s2, s1, s3 = xor(s2, "y", 2), xor(s1, "y", 1), xor(s3, "y", 3)
-        whole_send, rows_send = call(second_sum, [small_b, wide], [VMEM] * 5, 0, block)(
-            whole, s1, s2, s3, rows
-        )
+        whole, whole_send, rows_send = call(
+            second_sum,
+            [small, shape(bf16, 27, WIDTH), wide],
+            [VMEM] * 5,
+            0,
+            block,
+            [pltpu.VMEM((36, WIDTH), f32)],
+        )(whole, s2, s1, s3, rows)
         arrived = xor(whole_send, "zl", 1)
         whole, near, far = call(
             third_sum,
-            [shape(f32, 9, WIDTH)] * 3,
+            [shape(f32, 9, WIDTH)] + [shape(bf16, 9, WIDTH)] * 2,
             [VMEM] * 2,
             0,
             block,
-            [pltpu.VMEM((36, WIDTH), f32)] * 2,
-        )(whole_send, arrived)
-        got = [along_z(near, 1, 1), along_z(near, 2, 1), along_z(far, 3, 0)]
+            [pltpu.VMEM((27, WIDTH), f32)],
+        )(whole, arrived)
+        got = [along_z(near, 1, 1), along_z(far, 3, 0), along_z(near, 2, 1)]
     with jax.named_scope("hidden"):
         rows_x = xor(rows_send, "x0", 1)
         hidden_grad, done = call(

time: 79.9 us -> 76.2 us (0.954)
  waiting for transfers between devices: 30.1 us -> 26.8 us
    ppermute x18, waiting for transfers between devices: 26.4 us -> 24.3 us  [xor(): return lax.ppermute(x, axis, [(i, i ^ step) for i in range(size)])]
    ppermute x3, waiting for transfers between devices: 3.7 us -> 2.53 us  [along_z(): return lax.ppermute(x, ('zh', 'c', 'zl'), pairs)]
    ppermute x18, starting transfers between devices: 22.4 us -> 21.5 us  [xor(): return lax.ppermute(x, axis, [(i, i ^ step) for i in range(size)])]
  transfers between devices with their start and end apart: 21 -> 21, of which waited for: 15 -> 16; matrix products, arithmetic and copies ran while one was open for 0% -> 0% of each run, Pallas kernels for 11% -> 12%
where the time goes in v7:
time: 76.2 us; the launch traced here: 75.9 us
  starting transfers between devices  32.2 us (42%)
  waiting for transfers between devices  26.8 us (35%)
  Pallas kernels  13.4 us (18%)
  between operations  2.67 us (4%)
  local copies, waits for them, and re-layouts  0.83 us (1%)
    ppermute x18, waiting for transfers between devices, xor(): return lax.ppermute(x, axis, [(i, i ^ step) for i in range(size)])  24.3 us
    ppermute x18, starting transfers between devices, xor(): return lax.ppermute(x, axis, [(i, i ^ step) for i in range(size)])  21.5 us
    ppermute x3, starting transfers between devices, along_z(): return lax.ppermute(x, ('zh', 'c', 'zl'), pairs)  10.8 us
    pallas_call x1, Pallas kernels, per_device(): call(project, [shape(bf16, 512, WIDTH), tall, shape(f32, 512, 1), shape(b...  2.7 us
    ppermute x3, waiting for transfers between devices, along_z(): return lax.ppermute(x, ('zh', 'c', 'zl'), pairs)  2.53 us
    pallas_call x1, Pallas kernels, per_device(): call(tile, [shape(bf16, 512, 512), tall, shape(bf16, 512, WIDTH)], [VMEM]...  2.09 us
    pallas_call x1, Pallas kernels, per_device(): call(ahead, [shape(bf16, WIDTH, WIDTH), shape(bf16, 576, WIDTH), shape(jn...  1.78 us
    pallas_call x1, Pallas kernels, per_device(): call(back, [wide, shape(f32, 8, ROWS)], [SMEM] + [VMEM] * 3, 2 * block *...  1.65 us
  transfers between devices with their start and end apart: 21, of which 16 were waited for; matrix products, arithmetic and copies ran while one was open for 0% of the time, Pallas kernels for 12%

profile of v7, /device:TPU:1, one launch (start us, length us, event | category | flops | bytes accessed | tf_op | source)
XLA Modules:
  0.0 75.9 jit_solution(10823624076822916763)
XLA Ops:
  2.5 2.1 %collective-permute-start = (bf16[128,1152]{1,0:T(8,128)(2,1)S(1)}, bf16[128,1152]{1,0:T(8,128)(2,1)S(1)}, u32[]{:S(2)}, u32[]{:S(2)}) collective-permute-start(bf16[128,1152]{1,0:T(8,128)(2,1)S(1)} %get-tuple-element.41.after.own), channel_id=1, source_target_pairs={{0,16},{16,0},{1,17},{17,1},{2,18},{18,2},{3,19},{19,3},{4,20},{20... | collective-permute-start | bytes 884744 | tf_op jit(solution)/shard_map/gather/ppermute | solution.py:26
  4.6 2.7 %collective-permute-start.2 = (bf16[128,1152]{1,0:T(8,128)(2,1)S(1)}, bf16[128,1152]{1,0:T(8,128)(2,1)S(1)}, u32[]{:S(2)}, u32[]{:S(2)}) collective-permute-start(bf16[128,1152]{1,0:T(8,128)(2,1)S(1)} %get-tuple-element.46.t0), channel_id=1, source_target_pairs={{0,12},{4,8},{8,4},{12,0},{1,13},{5,9},{9,5},{13,1},{2,14},{6,10},... | collective-permute-start | bytes 884744 | tf_op jit(solution)/shard_map/gather/ppermute | solution.py:26
  9.5 1.8 %gather.2 = (bf16[1152,1152]{1,0:T(8,128)(2,1)S(1)}, bf16[576,1152]{1,0:T(8,128)(2,1)S(1)}, s32[512,1]{1,0:T(8,128)S(1)}, s32[1,512]{1,0:T(1,128)S(1)}, f32[2,128]{1,0:T(2,128)S(1)}) custom-call(bf16[128,1152]{1,0:T(8,128)(2,1)S(1)} %get-tuple-element.41.after.own, f32[1]{0:T(128)} %bitcast.2.scale, f32[1]{0:T(128)} %bitcast.3.bias, s32[1,16384]{1,0:T(1,128)S(1)} %copy-done, ...), custom_call_target="tpu_custom_call" | custom-call | flops 147456000 | bytes 147456 | tf_op jit(solution)/shard_map/gather/pallas_call | solution.py:215
  11.3 1.9 %collective-permute-done.2.t3 = bf16[128,1152]{1,0:T(8,128)(2,1)S(1)} collective-permute-done((bf16[128,1152]{1,0:T(8,128)(2,1)S(1)}, bf16[128,1152]{1,0:T(8,128)(2,1)S(1)}, u32[]{:S(2)}, u32[]{:S(2)}) %collective-permute-start.2) | collective-permute-done | bytes 294944 | tf_op jit(solution)/shard_map/gather/ppermute | solution.py:26
  13.1 1.5 %collective-permute-done.1.t1 = bf16[128,1152]{1,0:T(8,128)(2,1)S(1)} collective-permute-done((bf16[128,1152]{1,0:T(8,128)(2,1)S(1)}, bf16[128,1152]{1,0:T(8,128)(2,1)S(1)}, u32[]{:S(2)}, u32[]{:S(2)}) %collective-permute-start.1) | collective-permute-done | bytes 294944 | tf_op jit(solution)/shard_map/gather/ppermute | solution.py:26
  14.7 2.2 %collective-permute-start.3 = (bf16[256,1152]{1,0:T(8,128)(2,1)S(1)}, bf16[256,1152]{1,0:T(8,128)(2,1)S(1)}, u32[]{:S(2)}, u32[]{:S(2)}) collective-permute-start(bf16[256,1152]{1,0:T(8,128)(2,1)S(1)} %get-tuple-element.47.both), channel_id=1, source_target_pairs={{0,2},{2,0},{1,3},{3,1},{4,6},{6,4},{5,7},{7,5},{8,10},{10,8},{9,1... | collective-permute-start | bytes 1769480 | tf_op jit(solution)/shard_map/gather/ppermute | solution.py:26
  16.9 1.2 %collective-permute-start.5 = (bf16[64,1152]{1,0:T(8,128)(2,1)S(1)}, bf16[64,1152]{1,0:T(8,128)(2,1)S(1)}, u32[]{:S(2)}, u32[]{:S(2)}) collective-permute-start(bf16[64,1152]{1,0:T(8,128)(2,1)S(1)} %get-tuple-element.53), channel_id=1, source_target_pairs={{0,12},{4,8},{8,4},{12,0},{1,13},{5,9},{9,5},{13,1},{2,14},{6,10},... | collective-permute-start | bytes 442376 | tf_op jit(solution)/shard_map/gather/ppermute | solution.py:26
  18.5 2.7 %project.1 = (bf16[512,1152]{1,0:T(8,128)(2,1)S(1)}, f32[512,1152]{1,0:T(8,128)S(1)}, f32[512,1]{1,0:T(8,128)S(1)}, bf16[576,512]{1,0:T(8,128)(2,1)S(1)}) custom-call(bf16[256,1152]{1,0:T(8,128)(2,1)S(1)} %get-tuple-element.47.both, bf16[256,1152]{1,0:T(8,128)(2,1)S(1)} %collective-permute-done.3.cores, bf16[1152,1152]{1,0:T(8,128)(2,1)S(1)} %get-tuple-element.48.weight, ...), custom_call_target="tpu_custom_call" | custom-call | bytes 147456 | tf_op jit(solution)/shard_map/project/pallas_call | solution.py:240
  23.2 2.1 %tile.1 = (bf16[512,512]{1,0:T(8,128)(2,1)S(1)}, f32[512,1152]{1,0:T(8,128)S(1)}, bf16[512,1152]{1,0:T(8,128)(2,1)S(1)}) custom-call(f32[2,128]{1,0:T(2,128)S(1)} %get-tuple-element.42.settings, s32[512,1]{1,0:T(8,128)S(1)} %get-tuple-element.43.left, s32[1,512]{1,0:T(1,128)S(1)} %get-tuple-element.44.right, bf16[512,1152]{1,0:T(8,128)(2,1)S(1)} %get-tuple-element.49.embed, ...), custom_call_target="tpu_custom_call" | custom-call | bytes 147456 | tf_op jit(solution)/shard_map/tile/pallas_call | solution.py:249
  25.3 1.3 %collective-permute-start.6 = (bf16[512,1152]{1,0:T(8,128)(2,1)S(1)}, bf16[512,1152]{1,0:T(8,128)(2,1)S(1)}, u32[]{:S(2)}, u32[]{:S(2)}) collective-permute-start(bf16[512,1152]{1,0:T(8,128)(2,1)S(1)} %get-tuple-element.55), channel_id=1, source_target_pairs={{0,2},{2,0},{1,3},{3,1},{4,6},{6,4},{5,7},{7,5},{8,10},{10,8},{9,1... | collective-permute-start | bytes 3538952 | tf_op jit(solution)/shard_map/core/ppermute | solution.py:26
  27.5 1.4 %collective-permute-start.11 = (bf16[128,1152]{1,0:T(8,128)(2,1)S(1)}, bf16[128,1152]{1,0:T(8,128)(2,1)S(1)}, u32[]{:S(2)}, u32[]{:S(2)}) collective-permute-start(bf16[128,1152]{1,0:T(8,128)(2,1)S(1)} %get-tuple-element.65), channel_id=1, source_target_pairs={{0,8},{4,12},{8,0},{12,4},{1,9},{5,13},{9,1},{13,5},{2,10},{6,14},... | collective-permute-start | bytes 884744 | tf_op jit(solution)/shard_map/text/ppermute | solution.py:26
  30.1 2.5 %collective-permute-start.7 = (bf16[144,1152]{1,0:T(8,128)(2,1)S(1)}, bf16[144,1152]{1,0:T(8,128)(2,1)S(1)}, u32[]{:S(2)}, u32[]{:S(2)}) collective-permute-start(bf16[144,1152]{1,0:T(8,128)(2,1)S(1)} %get-tuple-element.61), channel_id=1, source_target_pairs={{0,32},{16,48},{32,0},{48,16},{1,33},{17,49},{33,1},{49,17},{2,34}... | collective-permute-start | bytes 995336 | tf_op jit(solution)/shard_map/weight/ppermute | solution.py:26
  33.9 4.0 %collective-permute-done.11.b2 = bf16[128,1152]{1,0:T(8,128)(2,1)S(1)} collective-permute-done((bf16[128,1152]{1,0:T(8,128)(2,1)S(1)}, bf16[128,1152]{1,0:T(8,128)(2,1)S(1)}, u32[]{:S(2)}, u32[]{:S(2)}) %collective-permute-start.11) | collective-permute-done | bytes 294944 | tf_op jit(solution)/shard_map/text/ppermute | solution.py:26
  39.1 3.5 %collective-permute-done.10.b1 = bf16[128,1152]{1,0:T(8,128)(2,1)S(1)} collective-permute-done((bf16[128,1152]{1,0:T(8,128)(2,1)S(1)}, bf16[128,1152]{1,0:T(8,128)(2,1)S(1)}, u32[]{:S(2)}, u32[]{:S(2)}) %collective-permute-start.10) | collective-permute-done | bytes 294944 | tf_op jit(solution)/shard_map/weight/ppermute | solution.py:26
  42.6 3.8 %collective-permute-done.12.b3 = bf16[128,1152]{1,0:T(8,128)(2,1)S(1)} collective-permute-done((bf16[128,1152]{1,0:T(8,128)(2,1)S(1)}, bf16[128,1152]{1,0:T(8,128)(2,1)S(1)}, u32[]{:S(2)}, u32[]{:S(2)}) %collective-permute-start.12) | collective-permute-done | bytes 294944 | tf_op jit(solution)/shard_map/weight/ppermute | solution.py:26
  47.3 1.2 %collective-permute-done.9.a3 = bf16[144,1152]{1,0:T(8,128)(2,1)S(1)} collective-permute-done((bf16[144,1152]{1,0:T(8,128)(2,1)S(1)}, bf16[144,1152]{1,0:T(8,128)(2,1)S(1)}, u32[]{:S(2)}, u32[]{:S(2)}) %collective-permute-start.9) | collective-permute-done | bytes 331808 | tf_op jit(solution)/shard_map/weight/ppermute | solution.py:26
  48.8 1.7 %collective-permute-start.13 = (bf16[36,1152]{1,0:T(8,128)(2,1)S(1)}, bf16[36,1152]{1,0:T(8,128)(2,1)S(1)}, u32[]{:S(2)}, u32[]{:S(2)}) collective-permute-start(bf16[36,1152]{1,0:T(8,128)(2,1)S(1)} %get-tuple-element.68), channel_id=1, source_target_pairs={{0,8},{4,12},{8,0},{12,4},{1,9},{5,13},{9,1},{13,5},{2,10},{6,14},... | collective-permute-start | bytes 248840 | tf_op jit(solution)/shard_map/weight/ppermute | solution.py:26
  50.8 1.3 %collective-permute-start.15 = (bf16[36,1152]{1,0:T(8,128)(2,1)S(1)}, bf16[36,1152]{1,0:T(8,128)(2,1)S(1)}, u32[]{:S(2)}, u32[]{:S(2)}) collective-permute-start(bf16[36,1152]{1,0:T(8,128)(2,1)S(1)} %get-tuple-element.70), channel_id=1, source_target_pairs={{0,12},{4,8},{8,4},{12,0},{1,13},{5,9},{9,5},{13,1},{2,14},{6,10},... | collective-permute-start | bytes 248840 | tf_op jit(solution)/shard_map/weight/ppermute | solution.py:26
  52.1 2.0 %collective-permute-done.13.a2 = bf16[36,1152]{1,0:T(8,128)(2,1)S(1)} collective-permute-done((bf16[36,1152]{1,0:T(8,128)(2,1)S(1)}, bf16[36,1152]{1,0:T(8,128)(2,1)S(1)}, u32[]{:S(2)}, u32[]{:S(2)}) %collective-permute-start.13) | collective-permute-done | bytes 82976 | tf_op jit(solution)/shard_map/weight/ppermute | solution.py:26
  56.9 1.6 %collective-permute-start.17 = (bf16[27,1152]{1,0:T(8,128)(2,1)S(1)}, bf16[27,1152]{1,0:T(8,128)(2,1)S(1)}, u32[]{:S(2)}, u32[]{:S(2)}) collective-permute-start(bf16[27,1152]{1,0:T(8,128)(2,1)S(1)} %get-tuple-element.75.after), channel_id=1, source_target_pairs={{0,1},{1,0},{2,3},{3,2},{4,5},{5,4},{6,7},{7,6},{8,9},{9,8},{10,11... | collective-permute-start | bytes 186632 | tf_op jit(solution)/shard_map/weight/ppermute | solution.py:26
  60.4 9.1 %collective-permute-start.20 = (bf16[9,1152]{1,0:T(8,128)(2,1)S(1)}, bf16[9,1152]{1,0:T(8,128)(2,1)S(1)}, u32[]{:S(2)}, u32[]{:S(2)}) collective-permute-start(bf16[9,1152]{1,0:T(8,128)(2,1)S(1)} %get-tuple-element.77), channel_id=1, source_target_pairs={{0,194},{2,192},{1,67},{3,65},{64,2},{66,0},{65,131},{67,129},{128... | collective-permute-start | bytes 62216 | tf_op jit(solution)/shard_map/weight/ppermute | solution.py:195
  69.5 1.6 %collective-permute-start.19 = (bf16[9,1152]{1,0:T(8,128)(2,1)S(1)}, bf16[9,1152]{1,0:T(8,128)(2,1)S(1)}, u32[]{:S(2)}, u32[]{:S(2)}) collective-permute-start(bf16[9,1152]{1,0:T(8,128)(2,1)S(1)} %get-tuple-element.78), channel_id=1, source_target_pairs={{0,129},{2,131},{1,128},{3,130},{64,193},{66,195},{65,192},{67,194... | collective-permute-start | bytes 62216 | tf_op jit(solution)/shard_map/weight/ppermute | solution.py:195
  71.1 1.6 %hidden.3 = (bf16[128,1152]{1,0:T(8,128)(2,1)}, f32[8,128]{1,0:T(8,128)S(1)}) custom-call(s32[1]{0:T(128)S(6)} %copy.10.count, f32[256,1152]{1,0:T(8,128)S(1)} %get-tuple-element.59.rows, bf16[128,1152]{1,0:T(8,128)(2,1)S(1)} %collective-permute-done.16.arrived, bf16[1152,1152]{1,0:T(8,128)(2,1)S(1)} %get-tuple-element.48.weight), custom_call_target="tpu_custom_call" | custom-call | flops 339738624 | bytes 2654208 | tf_op jit(solution)/shard_map/hidden/pallas_call | solution.py:307
  72.8 2.5 %collective-permute-done.19.a3 = bf16[9,1152]{1,0:T(8,128)(2,1)S(1)} collective-permute-done((bf16[9,1152]{1,0:T(8,128)(2,1)S(1)}, bf16[9,1152]{1,0:T(8,128)(2,1)S(1)}, u32[]{:S(2)}, u32[]{:S(2)}) %collective-permute-start.19) | collective-permute-done | bytes 20768 | tf_op jit(solution)/shard_map/weight/ppermute | solution.py:195
  (33 shorter events, 15.6 us)
Async XLA Ops:
  2.5 8.8 %collective-permute-start = (bf16[128,1152]{1,0:T(8,128)(2,1)S(1)}, bf16[128,1152]{1,0:T(8,128)(2,1)S(1)}, u32[]{:S(2)}, u32[]{:S(2)}) collective-permute-start(bf16[128,1152]{1,0:T(8,128)(2,1)S(1)} %get-tuple-element.41.after.own), channel_id=1, source_target_pairs={{0,16},{16,0},{1,17},{17,1},{2,18},{18,2},{3,19},{19,3},{4,20},{20... | collective-permute-start | bytes 884744 | tf_op jit(solution)/shard_map/gather/ppermute | solution.py:26
  4.6 8.5 %collective-permute-start.2 = (bf16[128,1152]{1,0:T(8,128)(2,1)S(1)}, bf16[128,1152]{1,0:T(8,128)(2,1)S(1)}, u32[]{:S(2)}, u32[]{:S(2)}) collective-permute-start(bf16[128,1152]{1,0:T(8,128)(2,1)S(1)} %get-tuple-element.46.t0), channel_id=1, source_target_pairs={{0,12},{4,8},{8,4},{12,0},{1,13},{5,9},{9,5},{13,1},{2,14},{6,10},... | collective-permute-start | bytes 884744 | tf_op jit(solution)/shard_map/gather/ppermute | solution.py:26
  7.3 7.3 %collective-permute-start.1 = (bf16[128,1152]{1,0:T(8,128)(2,1)S(1)}, bf16[128,1152]{1,0:T(8,128)(2,1)S(1)}, u32[]{:S(2)}, u32[]{:S(2)}) collective-permute-start(bf16[128,1152]{1,0:T(8,128)(2,1)S(1)} %get-tuple-element.46.t0), channel_id=1, source_target_pairs={{0,4},{4,0},{8,12},{12,8},{1,5},{5,1},{9,13},{13,9},{2,6},{6,2},{1... | collective-permute-start | bytes 884744 | tf_op jit(solution)/shard_map/gather/ppermute | solution.py:26
  8.6 0.8 %copy-start = (s32[1,16384]{1,0:T(1,128)S(1)}, s32[1,16384]{1,0:T(1,128)}, u32[]{:S(2)}) copy-start(s32[1,16384]{1,0:T(1,128)} %pair_ids.1) | copy-start | bytes 196612
  14.7 3.9 %collective-permute-start.3 = (bf16[256,1152]{1,0:T(8,128)(2,1)S(1)}, bf16[256,1152]{1,0:T(8,128)(2,1)S(1)}, u32[]{:S(2)}, u32[]{:S(2)}) collective-permute-start(bf16[256,1152]{1,0:T(8,128)(2,1)S(1)} %get-tuple-element.47.both), channel_id=1, source_target_pairs={{0,2},{2,0},{1,3},{3,1},{4,6},{6,4},{5,7},{7,5},{8,10},{10,8},{9,1... | collective-permute-start | bytes 1769480 | tf_op jit(solution)/shard_map/gather/ppermute | solution.py:26
  16.9 5.4 %collective-permute-start.4 = (bf16[64,1152]{1,0:T(8,128)(2,1)S(1)}, bf16[64,1152]{1,0:T(8,128)(2,1)S(1)}, u32[]{:S(2)}, u32[]{:S(2)}) collective-permute-start(bf16[64,1152]{1,0:T(8,128)(2,1)S(1)} %get-tuple-element.52), channel_id=1, source_target_pairs={{0,4},{4,0},{8,12},{12,8},{1,5},{5,1},{9,13},{13,9},{2,6},{6,2},{1... | collective-permute-start | bytes 442376 | tf_op jit(solution)/shard_map/gather/ppermute | solution.py:26
  16.9 6.3 %collective-permute-start.5 = (bf16[64,1152]{1,0:T(8,128)(2,1)S(1)}, bf16[64,1152]{1,0:T(8,128)(2,1)S(1)}, u32[]{:S(2)}, u32[]{:S(2)}) collective-permute-start(bf16[64,1152]{1,0:T(8,128)(2,1)S(1)} %get-tuple-element.53), channel_id=1, source_target_pairs={{0,12},{4,8},{8,4},{12,0},{1,13},{5,9},{9,5},{13,1},{2,14},{6,10},... | collective-permute-start | bytes 442376 | tf_op jit(solution)/shard_map/gather/ppermute | solution.py:26
  25.3 3.8 %collective-permute-start.6 = (bf16[512,1152]{1,0:T(8,128)(2,1)S(1)}, bf16[512,1152]{1,0:T(8,128)(2,1)S(1)}, u32[]{:S(2)}, u32[]{:S(2)}) collective-permute-start(bf16[512,1152]{1,0:T(8,128)(2,1)S(1)} %get-tuple-element.55), channel_id=1, source_target_pairs={{0,2},{2,0},{1,3},{3,1},{4,6},{6,4},{5,7},{7,5},{8,10},{10,8},{9,1... | collective-permute-start | bytes 3538952 | tf_op jit(solution)/shard_map/core/ppermute | solution.py:26
  27.5 10.4 %collective-permute-start.11 = (bf16[128,1152]{1,0:T(8,128)(2,1)S(1)}, bf16[128,1152]{1,0:T(8,128)(2,1)S(1)}, u32[]{:S(2)}, u32[]{:S(2)}) collective-permute-start(bf16[128,1152]{1,0:T(8,128)(2,1)S(1)} %get-tuple-element.65), channel_id=1, source_target_pairs={{0,8},{4,12},{8,0},{12,4},{1,9},{5,13},{9,1},{13,5},{2,10},{6,14},... | collective-permute-start | bytes 884744 | tf_op jit(solution)/shard_map/text/ppermute | solution.py:26
  30.1 16.3 %collective-permute-start.7 = (bf16[144,1152]{1,0:T(8,128)(2,1)S(1)}, bf16[144,1152]{1,0:T(8,128)(2,1)S(1)}, u32[]{:S(2)}, u32[]{:S(2)}) collective-permute-start(bf16[144,1152]{1,0:T(8,128)(2,1)S(1)} %get-tuple-element.61), channel_id=1, source_target_pairs={{0,32},{16,48},{32,0},{48,16},{1,33},{17,49},{33,1},{49,17},{2,34}... | collective-permute-start | bytes 995336 | tf_op jit(solution)/shard_map/weight/ppermute | solution.py:26
  32.6 14.6 %collective-permute-start.8 = (bf16[144,1152]{1,0:T(8,128)(2,1)S(1)}, bf16[144,1152]{1,0:T(8,128)(2,1)S(1)}, u32[]{:S(2)}, u32[]{:S(2)}) collective-permute-start(bf16[144,1152]{1,0:T(8,128)(2,1)S(1)} %get-tuple-element.62), channel_id=1, source_target_pairs={{0,16},{16,0},{32,48},{48,32},{1,17},{17,1},{33,49},{49,33},{2,18}... | collective-permute-start | bytes 995336 | tf_op jit(solution)/shard_map/weight/ppermute | solution.py:26
  32.6 15.9 %collective-permute-start.9 = (bf16[144,1152]{1,0:T(8,128)(2,1)S(1)}, bf16[144,1152]{1,0:T(8,128)(2,1)S(1)}, u32[]{:S(2)}, u32[]{:S(2)}) collective-permute-start(bf16[144,1152]{1,0:T(8,128)(2,1)S(1)} %get-tuple-element.63), channel_id=1, source_target_pairs={{0,48},{16,32},{32,16},{48,0},{1,49},{17,33},{33,17},{49,1},{2,50}... | collective-permute-start | bytes 995336 | tf_op jit(solution)/shard_map/weight/ppermute | solution.py:26
  33.4 9.2 %collective-permute-start.10 = (bf16[128,1152]{1,0:T(8,128)(2,1)S(1)}, bf16[128,1152]{1,0:T(8,128)(2,1)S(1)}, u32[]{:S(2)}, u32[]{:S(2)}) collective-permute-start(bf16[128,1152]{1,0:T(8,128)(2,1)S(1)} %get-tuple-element.64), channel_id=1, source_target_pairs={{0,4},{4,0},{8,12},{12,8},{1,5},{5,1},{9,13},{13,9},{2,6},{6,2},{1... | collective-permute-start | bytes 884744 | tf_op jit(solution)/shard_map/weight/ppermute | solution.py:26
  37.9 8.5 %collective-permute-start.12 = (bf16[128,1152]{1,0:T(8,128)(2,1)S(1)}, bf16[128,1152]{1,0:T(8,128)(2,1)S(1)}, u32[]{:S(2)}, u32[]{:S(2)}) collective-permute-start(bf16[128,1152]{1,0:T(8,128)(2,1)S(1)} %get-tuple-element.66), channel_id=1, source_target_pairs={{0,12},{4,8},{8,4},{12,0},{1,13},{5,9},{9,5},{13,1},{2,14},{6,10},... | collective-permute-start | bytes 884744 | tf_op jit(solution)/shard_map/weight/ppermute | solution.py:26
  48.8 5.3 %collective-permute-start.13 = (bf16[36,1152]{1,0:T(8,128)(2,1)S(1)}, bf16[36,1152]{1,0:T(8,128)(2,1)S(1)}, u32[]{:S(2)}, u32[]{:S(2)}) collective-permute-start(bf16[36,1152]{1,0:T(8,128)(2,1)S(1)} %get-tuple-element.68), channel_id=1, source_target_pairs={{0,8},{4,12},{8,0},{12,4},{1,9},{5,13},{9,1},{13,5},{2,10},{6,14},... | collective-permute-start | bytes 248840 | tf_op jit(solution)/shard_map/weight/ppermute | solution.py:26
  50.5 4.7 %collective-permute-start.14 = (bf16[36,1152]{1,0:T(8,128)(2,1)S(1)}, bf16[36,1152]{1,0:T(8,128)(2,1)S(1)}, u32[]{:S(2)}, u32[]{:S(2)}) collective-permute-start(bf16[36,1152]{1,0:T(8,128)(2,1)S(1)} %get-tuple-element.69), channel_id=1, source_target_pairs={{0,4},{4,0},{8,12},{12,8},{1,5},{5,1},{9,13},{13,9},{2,6},{6,2},{1... | collective-permute-start | bytes 248840 | tf_op jit(solution)/shard_map/weight/ppermute | solution.py:26
  50.8 5.6 %collective-permute-start.15 = (bf16[36,1152]{1,0:T(8,128)(2,1)S(1)}, bf16[36,1152]{1,0:T(8,128)(2,1)S(1)}, u32[]{:S(2)}, u32[]{:S(2)}) collective-permute-start(bf16[36,1152]{1,0:T(8,128)(2,1)S(1)} %get-tuple-element.70), channel_id=1, source_target_pairs={{0,12},{4,8},{8,4},{12,0},{1,13},{5,9},{9,5},{13,1},{2,14},{6,10},... | collective-permute-start | bytes 248840 | tf_op jit(solution)/shard_map/weight/ppermute | solution.py:26
  56.5 14.6 %collective-permute-start.16 = (bf16[128,1152]{1,0:T(8,128)(2,1)S(1)}, bf16[128,1152]{1,0:T(8,128)(2,1)S(1)}, u32[]{:S(2)}, u32[]{:S(2)}) collective-permute-start(bf16[128,1152]{1,0:T(8,128)(2,1)S(1)} %get-tuple-element.71), channel_id=1, source_target_pairs={{0,16},{16,0},{1,17},{17,1},{2,18},{18,2},{3,19},{19,3},{4,20},{20... | collective-permute-start | bytes 884744 | tf_op jit(solution)/shard_map/hidden/ppermute | solution.py:26
  56.9 3.4 %collective-permute-start.17 = (bf16[27,1152]{1,0:T(8,128)(2,1)S(1)}, bf16[27,1152]{1,0:T(8,128)(2,1)S(1)}, u32[]{:S(2)}, u32[]{:S(2)}) collective-permute-start(bf16[27,1152]{1,0:T(8,128)(2,1)S(1)} %get-tuple-element.75.after), channel_id=1, source_target_pairs={{0,1},{1,0},{2,3},{3,2},{4,5},{5,4},{6,7},{7,6},{8,9},{9,8},{10,11... | collective-permute-start | bytes 186632 | tf_op jit(solution)/shard_map/weight/ppermute | solution.py:26
  60.4 14.9 %collective-permute-start.20 = (bf16[9,1152]{1,0:T(8,128)(2,1)S(1)}, bf16[9,1152]{1,0:T(8,128)(2,1)S(1)}, u32[]{:S(2)}, u32[]{:S(2)}) collective-permute-start(bf16[9,1152]{1,0:T(8,128)(2,1)S(1)} %get-tuple-element.77), channel_id=1, source_target_pairs={{0,194},{2,192},{1,67},{3,65},{64,2},{66,0},{65,131},{67,129},{128... | collective-permute-start | bytes 62216 | tf_op jit(solution)/shard_map/weight/ppermute | solution.py:195
  69.5 5.8 %collective-permute-start.18 = (bf16[9,1152]{1,0:T(8,128)(2,1)S(1)}, bf16[9,1152]{1,0:T(8,128)(2,1)S(1)}, u32[]{:S(2)}, u32[]{:S(2)}) collective-permute-start(bf16[9,1152]{1,0:T(8,128)(2,1)S(1)} %get-tuple-element.77), channel_id=1, source_target_pairs={{0,195},{2,193},{1,66},{3,64},{64,3},{66,1},{65,130},{67,128},{128... | collective-permute-start | bytes 62216 | tf_op jit(solution)/shard_map/weight/ppermute | solution.py:195
  69.5 5.8 %collective-permute-start.19 = (bf16[9,1152]{1,0:T(8,128)(2,1)S(1)}, bf16[9,1152]{1,0:T(8,128)(2,1)S(1)}, u32[]{:S(2)}, u32[]{:S(2)}) collective-permute-start(bf16[9,1152]{1,0:T(8,128)(2,1)S(1)} %get-tuple-element.78), channel_id=1, source_target_pairs={{0,129},{2,131},{1,128},{3,130},{64,193},{66,195},{65,192},{67,194... | collective-permute-start | bytes 62216 | tf_op jit(solution)/shard_map/weight/ppermute | solution.py:195

commit v8 on v7

--- a/solution.py
+++ b/solution.py
@@ -110,14 +110,26 @@
     inverse[...] = inv
 
 
-def tile(settings, left, right, embed, normed, inverse, t0, t1, t2a, t2b, t3, coef_out, part_out, part_send):
-    txt = jnp.concatenate([t0[...], t1[...], t2a[...], t2b[...], t3[...]], 0)
+def coefficients(settings, left, right, embed, txt):
     scale, bias = settings[0:1, 0:1], settings[1:2, 0:1]
-    scores = scale * dot(embed[...], txt, 1, 1) + bias
-    target = jnp.where(left[...] == right[...], 1.0, -1.0).astype(f32)
-    coef = (-target * jax.nn.sigmoid(-target * scores) * scale).astype(bf16)
+    scores = scale * dot(embed, txt, 1, 1) + bias
+    target = jnp.where(left == right, 1.0, -1.0).astype(f32)
+    return (-target * jax.nn.sigmoid(-target * scores) * scale).astype(bf16)
+
+
+def near_tile(settings, left, right, embed, t0, t1, t3, coef_out, grad):
+    txt = jnp.concatenate([t0[...], t1[...], t3[...]], 0)
+    there = jnp.concatenate([right[:, : 2 * ROWS], right[:, 3 * ROWS :]], 1)
+    coef = coefficients(settings, left[...], there, embed[...], txt)
     coef_out[...] = coef
-    grad = dot(coef, txt, 1, 0)
+    grad[...] = dot(coef, txt, 1, 0)
+
+
+def far_tile(settings, left, right, embed, normed, inverse, t2a, t2b, near, coef_out, part_out, part_send):
+    txt = jnp.concatenate([t2a[...], t2b[...]], 0)
+    coef = coefficients(settings, left[...], right[:, 2 * ROWS : 3 * ROWS], embed[...], txt)
+    coef_out[...] = coef
+    grad = near[...] + dot(coef, txt, 1, 0)
     unit = normed[...]
     radial = jnp.sum(unit * grad, axis=1, keepdims=True)
     part = (grad - unit * radial) * inverse[...]
@@ -125,10 +137,11 @@
     part_send[...] = part.astype(bf16)
 
 
-def text_terms(coef, embed, terms, t2):
-    grad = dot(coef[...], embed[...], 0, 0)
-    terms[...] = grad
-    t2[...] = grad[2 * ROWS : 3 * ROWS].astype(bf16)
+def text_terms(near, far, embed, terms, t2):
+    grad = dot(near[...], embed[...], 0, 0)
+    terms[: 2 * ROWS, :] = grad[: 2 * ROWS]
+    terms[3 * ROWS :, :] = grad[2 * ROWS :]
+    t2[...] = dot(far[...], embed[...], 0, 0).astype(bf16)
 
 
 def weight_terms(part, arrived, turned, terms, rows, own, s1, s2, s3, t1, t3):
@@ -144,7 +157,7 @@
     t3[...] = terms[3 * ROWS :].astype(bf16)
 
 
-def first_sum(own, a2, a1, a3, b1, b2, b3, out, s1, s2, s3, held):
+def first_sum(own, a1, a3, a2, b1, b2, b3, out, s1, s2, s3, held):
     held[...] = own[...] + a2[...].astype(f32) + a1[...].astype(f32) + a3[...].astype(f32)
     out[...] = held[:36]
     for k, send in enumerate((s1, s2, s3)):
@@ -246,20 +259,21 @@
             vmem=16,
         )(both, hid_c, held, chosen)
     with jax.named_scope("tile"):
-        coef, part, part_send = call(
-            tile,
-            [shape(bf16, 512, 512), tall, shape(bf16, 512, WIDTH)],
-            [VMEM] * 11,
+        coef, grad = call(
+            near_tile, [shape(bf16, 512, 384), tall], [VMEM] * 7, 0, block, vmem=16
+        )(settings, left, right, embed, txt, txt_1, txt_3)
+        coef_2, part, part_send = call(
+            far_tile,
+            [shape(bf16, 512, ROWS), tall, shape(bf16, 512, WIDTH)],
+            [VMEM] * 9,
             0,
             block,
             vmem=16,
-        )(
-            settings, left, right, embed, normed, inverse, txt, txt_1, txt_2a, txt_2b, txt_3,
-        )
+        )(settings, left, right, embed, normed, inverse, txt_2a, txt_2b, grad)
     with jax.named_scope("core"):
         arrived = xor(part_send, "c", 1)
     with jax.named_scope("text"):
-        terms, u2 = call(text_terms, [tall, wide], [VMEM] * 2, 0, block)(coef, embed)
+        terms, u2 = call(text_terms, [tall, wide], [VMEM] * 3, 0, block)(coef, coef_2, embed)
         u2 = xor(u2, "y", 2)
     with jax.named_scope("weight"):
         rows, own, s1, s2, s3, u1, u3 = call(
@@ -282,7 +296,7 @@
             0,
             block,
             [pltpu.VMEM((144, WIDTH), f32)],
-        )(own, s2, s1, s3, u1, u2, u3)
+        )(own, s1, s3, s2, u1, u2, u3)
         s2, s1, s3 = xor(s2, "y", 2), xor(s1, "y", 1), xor(s3, "y", 3)
         whole, whole_send, rows_send = call(
             second_sum,

time: 76.2 us -> 75.2 us (0.987)
  waiting for transfers between devices: 26.8 us -> 24.5 us
  Pallas kernels: 13.4 us -> 14.8 us
    ppermute x18, waiting for transfers between devices: 24.3 us -> 22 us  [xor(): return lax.ppermute(x, axis, [(i, i ^ step) for i in range(size)])]
    pallas_call x2 -> x3, Pallas kernels: 2.98 us -> 4.37 us  [the longest x1 1.83 us: per_device(): call(far_tile, [shape(bf16, 512, ROWS), tall, shape(bf16, 512, WIDTH)], [...]
  transfers between devices with their start and end apart: 21 -> 21, of which waited for: 16 -> 14; matrix products, arithmetic and copies ran while one was open for 0% -> 0% of each run, Pallas kernels for 12% -> 14%
where the time goes in v8:
time: 75.2 us; the launch traced here: 75 us
  starting transfers between devices  32.2 us (43%)
  waiting for transfers between devices  24.5 us (33%)
  Pallas kernels  14.8 us (20%)
  between operations  2.69 us (4%)
  local copies, waits for them, and re-layouts  0.83 us (1%)
    ppermute x18, waiting for transfers between devices, xor(): return lax.ppermute(x, axis, [(i, i ^ step) for i in range(size)])  22 us
    ppermute x18, starting transfers between devices, xor(): return lax.ppermute(x, axis, [(i, i ^ step) for i in range(size)])  21.4 us
    ppermute x3, starting transfers between devices, along_z(): return lax.ppermute(x, ('zh', 'c', 'zl'), pairs)  10.8 us
    pallas_call x1, Pallas kernels, per_device(): call(project, [shape(bf16, 512, WIDTH), tall, shape(f32, 512, 1), shape(b...  2.7 us
    ppermute x3, waiting for transfers between devices, along_z(): return lax.ppermute(x, ('zh', 'c', 'zl'), pairs)  2.54 us
    pallas_call x1, Pallas kernels, per_device(): call(far_tile, [shape(bf16, 512, ROWS), tall, shape(bf16, 512, WIDTH)], [...  1.83 us
    pallas_call x1, Pallas kernels, per_device(): call(ahead, [shape(bf16, WIDTH, WIDTH), shape(bf16, 576, WIDTH), shape(jn...  1.78 us
    pallas_call x1, Pallas kernels, per_device(): call(near_tile, [shape(bf16, 512, 384), tall], [VMEM] * 7, 0, block, vmem...  1.66 us
  transfers between devices with their start and end apart: 21, of which 14 were waited for; matrix products, arithmetic and copies ran while one was open for 0% of the time, Pallas kernels for 14%

profile of v8, /device:TPU:1, one launch (start us, length us, event | category | flops | bytes accessed | tf_op | source)
XLA Modules:
  0.0 75.0 jit_solution(8271762690935686872)
XLA Ops:
  2.5 2.1 %collective-permute-start = (bf16[128,1152]{1,0:T(8,128)(2,1)S(1)}, bf16[128,1152]{1,0:T(8,128)(2,1)S(1)}, u32[]{:S(2)}, u32[]{:S(2)}) collective-permute-start(bf16[128,1152]{1,0:T(8,128)(2,1)S(1)} %get-tuple-element.43.after.own), channel_id=1, source_target_pairs={{0,16},{16,0},{1,17},{17,1},{2,18},{18,2},{3,19},{19,3},{4,20},{20... | collective-permute-start | bytes 884744 | tf_op jit(solution)/shard_map/gather/ppermute | solution.py:26
  4.6 2.7 %collective-permute-start.2 = (bf16[128,1152]{1,0:T(8,128)(2,1)S(1)}, bf16[128,1152]{1,0:T(8,128)(2,1)S(1)}, u32[]{:S(2)}, u32[]{:S(2)}) collective-permute-start(bf16[128,1152]{1,0:T(8,128)(2,1)S(1)} %get-tuple-element.48.t0), channel_id=1, source_target_pairs={{0,12},{4,8},{8,4},{12,0},{1,13},{5,9},{9,5},{13,1},{2,14},{6,10},... | collective-permute-start | bytes 884744 | tf_op jit(solution)/shard_map/gather/ppermute | solution.py:26
  9.5 1.8 %gather.2 = (bf16[1152,1152]{1,0:T(8,128)(2,1)S(1)}, bf16[576,1152]{1,0:T(8,128)(2,1)S(1)}, s32[512,1]{1,0:T(8,128)S(1)}, s32[1,512]{1,0:T(1,128)S(1)}, f32[2,128]{1,0:T(2,128)S(1)}) custom-call(bf16[128,1152]{1,0:T(8,128)(2,1)S(1)} %get-tuple-element.43.after.own, f32[1]{0:T(128)} %bitcast.2.scale, f32[1]{0:T(128)} %bitcast.3.bias, s32[1,16384]{1,0:T(1,128)S(1)} %copy-done, ...), custom_call_target="tpu_custom_call" | custom-call | flops 147456000 | bytes 147456 | tf_op jit(solution)/shard_map/gather/pallas_call | solution.py:228
  11.3 1.9 %collective-permute-done.2.t3 = bf16[128,1152]{1,0:T(8,128)(2,1)S(1)} collective-permute-done((bf16[128,1152]{1,0:T(8,128)(2,1)S(1)}, bf16[128,1152]{1,0:T(8,128)(2,1)S(1)}, u32[]{:S(2)}, u32[]{:S(2)}) %collective-permute-start.2) | collective-permute-done | bytes 294944 | tf_op jit(solution)/shard_map/gather/ppermute | solution.py:26
  13.1 1.5 %collective-permute-done.1.t1 = bf16[128,1152]{1,0:T(8,128)(2,1)S(1)} collective-permute-done((bf16[128,1152]{1,0:T(8,128)(2,1)S(1)}, bf16[128,1152]{1,0:T(8,128)(2,1)S(1)}, u32[]{:S(2)}, u32[]{:S(2)}) %collective-permute-start.1) | collective-permute-done | bytes 294944 | tf_op jit(solution)/shard_map/gather/ppermute | solution.py:26
  14.7 2.2 %collective-permute-start.3 = (bf16[256,1152]{1,0:T(8,128)(2,1)S(1)}, bf16[256,1152]{1,0:T(8,128)(2,1)S(1)}, u32[]{:S(2)}, u32[]{:S(2)}) collective-permute-start(bf16[256,1152]{1,0:T(8,128)(2,1)S(1)} %get-tuple-element.49.both), channel_id=1, source_target_pairs={{0,2},{2,0},{1,3},{3,1},{4,6},{6,4},{5,7},{7,5},{8,10},{10,8},{9,1... | collective-permute-start | bytes 1769480 | tf_op jit(solution)/shard_map/gather/ppermute | solution.py:26
  18.5 2.7 %project.1 = (bf16[512,1152]{1,0:T(8,128)(2,1)S(1)}, f32[512,1152]{1,0:T(8,128)S(1)}, f32[512,1]{1,0:T(8,128)S(1)}, bf16[576,512]{1,0:T(8,128)(2,1)S(1)}) custom-call(bf16[256,1152]{1,0:T(8,128)(2,1)S(1)} %get-tuple-element.49.both, bf16[256,1152]{1,0:T(8,128)(2,1)S(1)} %collective-permute-done.3.cores, bf16[1152,1152]{1,0:T(8,128)(2,1)S(1)} %get-tuple-element.50.weight, ...), custom_call_target="tpu_custom_call" | custom-call | bytes 147456 | tf_op jit(solution)/shard_map/project/pallas_call | solution.py:253
  21.3 1.7 %tile.2 = (bf16[512,384]{1,0:T(8,128)(2,1)S(1)}, f32[512,1152]{1,0:T(8,128)S(1)}) custom-call(f32[2,128]{1,0:T(2,128)S(1)} %get-tuple-element.44.settings, s32[512,1]{1,0:T(8,128)S(1)} %get-tuple-element.45.left, s32[1,512]{1,0:T(1,128)S(1)} %get-tuple-element.46.right, bf16[512,1152]{1,0:T(8,128)(2,1)S(1)} %get-tuple-element.51.embed, ...), custom_call_target="tpu_custom_call" | custom-call | bytes 147456 | tf_op jit(solution)/shard_map/tile/pallas_call | solution.py:262
  23.2 1.8 %tile.3 = (bf16[512,128]{1,0:T(8,128)(2,1)S(1)}, f32[512,1152]{1,0:T(8,128)S(1)}, bf16[512,1152]{1,0:T(8,128)(2,1)S(1)}) custom-call(f32[2,128]{1,0:T(2,128)S(1)} %get-tuple-element.44.settings, s32[512,1]{1,0:T(8,128)S(1)} %get-tuple-element.45.left, s32[1,512]{1,0:T(1,128)S(1)} %get-tuple-element.46.right, bf16[512,1152]{1,0:T(8,128)(2,1)S(1)} %get-tuple-element.51.embed, ...), custom_call_target="tpu_custom_call" | custom-call | bytes 147456 | tf_op jit(solution)/shard_map/tile/pallas_call | solution.py:265
  25.1 1.3 %collective-permute-start.6 = (bf16[512,1152]{1,0:T(8,128)(2,1)S(1)}, bf16[512,1152]{1,0:T(8,128)(2,1)S(1)}, u32[]{:S(2)}, u32[]{:S(2)}) collective-permute-start(bf16[512,1152]{1,0:T(8,128)(2,1)S(1)} %get-tuple-element.58), channel_id=1, source_target_pairs={{0,2},{2,0},{1,3},{3,1},{4,6},{6,4},{5,7},{7,5},{8,10},{10,8},{9,1... | collective-permute-start | bytes 3538952 | tf_op jit(solution)/shard_map/core/ppermute | solution.py:26
  27.2 1.5 %collective-permute-start.11 = (bf16[128,1152]{1,0:T(8,128)(2,1)S(1)}, bf16[128,1152]{1,0:T(8,128)(2,1)S(1)}, u32[]{:S(2)}, u32[]{:S(2)}) collective-permute-start(bf16[128,1152]{1,0:T(8,128)(2,1)S(1)} %get-tuple-element.69), channel_id=1, source_target_pairs={{0,8},{4,12},{8,0},{12,4},{1,9},{5,13},{9,1},{13,5},{2,10},{6,14},... | collective-permute-start | bytes 884744 | tf_op jit(solution)/shard_map/text/ppermute | solution.py:26
  30.1 2.5 %collective-permute-start.8 = (bf16[144,1152]{1,0:T(8,128)(2,1)S(1)}, bf16[144,1152]{1,0:T(8,128)(2,1)S(1)}, u32[]{:S(2)}, u32[]{:S(2)}) collective-permute-start(bf16[144,1152]{1,0:T(8,128)(2,1)S(1)} %get-tuple-element.66), channel_id=1, source_target_pairs={{0,48},{16,32},{32,16},{48,0},{1,49},{17,33},{33,17},{49,1},{2,50}... | collective-permute-start | bytes 995336 | tf_op jit(solution)/shard_map/weight/ppermute | solution.py:26
  33.6 4.0 %collective-permute-done.11.b2 = bf16[128,1152]{1,0:T(8,128)(2,1)S(1)} collective-permute-done((bf16[128,1152]{1,0:T(8,128)(2,1)S(1)}, bf16[128,1152]{1,0:T(8,128)(2,1)S(1)}, u32[]{:S(2)}, u32[]{:S(2)}) %collective-permute-start.11) | collective-permute-done | bytes 294944 | tf_op jit(solution)/shard_map/text/ppermute | solution.py:26
  38.8 3.6 %collective-permute-done.10.b1 = bf16[128,1152]{1,0:T(8,128)(2,1)S(1)} collective-permute-done((bf16[128,1152]{1,0:T(8,128)(2,1)S(1)}, bf16[128,1152]{1,0:T(8,128)(2,1)S(1)}, u32[]{:S(2)}, u32[]{:S(2)}) %collective-permute-start.10) | collective-permute-done | bytes 294944 | tf_op jit(solution)/shard_map/weight/ppermute | solution.py:26
  42.4 3.8 %collective-permute-done.12.b3 = bf16[128,1152]{1,0:T(8,128)(2,1)S(1)} collective-permute-done((bf16[128,1152]{1,0:T(8,128)(2,1)S(1)}, bf16[128,1152]{1,0:T(8,128)(2,1)S(1)}, u32[]{:S(2)}, u32[]{:S(2)}) %collective-permute-start.12) | collective-permute-done | bytes 294944 | tf_op jit(solution)/shard_map/weight/ppermute | solution.py:26
  46.2 1.4 %collective-permute-done.9.a2 = bf16[144,1152]{1,0:T(8,128)(2,1)S(1)} collective-permute-done((bf16[144,1152]{1,0:T(8,128)(2,1)S(1)}, bf16[144,1152]{1,0:T(8,128)(2,1)S(1)}, u32[]{:S(2)}, u32[]{:S(2)}) %collective-permute-start.9) | collective-permute-done | bytes 331808 | tf_op jit(solution)/shard_map/weight/ppermute | solution.py:26
  47.8 1.8 %collective-permute-start.13 = (bf16[36,1152]{1,0:T(8,128)(2,1)S(1)}, bf16[36,1152]{1,0:T(8,128)(2,1)S(1)}, u32[]{:S(2)}, u32[]{:S(2)}) collective-permute-start(bf16[36,1152]{1,0:T(8,128)(2,1)S(1)} %get-tuple-element.72), channel_id=1, source_target_pairs={{0,8},{4,12},{8,0},{12,4},{1,9},{5,13},{9,1},{13,5},{2,10},{6,14},... | collective-permute-start | bytes 248840 | tf_op jit(solution)/shard_map/weight/ppermute | solution.py:26
  51.2 1.7 %collective-permute-done.13.a2 = bf16[36,1152]{1,0:T(8,128)(2,1)S(1)} collective-permute-done((bf16[36,1152]{1,0:T(8,128)(2,1)S(1)}, bf16[36,1152]{1,0:T(8,128)(2,1)S(1)}, u32[]{:S(2)}, u32[]{:S(2)}) %collective-permute-start.13) | collective-permute-done | bytes 82976 | tf_op jit(solution)/shard_map/weight/ppermute | solution.py:26
  54.1 1.4 %collective-permute-done.15.a3 = bf16[36,1152]{1,0:T(8,128)(2,1)S(1)} collective-permute-done((bf16[36,1152]{1,0:T(8,128)(2,1)S(1)}, bf16[36,1152]{1,0:T(8,128)(2,1)S(1)}, u32[]{:S(2)}, u32[]{:S(2)}) %collective-permute-start.15) | collective-permute-done | bytes 82976 | tf_op jit(solution)/shard_map/weight/ppermute | solution.py:26
  56.0 1.6 %collective-permute-start.17 = (bf16[27,1152]{1,0:T(8,128)(2,1)S(1)}, bf16[27,1152]{1,0:T(8,128)(2,1)S(1)}, u32[]{:S(2)}, u32[]{:S(2)}) collective-permute-start(bf16[27,1152]{1,0:T(8,128)(2,1)S(1)} %get-tuple-element.79.after), channel_id=1, source_target_pairs={{0,1},{1,0},{2,3},{3,2},{4,5},{5,4},{6,7},{7,6},{8,9},{9,8},{10,11... | collective-permute-start | bytes 186632 | tf_op jit(solution)/shard_map/weight/ppermute | solution.py:26
  59.4 9.1 %collective-permute-start.20 = (bf16[9,1152]{1,0:T(8,128)(2,1)S(1)}, bf16[9,1152]{1,0:T(8,128)(2,1)S(1)}, u32[]{:S(2)}, u32[]{:S(2)}) collective-permute-start(bf16[9,1152]{1,0:T(8,128)(2,1)S(1)} %get-tuple-element.81), channel_id=1, source_target_pairs={{0,194},{2,192},{1,67},{3,65},{64,2},{66,0},{65,131},{67,129},{128... | collective-permute-start | bytes 62216 | tf_op jit(solution)/shard_map/weight/ppermute | solution.py:208
  68.5 1.6 %collective-permute-start.19 = (bf16[9,1152]{1,0:T(8,128)(2,1)S(1)}, bf16[9,1152]{1,0:T(8,128)(2,1)S(1)}, u32[]{:S(2)}, u32[]{:S(2)}) collective-permute-start(bf16[9,1152]{1,0:T(8,128)(2,1)S(1)} %get-tuple-element.82), channel_id=1, source_target_pairs={{0,129},{2,131},{1,128},{3,130},{64,193},{66,195},{65,192},{67,194... | collective-permute-start | bytes 62216 | tf_op jit(solution)/shard_map/weight/ppermute | solution.py:208
  70.2 1.6 %hidden.3 = (bf16[128,1152]{1,0:T(8,128)(2,1)}, f32[8,128]{1,0:T(8,128)S(1)}) custom-call(s32[1]{0:T(128)S(6)} %copy.10.count, f32[256,1152]{1,0:T(8,128)S(1)} %get-tuple-element.63.rows, bf16[128,1152]{1,0:T(8,128)(2,1)S(1)} %collective-permute-done.16.arrived, bf16[1152,1152]{1,0:T(8,128)(2,1)S(1)} %get-tuple-element.50.weight), custom_call_target="tpu_custom_call" | custom-call | flops 339738624 | bytes 2654208 | tf_op jit(solution)/shard_map/hidden/pallas_call | solution.py:321
  71.8 2.5 %collective-permute-done.19.a3 = bf16[9,1152]{1,0:T(8,128)(2,1)S(1)} collective-permute-done((bf16[9,1152]{1,0:T(8,128)(2,1)S(1)}, bf16[9,1152]{1,0:T(8,128)(2,1)S(1)}, u32[]{:S(2)}, u32[]{:S(2)}) %collective-permute-start.19) | collective-permute-done | bytes 20768 | tf_op jit(solution)/shard_map/weight/ppermute | solution.py:208
  (34 shorter events, 14.5 us)
Async XLA Ops:
  2.5 8.8 %collective-permute-start = (bf16[128,1152]{1,0:T(8,128)(2,1)S(1)}, bf16[128,1152]{1,0:T(8,128)(2,1)S(1)}, u32[]{:S(2)}, u32[]{:S(2)}) collective-permute-start(bf16[128,1152]{1,0:T(8,128)(2,1)S(1)} %get-tuple-element.43.after.own), channel_id=1, source_target_pairs={{0,16},{16,0},{1,17},{17,1},{2,18},{18,2},{3,19},{19,3},{4,20},{20... | collective-permute-start | bytes 884744 | tf_op jit(solution)/shard_map/gather/ppermute | solution.py:26
  4.6 8.5 %collective-permute-start.2 = (bf16[128,1152]{1,0:T(8,128)(2,1)S(1)}, bf16[128,1152]{1,0:T(8,128)(2,1)S(1)}, u32[]{:S(2)}, u32[]{:S(2)}) collective-permute-start(bf16[128,1152]{1,0:T(8,128)(2,1)S(1)} %get-tuple-element.48.t0), channel_id=1, source_target_pairs={{0,12},{4,8},{8,4},{12,0},{1,13},{5,9},{9,5},{13,1},{2,14},{6,10},... | collective-permute-start | bytes 884744 | tf_op jit(solution)/shard_map/gather/ppermute | solution.py:26
  7.3 7.3 %collective-permute-start.1 = (bf16[128,1152]{1,0:T(8,128)(2,1)S(1)}, bf16[128,1152]{1,0:T(8,128)(2,1)S(1)}, u32[]{:S(2)}, u32[]{:S(2)}) collective-permute-start(bf16[128,1152]{1,0:T(8,128)(2,1)S(1)} %get-tuple-element.48.t0), channel_id=1, source_target_pairs={{0,4},{4,0},{8,12},{12,8},{1,5},{5,1},{9,13},{13,9},{2,6},{6,2},{1... | collective-permute-start | bytes 884744 | tf_op jit(solution)/shard_map/gather/ppermute | solution.py:26
  8.6 0.8 %copy-start = (s32[1,16384]{1,0:T(1,128)S(1)}, s32[1,16384]{1,0:T(1,128)}, u32[]{:S(2)}) copy-start(s32[1,16384]{1,0:T(1,128)} %pair_ids.1) | copy-start | bytes 196612
  14.7 3.9 %collective-permute-start.3 = (bf16[256,1152]{1,0:T(8,128)(2,1)S(1)}, bf16[256,1152]{1,0:T(8,128)(2,1)S(1)}, u32[]{:S(2)}, u32[]{:S(2)}) collective-permute-start(bf16[256,1152]{1,0:T(8,128)(2,1)S(1)} %get-tuple-element.49.both), channel_id=1, source_target_pairs={{0,2},{2,0},{1,3},{3,1},{4,6},{6,4},{5,7},{7,5},{8,10},{10,8},{9,1... | collective-permute-start | bytes 1769480 | tf_op jit(solution)/shard_map/gather/ppermute | solution.py:26
  16.9 6.0 %collective-permute-start.4 = (bf16[64,1152]{1,0:T(8,128)(2,1)S(1)}, bf16[64,1152]{1,0:T(8,128)(2,1)S(1)}, u32[]{:S(2)}, u32[]{:S(2)}) collective-permute-start(bf16[64,1152]{1,0:T(8,128)(2,1)S(1)} %get-tuple-element.54), channel_id=1, source_target_pairs={{0,4},{4,0},{8,12},{12,8},{1,5},{5,1},{9,13},{13,9},{2,6},{6,2},{1... | collective-permute-start | bytes 442376 | tf_op jit(solution)/shard_map/gather/ppermute | solution.py:26
  16.9 6.3 %collective-permute-start.5 = (bf16[64,1152]{1,0:T(8,128)(2,1)S(1)}, bf16[64,1152]{1,0:T(8,128)(2,1)S(1)}, u32[]{:S(2)}, u32[]{:S(2)}) collective-permute-start(bf16[64,1152]{1,0:T(8,128)(2,1)S(1)} %get-tuple-element.55), channel_id=1, source_target_pairs={{0,12},{4,8},{8,4},{12,0},{1,13},{5,9},{9,5},{13,1},{2,14},{6,10},... | collective-permute-start | bytes 442376 | tf_op jit(solution)/shard_map/gather/ppermute | solution.py:26
  25.1 3.8 %collective-permute-start.6 = (bf16[512,1152]{1,0:T(8,128)(2,1)S(1)}, bf16[512,1152]{1,0:T(8,128)(2,1)S(1)}, u32[]{:S(2)}, u32[]{:S(2)}) collective-permute-start(bf16[512,1152]{1,0:T(8,128)(2,1)S(1)} %get-tuple-element.58), channel_id=1, source_target_pairs={{0,2},{2,0},{1,3},{3,1},{4,6},{6,4},{5,7},{7,5},{8,10},{10,8},{9,1... | collective-permute-start | bytes 3538952 | tf_op jit(solution)/shard_map/core/ppermute | solution.py:26
  27.2 10.4 %collective-permute-start.11 = (bf16[128,1152]{1,0:T(8,128)(2,1)S(1)}, bf16[128,1152]{1,0:T(8,128)(2,1)S(1)}, u32[]{:S(2)}, u32[]{:S(2)}) collective-permute-start(bf16[128,1152]{1,0:T(8,128)(2,1)S(1)} %get-tuple-element.69), channel_id=1, source_target_pairs={{0,8},{4,12},{8,0},{12,4},{1,9},{5,13},{9,1},{13,5},{2,10},{6,14},... | collective-permute-start | bytes 884744 | tf_op jit(solution)/shard_map/text/ppermute | solution.py:26
  29.8 16.3 %collective-permute-start.7 = (bf16[144,1152]{1,0:T(8,128)(2,1)S(1)}, bf16[144,1152]{1,0:T(8,128)(2,1)S(1)}, u32[]{:S(2)}, u32[]{:S(2)}) collective-permute-start(bf16[144,1152]{1,0:T(8,128)(2,1)S(1)} %get-tuple-element.65), channel_id=1, source_target_pairs={{0,16},{16,0},{32,48},{48,32},{1,17},{17,1},{33,49},{49,33},{2,18}... | collective-permute-start | bytes 995336 | tf_op jit(solution)/shard_map/weight/ppermute | solution.py:26
  30.1 16.0 %collective-permute-start.8 = (bf16[144,1152]{1,0:T(8,128)(2,1)S(1)}, bf16[144,1152]{1,0:T(8,128)(2,1)S(1)}, u32[]{:S(2)}, u32[]{:S(2)}) collective-permute-start(bf16[144,1152]{1,0:T(8,128)(2,1)S(1)} %get-tuple-element.66), channel_id=1, source_target_pairs={{0,48},{16,32},{32,16},{48,0},{1,49},{17,33},{33,17},{49,1},{2,50}... | collective-permute-start | bytes 995336 | tf_op jit(solution)/shard_map/weight/ppermute | solution.py:26
  32.6 14.9 %collective-permute-start.9 = (bf16[144,1152]{1,0:T(8,128)(2,1)S(1)}, bf16[144,1152]{1,0:T(8,128)(2,1)S(1)}, u32[]{:S(2)}, u32[]{:S(2)}) collective-permute-start(bf16[144,1152]{1,0:T(8,128)(2,1)S(1)} %get-tuple-element.67), channel_id=1, source_target_pairs={{0,32},{16,48},{32,0},{48,16},{1,33},{17,49},{33,1},{49,17},{2,34}... | collective-permute-start | bytes 995336 | tf_op jit(solution)/shard_map/weight/ppermute | solution.py:26
  33.1 9.2 %collective-permute-start.10 = (bf16[128,1152]{1,0:T(8,128)(2,1)S(1)}, bf16[128,1152]{1,0:T(8,128)(2,1)S(1)}, u32[]{:S(2)}, u32[]{:S(2)}) collective-permute-start(bf16[128,1152]{1,0:T(8,128)(2,1)S(1)} %get-tuple-element.68), channel_id=1, source_target_pairs={{0,4},{4,0},{8,12},{12,8},{1,5},{5,1},{9,13},{13,9},{2,6},{6,2},{1... | collective-permute-start | bytes 884744 | tf_op jit(solution)/shard_map/weight/ppermute | solution.py:26
  37.6 8.5 %collective-permute-start.12 = (bf16[128,1152]{1,0:T(8,128)(2,1)S(1)}, bf16[128,1152]{1,0:T(8,128)(2,1)S(1)}, u32[]{:S(2)}, u32[]{:S(2)}) collective-permute-start(bf16[128,1152]{1,0:T(8,128)(2,1)S(1)} %get-tuple-element.70), channel_id=1, source_target_pairs={{0,12},{4,8},{8,4},{12,0},{1,13},{5,9},{9,5},{13,1},{2,14},{6,10},... | collective-permute-start | bytes 884744 | tf_op jit(solution)/shard_map/weight/ppermute | solution.py:26
  47.8 5.0 %collective-permute-start.13 = (bf16[36,1152]{1,0:T(8,128)(2,1)S(1)}, bf16[36,1152]{1,0:T(8,128)(2,1)S(1)}, u32[]{:S(2)}, u32[]{:S(2)}) collective-permute-start(bf16[36,1152]{1,0:T(8,128)(2,1)S(1)} %get-tuple-element.72), channel_id=1, source_target_pairs={{0,8},{4,12},{8,0},{12,4},{1,9},{5,13},{9,1},{13,5},{2,10},{6,14},... | collective-permute-start | bytes 248840 | tf_op jit(solution)/shard_map/weight/ppermute | solution.py:26
  49.7 4.4 %collective-permute-start.14 = (bf16[36,1152]{1,0:T(8,128)(2,1)S(1)}, bf16[36,1152]{1,0:T(8,128)(2,1)S(1)}, u32[]{:S(2)}, u32[]{:S(2)}) collective-permute-start(bf16[36,1152]{1,0:T(8,128)(2,1)S(1)} %get-tuple-element.73), channel_id=1, source_target_pairs={{0,4},{4,0},{8,12},{12,8},{1,5},{5,1},{9,13},{13,9},{2,6},{6,2},{1... | collective-permute-start | bytes 248840 | tf_op jit(solution)/shard_map/weight/ppermute | solution.py:26
  49.9 5.6 %collective-permute-start.15 = (bf16[36,1152]{1,0:T(8,128)(2,1)S(1)}, bf16[36,1152]{1,0:T(8,128)(2,1)S(1)}, u32[]{:S(2)}, u32[]{:S(2)}) collective-permute-start(bf16[36,1152]{1,0:T(8,128)(2,1)S(1)} %get-tuple-element.74), channel_id=1, source_target_pairs={{0,12},{4,8},{8,4},{12,0},{1,13},{5,9},{9,5},{13,1},{2,14},{6,10},... | collective-permute-start | bytes 248840 | tf_op jit(solution)/shard_map/weight/ppermute | solution.py:26
  55.6 14.6 %collective-permute-start.16 = (bf16[128,1152]{1,0:T(8,128)(2,1)S(1)}, bf16[128,1152]{1,0:T(8,128)(2,1)S(1)}, u32[]{:S(2)}, u32[]{:S(2)}) collective-permute-start(bf16[128,1152]{1,0:T(8,128)(2,1)S(1)} %get-tuple-element.75), channel_id=1, source_target_pairs={{0,16},{16,0},{1,17},{17,1},{2,18},{18,2},{3,19},{19,3},{4,20},{20... | collective-permute-start | bytes 884744 | tf_op jit(solution)/shard_map/hidden/ppermute | solution.py:26
  56.0 3.4 %collective-permute-start.17 = (bf16[27,1152]{1,0:T(8,128)(2,1)S(1)}, bf16[27,1152]{1,0:T(8,128)(2,1)S(1)}, u32[]{:S(2)}, u32[]{:S(2)}) collective-permute-start(bf16[27,1152]{1,0:T(8,128)(2,1)S(1)} %get-tuple-element.79.after), channel_id=1, source_target_pairs={{0,1},{1,0},{2,3},{3,2},{4,5},{5,4},{6,7},{7,6},{8,9},{9,8},{10,11... | collective-permute-start | bytes 186632 | tf_op jit(solution)/shard_map/weight/ppermute | solution.py:26
  59.4 14.9 %collective-permute-start.20 = (bf16[9,1152]{1,0:T(8,128)(2,1)S(1)}, bf16[9,1152]{1,0:T(8,128)(2,1)S(1)}, u32[]{:S(2)}, u32[]{:S(2)}) collective-permute-start(bf16[9,1152]{1,0:T(8,128)(2,1)S(1)} %get-tuple-element.81), channel_id=1, source_target_pairs={{0,194},{2,192},{1,67},{3,65},{64,2},{66,0},{65,131},{67,129},{128... | collective-permute-start | bytes 62216 | tf_op jit(solution)/shard_map/weight/ppermute | solution.py:208
  68.5 5.8 %collective-permute-start.18 = (bf16[9,1152]{1,0:T(8,128)(2,1)S(1)}, bf16[9,1152]{1,0:T(8,128)(2,1)S(1)}, u32[]{:S(2)}, u32[]{:S(2)}) collective-permute-start(bf16[9,1152]{1,0:T(8,128)(2,1)S(1)} %get-tuple-element.81), channel_id=1, source_target_pairs={{0,195},{2,193},{1,66},{3,64},{64,3},{66,1},{65,130},{67,128},{128... | collective-permute-start | bytes 62216 | tf_op jit(solution)/shard_map/weight/ppermute | solution.py:208
  68.5 5.8 %collective-permute-start.19 = (bf16[9,1152]{1,0:T(8,128)(2,1)S(1)}, bf16[9,1152]{1,0:T(8,128)(2,1)S(1)}, u32[]{:S(2)}, u32[]{:S(2)}) collective-permute-start(bf16[9,1152]{1,0:T(8,128)(2,1)S(1)} %get-tuple-element.82), channel_id=1, source_target_pairs={{0,129},{2,131},{1,128},{3,130},{64,193},{66,195},{65,192},{67,194... | collective-permute-start | bytes 62216 | tf_op jit(solution)/shard_map/weight/ppermute | solution.py:208

commit v9 on v8

--- a/solution.py
+++ b/solution.py
@@ -11,6 +11,7 @@
 bf16 = jnp.bfloat16
 ROWS = 128
 WIDTH = 1152
+CUT = 80
 VMEM = pl.BlockSpec(memory_space=pltpu.VMEM)
 SMEM = pl.BlockSpec(memory_space=pltpu.SMEM)
 ANY = pl.BlockSpec(memory_space=pl.ANY)
@@ -65,8 +66,8 @@
 def join(after, own, paired, t1, t3, both, first, second):
     both[:ROWS] = own[...]
     both[ROWS:] = paired[...]
-    first[...] = t3[: ROWS // 2]
-    second[...] = t1[ROWS // 2 :]
+    first[...] = t3[:CUT]
+    second[...] = t1[CUT:]
 
 
 def ahead(after, scale, bias, pair_ids, weight, held, chosen, left, right, settings, sem):
@@ -241,7 +242,7 @@
         )(hid, logit_scale.reshape(1), logit_bias.reshape(1), pair_ids, in_hbm(weight))
         both, first, second = call(
             join,
-            [shape(bf16, 256, WIDTH)] + [shape(bf16, 64, WIDTH)] * 2,
+            [shape(bf16, 256, WIDTH), shape(bf16, CUT, WIDTH), shape(bf16, ROWS - CUT, WIDTH)],
             [ANY] + [VMEM] * 4,
             0,
             block,

time: 75.2 us -> 74.7 us (level)
  no operation moved by 1% of the time
where the time goes in v9:
time: 74.7 us; the launch traced here: 74.5 us
  starting transfers between devices  32 us (43%)
  waiting for transfers between devices  24.1 us (32%)
  Pallas kernels  14.8 us (20%)
  between operations  2.69 us (4%)
  local copies, waits for them, and re-layouts  0.83 us (1%)
    ppermute x18, waiting for transfers between devices, xor(): return lax.ppermute(x, axis, [(i, i ^ step) for i in range(size)])  21.6 us
    ppermute x18, starting transfers between devices, xor(): return lax.ppermute(x, axis, [(i, i ^ step) for i in range(size)])  21.2 us
    ppermute x3, starting transfers between devices, along_z(): return lax.ppermute(x, ('zh', 'c', 'zl'), pairs)  10.8 us
    pallas_call x1, Pallas kernels, per_device(): call(project, [shape(bf16, 512, WIDTH), tall, shape(f32, 512, 1), shape(b...  2.7 us
    ppermute x3, waiting for transfers between devices, along_z(): return lax.ppermute(x, ('zh', 'c', 'zl'), pairs)  2.54 us
    pallas_call x1, Pallas kernels, per_device(): call(far_tile, [shape(bf16, 512, ROWS), tall, shape(bf16, 512, WIDTH)], [...  1.82 us
    pallas_call x1, Pallas kernels, per_device(): call(ahead, [shape(bf16, WIDTH, WIDTH), shape(bf16, 576, WIDTH), shape(jn...  1.78 us
    pallas_call x1, Pallas kernels, per_device(): call(near_tile, [shape(bf16, 512, 384), tall], [VMEM] * 7, 0, block, vmem...  1.66 us
  transfers between devices with their start and end apart: 21, of which 14 were waited for; matrix products, arithmetic and copies ran while one was open for 0% of the time, Pallas kernels for 14%

profile of v9, /device:TPU:1, one launch (start us, length us, event | category | flops | bytes accessed | tf_op | source)
XLA Modules:
  0.0 74.5 jit_solution(2301257511832285858)
XLA Ops:
  2.5 2.1 %collective-permute-start = (bf16[128,1152]{1,0:T(8,128)(2,1)S(1)}, bf16[128,1152]{1,0:T(8,128)(2,1)S(1)}, u32[]{:S(2)}, u32[]{:S(2)}) collective-permute-start(bf16[128,1152]{1,0:T(8,128)(2,1)S(1)} %get-tuple-element.43.after.own), channel_id=1, source_target_pairs={{0,16},{16,0},{1,17},{17,1},{2,18},{18,2},{3,19},{19,3},{4,20},{20... | collective-permute-start | bytes 884744 | tf_op jit(solution)/shard_map/gather/ppermute | solution.py:27
  4.6 2.7 %collective-permute-start.2 = (bf16[128,1152]{1,0:T(8,128)(2,1)S(1)}, bf16[128,1152]{1,0:T(8,128)(2,1)S(1)}, u32[]{:S(2)}, u32[]{:S(2)}) collective-permute-start(bf16[128,1152]{1,0:T(8,128)(2,1)S(1)} %get-tuple-element.48.t0), channel_id=1, source_target_pairs={{0,12},{4,8},{8,4},{12,0},{1,13},{5,9},{9,5},{13,1},{2,14},{6,10},... | collective-permute-start | bytes 884744 | tf_op jit(solution)/shard_map/gather/ppermute | solution.py:27
  9.5 1.8 %gather.2 = (bf16[1152,1152]{1,0:T(8,128)(2,1)S(1)}, bf16[576,1152]{1,0:T(8,128)(2,1)S(1)}, s32[512,1]{1,0:T(8,128)S(1)}, s32[1,512]{1,0:T(1,128)S(1)}, f32[2,128]{1,0:T(2,128)S(1)}) custom-call(bf16[128,1152]{1,0:T(8,128)(2,1)S(1)} %get-tuple-element.43.after.own, f32[1]{0:T(128)} %bitcast.2.scale, f32[1]{0:T(128)} %bitcast.3.bias, s32[1,16384]{1,0:T(1,128)S(1)} %copy-done, ...), custom_call_target="tpu_custom_call" | custom-call | flops 147456000 | bytes 147456 | tf_op jit(solution)/shard_map/gather/pallas_call | solution.py:229
  11.3 1.9 %collective-permute-done.2.t3 = bf16[128,1152]{1,0:T(8,128)(2,1)S(1)} collective-permute-done((bf16[128,1152]{1,0:T(8,128)(2,1)S(1)}, bf16[128,1152]{1,0:T(8,128)(2,1)S(1)}, u32[]{:S(2)}, u32[]{:S(2)}) %collective-permute-start.2) | collective-permute-done | bytes 294944 | tf_op jit(solution)/shard_map/gather/ppermute | solution.py:27
  13.1 1.5 %collective-permute-done.1.t1 = bf16[128,1152]{1,0:T(8,128)(2,1)S(1)} collective-permute-done((bf16[128,1152]{1,0:T(8,128)(2,1)S(1)}, bf16[128,1152]{1,0:T(8,128)(2,1)S(1)}, u32[]{:S(2)}, u32[]{:S(2)}) %collective-permute-start.1) | collective-permute-done | bytes 294944 | tf_op jit(solution)/shard_map/gather/ppermute | solution.py:27
  14.7 2.2 %collective-permute-start.3 = (bf16[256,1152]{1,0:T(8,128)(2,1)S(1)}, bf16[256,1152]{1,0:T(8,128)(2,1)S(1)}, u32[]{:S(2)}, u32[]{:S(2)}) collective-permute-start(bf16[256,1152]{1,0:T(8,128)(2,1)S(1)} %get-tuple-element.49.both), channel_id=1, source_target_pairs={{0,2},{2,0},{1,3},{3,1},{4,6},{6,4},{5,7},{7,5},{8,10},{10,8},{9,1... | collective-permute-start | bytes 1769480 | tf_op jit(solution)/shard_map/gather/ppermute | solution.py:27
  18.5 2.7 %project.1 = (bf16[512,1152]{1,0:T(8,128)(2,1)S(1)}, f32[512,1152]{1,0:T(8,128)S(1)}, f32[512,1]{1,0:T(8,128)S(1)}, bf16[576,512]{1,0:T(8,128)(2,1)S(1)}) custom-call(bf16[256,1152]{1,0:T(8,128)(2,1)S(1)} %get-tuple-element.49.both, bf16[256,1152]{1,0:T(8,128)(2,1)S(1)} %collective-permute-done.3.cores, bf16[1152,1152]{1,0:T(8,128)(2,1)S(1)} %get-tuple-element.50.weight, ...), custom_call_target="tpu_custom_call" | custom-call | bytes 147456 | tf_op jit(solution)/shard_map/project/pallas_call | solution.py:254
  21.3 1.7 %tile.2 = (bf16[512,384]{1,0:T(8,128)(2,1)S(1)}, f32[512,1152]{1,0:T(8,128)S(1)}) custom-call(f32[2,128]{1,0:T(2,128)S(1)} %get-tuple-element.44.settings, s32[512,1]{1,0:T(8,128)S(1)} %get-tuple-element.45.left, s32[1,512]{1,0:T(1,128)S(1)} %get-tuple-element.46.right, bf16[512,1152]{1,0:T(8,128)(2,1)S(1)} %get-tuple-element.51.embed, ...), custom_call_target="tpu_custom_call" | custom-call | bytes 147456 | tf_op jit(solution)/shard_map/tile/pallas_call | solution.py:263
  23.1 1.8 %tile.3 = (bf16[512,128]{1,0:T(8,128)(2,1)S(1)}, f32[512,1152]{1,0:T(8,128)S(1)}, bf16[512,1152]{1,0:T(8,128)(2,1)S(1)}) custom-call(f32[2,128]{1,0:T(2,128)S(1)} %get-tuple-element.44.settings, s32[512,1]{1,0:T(8,128)S(1)} %get-tuple-element.45.left, s32[1,512]{1,0:T(1,128)S(1)} %get-tuple-element.46.right, bf16[512,1152]{1,0:T(8,128)(2,1)S(1)} %get-tuple-element.51.embed, ...), custom_call_target="tpu_custom_call" | custom-call | bytes 147456 | tf_op jit(solution)/shard_map/tile/pallas_call | solution.py:266
  26.8 1.5 %collective-permute-start.11 = (bf16[128,1152]{1,0:T(8,128)(2,1)S(1)}, bf16[128,1152]{1,0:T(8,128)(2,1)S(1)}, u32[]{:S(2)}, u32[]{:S(2)}) collective-permute-start(bf16[128,1152]{1,0:T(8,128)(2,1)S(1)} %get-tuple-element.69), channel_id=1, source_target_pairs={{0,8},{4,12},{8,0},{12,4},{1,9},{5,13},{9,1},{13,5},{2,10},{6,14},... | collective-permute-start | bytes 884744 | tf_op jit(solution)/shard_map/text/ppermute | solution.py:27
  29.7 2.5 %collective-permute-start.8 = (bf16[144,1152]{1,0:T(8,128)(2,1)S(1)}, bf16[144,1152]{1,0:T(8,128)(2,1)S(1)}, u32[]{:S(2)}, u32[]{:S(2)}) collective-permute-start(bf16[144,1152]{1,0:T(8,128)(2,1)S(1)} %get-tuple-element.66), channel_id=1, source_target_pairs={{0,48},{16,32},{32,16},{48,0},{1,49},{17,33},{33,17},{49,1},{2,50}... | collective-permute-start | bytes 995336 | tf_op jit(solution)/shard_map/weight/ppermute | solution.py:27
  33.2 4.0 %collective-permute-done.11.b2 = bf16[128,1152]{1,0:T(8,128)(2,1)S(1)} collective-permute-done((bf16[128,1152]{1,0:T(8,128)(2,1)S(1)}, bf16[128,1152]{1,0:T(8,128)(2,1)S(1)}, u32[]{:S(2)}, u32[]{:S(2)}) %collective-permute-start.11) | collective-permute-done | bytes 294944 | tf_op jit(solution)/shard_map/text/ppermute | solution.py:27
  38.4 3.6 %collective-permute-done.10.b1 = bf16[128,1152]{1,0:T(8,128)(2,1)S(1)} collective-permute-done((bf16[128,1152]{1,0:T(8,128)(2,1)S(1)}, bf16[128,1152]{1,0:T(8,128)(2,1)S(1)}, u32[]{:S(2)}, u32[]{:S(2)}) %collective-permute-start.10) | collective-permute-done | bytes 294944 | tf_op jit(solution)/shard_map/weight/ppermute | solution.py:27
  42.0 3.7 %collective-permute-done.12.b3 = bf16[128,1152]{1,0:T(8,128)(2,1)S(1)} collective-permute-done((bf16[128,1152]{1,0:T(8,128)(2,1)S(1)}, bf16[128,1152]{1,0:T(8,128)(2,1)S(1)}, u32[]{:S(2)}, u32[]{:S(2)}) %collective-permute-start.12) | collective-permute-done | bytes 294944 | tf_op jit(solution)/shard_map/weight/ppermute | solution.py:27
  45.7 1.4 %collective-permute-done.9.a2 = bf16[144,1152]{1,0:T(8,128)(2,1)S(1)} collective-permute-done((bf16[144,1152]{1,0:T(8,128)(2,1)S(1)}, bf16[144,1152]{1,0:T(8,128)(2,1)S(1)}, u32[]{:S(2)}, u32[]{:S(2)}) %collective-permute-start.9) | collective-permute-done | bytes 331808 | tf_op jit(solution)/shard_map/weight/ppermute | solution.py:27
  47.4 1.8 %collective-permute-start.13 = (bf16[36,1152]{1,0:T(8,128)(2,1)S(1)}, bf16[36,1152]{1,0:T(8,128)(2,1)S(1)}, u32[]{:S(2)}, u32[]{:S(2)}) collective-permute-start(bf16[36,1152]{1,0:T(8,128)(2,1)S(1)} %get-tuple-element.72), channel_id=1, source_target_pairs={{0,8},{4,12},{8,0},{12,4},{1,9},{5,13},{9,1},{13,5},{2,10},{6,14},... | collective-permute-start | bytes 248840 | tf_op jit(solution)/shard_map/weight/ppermute | solution.py:27
  49.3 1.5 %collective-permute-start.15 = (bf16[36,1152]{1,0:T(8,128)(2,1)S(1)}, bf16[36,1152]{1,0:T(8,128)(2,1)S(1)}, u32[]{:S(2)}, u32[]{:S(2)}) collective-permute-start(bf16[36,1152]{1,0:T(8,128)(2,1)S(1)} %get-tuple-element.74), channel_id=1, source_target_pairs={{0,12},{4,8},{8,4},{12,0},{1,13},{5,9},{9,5},{13,1},{2,14},{6,10},... | collective-permute-start | bytes 248840 | tf_op jit(solution)/shard_map/weight/ppermute | solution.py:27
  50.7 1.7 %collective-permute-done.13.a2 = bf16[36,1152]{1,0:T(8,128)(2,1)S(1)} collective-permute-done((bf16[36,1152]{1,0:T(8,128)(2,1)S(1)}, bf16[36,1152]{1,0:T(8,128)(2,1)S(1)}, u32[]{:S(2)}, u32[]{:S(2)}) %collective-permute-start.13) | collective-permute-done | bytes 82976 | tf_op jit(solution)/shard_map/weight/ppermute | solution.py:27
  52.4 1.3 %collective-permute-done.14.a1 = bf16[36,1152]{1,0:T(8,128)(2,1)S(1)} collective-permute-done((bf16[36,1152]{1,0:T(8,128)(2,1)S(1)}, bf16[36,1152]{1,0:T(8,128)(2,1)S(1)}, u32[]{:S(2)}, u32[]{:S(2)}) %collective-permute-start.14) | collective-permute-done | bytes 82976 | tf_op jit(solution)/shard_map/weight/ppermute | solution.py:27
  55.4 1.6 %collective-permute-start.17 = (bf16[27,1152]{1,0:T(8,128)(2,1)S(1)}, bf16[27,1152]{1,0:T(8,128)(2,1)S(1)}, u32[]{:S(2)}, u32[]{:S(2)}) collective-permute-start(bf16[27,1152]{1,0:T(8,128)(2,1)S(1)} %get-tuple-element.79.after), channel_id=1, source_target_pairs={{0,1},{1,0},{2,3},{3,2},{4,5},{5,4},{6,7},{7,6},{8,9},{9,8},{10,11... | collective-permute-start | bytes 186632 | tf_op jit(solution)/shard_map/weight/ppermute | solution.py:27
  58.8 9.2 %collective-permute-start.20 = (bf16[9,1152]{1,0:T(8,128)(2,1)S(1)}, bf16[9,1152]{1,0:T(8,128)(2,1)S(1)}, u32[]{:S(2)}, u32[]{:S(2)}) collective-permute-start(bf16[9,1152]{1,0:T(8,128)(2,1)S(1)} %get-tuple-element.81), channel_id=1, source_target_pairs={{0,194},{2,192},{1,67},{3,65},{64,2},{66,0},{65,131},{67,129},{128... | collective-permute-start | bytes 62216 | tf_op jit(solution)/shard_map/weight/ppermute | solution.py:209
  68.0 1.6 %collective-permute-start.19 = (bf16[9,1152]{1,0:T(8,128)(2,1)S(1)}, bf16[9,1152]{1,0:T(8,128)(2,1)S(1)}, u32[]{:S(2)}, u32[]{:S(2)}) collective-permute-start(bf16[9,1152]{1,0:T(8,128)(2,1)S(1)} %get-tuple-element.82), channel_id=1, source_target_pairs={{0,129},{2,131},{1,128},{3,130},{64,193},{66,195},{65,192},{67,194... | collective-permute-start | bytes 62216 | tf_op jit(solution)/shard_map/weight/ppermute | solution.py:209
  69.6 1.6 %hidden.3 = (bf16[128,1152]{1,0:T(8,128)(2,1)}, f32[8,128]{1,0:T(8,128)S(1)}) custom-call(s32[1]{0:T(128)S(6)} %copy.10.count, f32[256,1152]{1,0:T(8,128)S(1)} %get-tuple-element.63.rows, bf16[128,1152]{1,0:T(8,128)(2,1)S(1)} %collective-permute-done.16.arrived, bf16[1152,1152]{1,0:T(8,128)(2,1)S(1)} %get-tuple-element.50.weight), custom_call_target="tpu_custom_call" | custom-call | flops 339738624 | bytes 2654208 | tf_op jit(solution)/shard_map/hidden/pallas_call | solution.py:322
  71.3 2.5 %collective-permute-done.19.a3 = bf16[9,1152]{1,0:T(8,128)(2,1)S(1)} collective-permute-done((bf16[9,1152]{1,0:T(8,128)(2,1)S(1)}, bf16[9,1152]{1,0:T(8,128)(2,1)S(1)}, u32[]{:S(2)}, u32[]{:S(2)}) %collective-permute-start.19) | collective-permute-done | bytes 20768 | tf_op jit(solution)/shard_map/weight/ppermute | solution.py:209
  (34 shorter events, 13.9 us)
Async XLA Ops:
  2.5 8.8 %collective-permute-start = (bf16[128,1152]{1,0:T(8,128)(2,1)S(1)}, bf16[128,1152]{1,0:T(8,128)(2,1)S(1)}, u32[]{:S(2)}, u32[]{:S(2)}) collective-permute-start(bf16[128,1152]{1,0:T(8,128)(2,1)S(1)} %get-tuple-element.43.after.own), channel_id=1, source_target_pairs={{0,16},{16,0},{1,17},{17,1},{2,18},{18,2},{3,19},{19,3},{4,20},{20... | collective-permute-start | bytes 884744 | tf_op jit(solution)/shard_map/gather/ppermute | solution.py:27
  4.6 8.5 %collective-permute-start.2 = (bf16[128,1152]{1,0:T(8,128)(2,1)S(1)}, bf16[128,1152]{1,0:T(8,128)(2,1)S(1)}, u32[]{:S(2)}, u32[]{:S(2)}) collective-permute-start(bf16[128,1152]{1,0:T(8,128)(2,1)S(1)} %get-tuple-element.48.t0), channel_id=1, source_target_pairs={{0,12},{4,8},{8,4},{12,0},{1,13},{5,9},{9,5},{13,1},{2,14},{6,10},... | collective-permute-start | bytes 884744 | tf_op jit(solution)/shard_map/gather/ppermute | solution.py:27
  7.3 7.3 %collective-permute-start.1 = (bf16[128,1152]{1,0:T(8,128)(2,1)S(1)}, bf16[128,1152]{1,0:T(8,128)(2,1)S(1)}, u32[]{:S(2)}, u32[]{:S(2)}) collective-permute-start(bf16[128,1152]{1,0:T(8,128)(2,1)S(1)} %get-tuple-element.48.t0), channel_id=1, source_target_pairs={{0,4},{4,0},{8,12},{12,8},{1,5},{5,1},{9,13},{13,9},{2,6},{6,2},{1... | collective-permute-start | bytes 884744 | tf_op jit(solution)/shard_map/gather/ppermute | solution.py:27
  8.6 0.8 %copy-start = (s32[1,16384]{1,0:T(1,128)S(1)}, s32[1,16384]{1,0:T(1,128)}, u32[]{:S(2)}) copy-start(s32[1,16384]{1,0:T(1,128)} %pair_ids.1) | copy-start | bytes 196612
  14.7 3.9 %collective-permute-start.3 = (bf16[256,1152]{1,0:T(8,128)(2,1)S(1)}, bf16[256,1152]{1,0:T(8,128)(2,1)S(1)}, u32[]{:S(2)}, u32[]{:S(2)}) collective-permute-start(bf16[256,1152]{1,0:T(8,128)(2,1)S(1)} %get-tuple-element.49.both), channel_id=1, source_target_pairs={{0,2},{2,0},{1,3},{3,1},{4,6},{6,4},{5,7},{7,5},{8,10},{10,8},{9,1... | collective-permute-start | bytes 1769480 | tf_op jit(solution)/shard_map/gather/ppermute | solution.py:27
  16.9 6.2 %collective-permute-start.4 = (bf16[80,1152]{1,0:T(8,128)(2,1)S(1)}, bf16[80,1152]{1,0:T(8,128)(2,1)S(1)}, u32[]{:S(2)}, u32[]{:S(2)}) collective-permute-start(bf16[80,1152]{1,0:T(8,128)(2,1)S(1)} %get-tuple-element.54), channel_id=1, source_target_pairs={{0,4},{4,0},{8,12},{12,8},{1,5},{5,1},{9,13},{13,9},{2,6},{6,2},{1... | collective-permute-start | bytes 552968 | tf_op jit(solution)/shard_map/gather/ppermute | solution.py:27
  16.9 6.0 %collective-permute-start.5 = (bf16[48,1152]{1,0:T(8,128)(2,1)S(1)}, bf16[48,1152]{1,0:T(8,128)(2,1)S(1)}, u32[]{:S(2)}, u32[]{:S(2)}) collective-permute-start(bf16[48,1152]{1,0:T(8,128)(2,1)S(1)} %get-tuple-element.55), channel_id=1, source_target_pairs={{0,12},{4,8},{8,4},{12,0},{1,13},{5,9},{9,5},{13,1},{2,14},{6,10},... | collective-permute-start | bytes 331784 | tf_op jit(solution)/shard_map/gather/ppermute | solution.py:27
  24.9 3.4 %collective-permute-start.6 = (bf16[512,1152]{1,0:T(8,128)(2,1)S(1)}, bf16[512,1152]{1,0:T(8,128)(2,1)S(1)}, u32[]{:S(2)}, u32[]{:S(2)}) collective-permute-start(bf16[512,1152]{1,0:T(8,128)(2,1)S(1)} %get-tuple-element.58), channel_id=1, source_target_pairs={{0,2},{2,0},{1,3},{3,1},{4,6},{6,4},{5,7},{7,5},{8,10},{10,8},{9,1... | collective-permute-start | bytes 3538952 | tf_op jit(solution)/shard_map/core/ppermute | solution.py:27
  26.8 10.4 %collective-permute-start.11 = (bf16[128,1152]{1,0:T(8,128)(2,1)S(1)}, bf16[128,1152]{1,0:T(8,128)(2,1)S(1)}, u32[]{:S(2)}, u32[]{:S(2)}) collective-permute-start(bf16[128,1152]{1,0:T(8,128)(2,1)S(1)} %get-tuple-element.69), channel_id=1, source_target_pairs={{0,8},{4,12},{8,0},{12,4},{1,9},{5,13},{9,1},{13,5},{2,10},{6,14},... | collective-permute-start | bytes 884744 | tf_op jit(solution)/shard_map/text/ppermute | solution.py:27
  29.4 16.3 %collective-permute-start.7 = (bf16[144,1152]{1,0:T(8,128)(2,1)S(1)}, bf16[144,1152]{1,0:T(8,128)(2,1)S(1)}, u32[]{:S(2)}, u32[]{:S(2)}) collective-permute-start(bf16[144,1152]{1,0:T(8,128)(2,1)S(1)} %get-tuple-element.65), channel_id=1, source_target_pairs={{0,16},{16,0},{32,48},{48,32},{1,17},{17,1},{33,49},{49,33},{2,18}... | collective-permute-start | bytes 995336 | tf_op jit(solution)/shard_map/weight/ppermute | solution.py:27
  29.7 16.0 %collective-permute-start.8 = (bf16[144,1152]{1,0:T(8,128)(2,1)S(1)}, bf16[144,1152]{1,0:T(8,128)(2,1)S(1)}, u32[]{:S(2)}, u32[]{:S(2)}) collective-permute-start(bf16[144,1152]{1,0:T(8,128)(2,1)S(1)} %get-tuple-element.66), channel_id=1, source_target_pairs={{0,48},{16,32},{32,16},{48,0},{1,49},{17,33},{33,17},{49,1},{2,50}... | collective-permute-start | bytes 995336 | tf_op jit(solution)/shard_map/weight/ppermute | solution.py:27
  32.2 14.9 %collective-permute-start.9 = (bf16[144,1152]{1,0:T(8,128)(2,1)S(1)}, bf16[144,1152]{1,0:T(8,128)(2,1)S(1)}, u32[]{:S(2)}, u32[]{:S(2)}) collective-permute-start(bf16[144,1152]{1,0:T(8,128)(2,1)S(1)} %get-tuple-element.67), channel_id=1, source_target_pairs={{0,32},{16,48},{32,0},{48,16},{1,33},{17,49},{33,1},{49,17},{2,34}... | collective-permute-start | bytes 995336 | tf_op jit(solution)/shard_map/weight/ppermute | solution.py:27
  32.7 9.3 %collective-permute-start.10 = (bf16[128,1152]{1,0:T(8,128)(2,1)S(1)}, bf16[128,1152]{1,0:T(8,128)(2,1)S(1)}, u32[]{:S(2)}, u32[]{:S(2)}) collective-permute-start(bf16[128,1152]{1,0:T(8,128)(2,1)S(1)} %get-tuple-element.68), channel_id=1, source_target_pairs={{0,4},{4,0},{8,12},{12,8},{1,5},{5,1},{9,13},{13,9},{2,6},{6,2},{1... | collective-permute-start | bytes 884744 | tf_op jit(solution)/shard_map/weight/ppermute | solution.py:27
  37.2 8.5 %collective-permute-start.12 = (bf16[128,1152]{1,0:T(8,128)(2,1)S(1)}, bf16[128,1152]{1,0:T(8,128)(2,1)S(1)}, u32[]{:S(2)}, u32[]{:S(2)}) collective-permute-start(bf16[128,1152]{1,0:T(8,128)(2,1)S(1)} %get-tuple-element.70), channel_id=1, source_target_pairs={{0,12},{4,8},{8,4},{12,0},{1,13},{5,9},{9,5},{13,1},{2,14},{6,10},... | collective-permute-start | bytes 884744 | tf_op jit(solution)/shard_map/weight/ppermute | solution.py:27
  47.4 5.0 %collective-permute-start.13 = (bf16[36,1152]{1,0:T(8,128)(2,1)S(1)}, bf16[36,1152]{1,0:T(8,128)(2,1)S(1)}, u32[]{:S(2)}, u32[]{:S(2)}) collective-permute-start(bf16[36,1152]{1,0:T(8,128)(2,1)S(1)} %get-tuple-element.72), channel_id=1, source_target_pairs={{0,8},{4,12},{8,0},{12,4},{1,9},{5,13},{9,1},{13,5},{2,10},{6,14},... | collective-permute-start | bytes 248840 | tf_op jit(solution)/shard_map/weight/ppermute | solution.py:27
  49.2 4.4 %collective-permute-start.14 = (bf16[36,1152]{1,0:T(8,128)(2,1)S(1)}, bf16[36,1152]{1,0:T(8,128)(2,1)S(1)}, u32[]{:S(2)}, u32[]{:S(2)}) collective-permute-start(bf16[36,1152]{1,0:T(8,128)(2,1)S(1)} %get-tuple-element.73), channel_id=1, source_target_pairs={{0,4},{4,0},{8,12},{12,8},{1,5},{5,1},{9,13},{13,9},{2,6},{6,2},{1... | collective-permute-start | bytes 248840 | tf_op jit(solution)/shard_map/weight/ppermute | solution.py:27
  49.3 5.6 %collective-permute-start.15 = (bf16[36,1152]{1,0:T(8,128)(2,1)S(1)}, bf16[36,1152]{1,0:T(8,128)(2,1)S(1)}, u32[]{:S(2)}, u32[]{:S(2)}) collective-permute-start(bf16[36,1152]{1,0:T(8,128)(2,1)S(1)} %get-tuple-element.74), channel_id=1, source_target_pairs={{0,12},{4,8},{8,4},{12,0},{1,13},{5,9},{9,5},{13,1},{2,14},{6,10},... | collective-permute-start | bytes 248840 | tf_op jit(solution)/shard_map/weight/ppermute | solution.py:27
  55.0 14.6 %collective-permute-start.16 = (bf16[128,1152]{1,0:T(8,128)(2,1)S(1)}, bf16[128,1152]{1,0:T(8,128)(2,1)S(1)}, u32[]{:S(2)}, u32[]{:S(2)}) collective-permute-start(bf16[128,1152]{1,0:T(8,128)(2,1)S(1)} %get-tuple-element.75), channel_id=1, source_target_pairs={{0,16},{16,0},{1,17},{17,1},{2,18},{18,2},{3,19},{19,3},{4,20},{20... | collective-permute-start | bytes 884744 | tf_op jit(solution)/shard_map/hidden/ppermute | solution.py:27
  55.4 3.4 %collective-permute-start.17 = (bf16[27,1152]{1,0:T(8,128)(2,1)S(1)}, bf16[27,1152]{1,0:T(8,128)(2,1)S(1)}, u32[]{:S(2)}, u32[]{:S(2)}) collective-permute-start(bf16[27,1152]{1,0:T(8,128)(2,1)S(1)} %get-tuple-element.79.after), channel_id=1, source_target_pairs={{0,1},{1,0},{2,3},{3,2},{4,5},{5,4},{6,7},{7,6},{8,9},{9,8},{10,11... | collective-permute-start | bytes 186632 | tf_op jit(solution)/shard_map/weight/ppermute | solution.py:27
  58.8 15.0 %collective-permute-start.20 = (bf16[9,1152]{1,0:T(8,128)(2,1)S(1)}, bf16[9,1152]{1,0:T(8,128)(2,1)S(1)}, u32[]{:S(2)}, u32[]{:S(2)}) collective-permute-start(bf16[9,1152]{1,0:T(8,128)(2,1)S(1)} %get-tuple-element.81), channel_id=1, source_target_pairs={{0,194},{2,192},{1,67},{3,65},{64,2},{66,0},{65,131},{67,129},{128... | collective-permute-start | bytes 62216 | tf_op jit(solution)/shard_map/weight/ppermute | solution.py:209
  68.0 5.8 %collective-permute-start.18 = (bf16[9,1152]{1,0:T(8,128)(2,1)S(1)}, bf16[9,1152]{1,0:T(8,128)(2,1)S(1)}, u32[]{:S(2)}, u32[]{:S(2)}) collective-permute-start(bf16[9,1152]{1,0:T(8,128)(2,1)S(1)} %get-tuple-element.81), channel_id=1, source_target_pairs={{0,195},{2,193},{1,66},{3,64},{64,3},{66,1},{65,130},{67,128},{128... | collective-permute-start | bytes 62216 | tf_op jit(solution)/shard_map/weight/ppermute | solution.py:209
  68.0 5.8 %collective-permute-start.19 = (bf16[9,1152]{1,0:T(8,128)(2,1)S(1)}, bf16[9,1152]{1,0:T(8,128)(2,1)S(1)}, u32[]{:S(2)}, u32[]{:S(2)}) collective-permute-start(bf16[9,1152]{1,0:T(8,128)(2,1)S(1)} %get-tuple-element.82), channel_id=1, source_target_pairs={{0,129},{2,131},{1,128},{3,130},{64,193},{66,195},{65,192},{67,194... | collective-permute-start | bytes 62216 | tf_op jit(solution)/shard_map/weight/ppermute | solution.py:209

commit v10 on v9

--- a/solution.py
+++ b/solution.py
@@ -138,14 +138,18 @@
     part_send[...] = part.astype(bf16)
 
 
-def text_terms(near, far, embed, terms, t2):
+def far_text(far, embed, t2):
+    t2[...] = dot(far[...], embed[...], 0, 0).astype(bf16)
+
+
+def near_text(after, near, embed, own, t1, t3):
     grad = dot(near[...], embed[...], 0, 0)
-    terms[: 2 * ROWS, :] = grad[: 2 * ROWS]
-    terms[3 * ROWS :, :] = grad[2 * ROWS :]
-    t2[...] = dot(far[...], embed[...], 0, 0).astype(bf16)
-
-
-def weight_terms(part, arrived, turned, terms, rows, own, s1, s2, s3, t1, t3):
+    own[...] = grad[:ROWS]
+    t1[...] = grad[ROWS : 2 * ROWS].astype(bf16)
+    t3[...] = grad[2 * ROWS :].astype(bf16)
+
+
+def weight_terms(part, arrived, turned, rows, own, s1, s2, s3):
     half = 2 * ROWS
     top = part[:half] + arrived[half:].astype(f32)
     low = part[half:] + arrived[:half].astype(f32)
@@ -154,8 +158,6 @@
     own[...] = grad[:144]
     for k, out in enumerate((s1, s2, s3)):
         out[...] = grad[(k + 1) * 144 : (k + 2) * 144].astype(bf16)
-    t1[...] = terms[ROWS : 2 * ROWS].astype(bf16)
-    t3[...] = terms[3 * ROWS :].astype(bf16)
 
 
 def first_sum(own, a1, a3, a2, b1, b2, b3, out, s1, s2, s3, held):
@@ -188,7 +190,7 @@
 
 def text_sum(after, count, terms, b1, b2, b3, out):
     keep = lax.broadcasted_iota(jnp.int32, (ROWS, 1), 0) < count[0]
-    total = terms[:ROWS] + b2[...].astype(f32) + b1[...].astype(f32) + b3[...].astype(f32)
+    total = terms[...] + b2[...].astype(f32) + b1[...].astype(f32) + b3[...].astype(f32)
     out[...] = jnp.where(keep, total, 0.0)
 
 
@@ -274,20 +276,22 @@
     with jax.named_scope("core"):
         arrived = xor(part_send, "c", 1)
     with jax.named_scope("text"):
-        terms, u2 = call(text_terms, [tall, wide], [VMEM] * 3, 0, block)(coef, coef_2, embed)
+        (u2,) = call(far_text, [wide], [VMEM] * 2, 0, block)(coef_2, embed)
         u2 = xor(u2, "y", 2)
     with jax.named_scope("weight"):
-        rows, own, s1, s2, s3, u1, u3 = call(
+        rows, own, s1, s2, s3 = call(
             weight_terms,
             [shape(f32, 256, WIDTH), shape(f32, 144, WIDTH)]
-            + [shape(bf16, 144, WIDTH)] * 3
-            + [wide] * 2,
-            [VMEM] * 4,
+            + [shape(bf16, 144, WIDTH)] * 3,
+            [VMEM] * 3,
             0,
             block,
             vmem=16,
-        )(part, arrived, turned, terms)
+        )(part, arrived, turned)
         s2, s1, s3 = xor(s2, X, 2), xor(s1, X, 1), xor(s3, X, 3)
+        terms, u1, u3 = call(
+            near_text, [shape(f32, ROWS, WIDTH), wide, wide], [ANY] + [VMEM] * 2, 0, block
+        )(own, coef, embed)
         u1, u3 = xor(u1, "y", 1), xor(u3, "y", 3)
         small, small_b = shape(f32, 36, WIDTH), shape(bf16, 36, WIDTH)
         whole, s1, s2, s3 = call(

time: 74.7 us -> 74.7 us (level)
  transfers between devices with their start and end apart: 21 -> 21, of which waited for: 14 -> 13; matrix products, arithmetic and copies ran while one was open for 0% -> 0% of each run, Pallas kernels for 14% -> 15%
where the time goes in v10:
time: 74.7 us; the launch traced here: 74.5 us
  starting transfers between devices  31.7 us (42%)
  waiting for transfers between devices  24.2 us (32%)
  Pallas kernels  15 us (20%)
  between operations  2.69 us (4%)
  local copies, waits for them, and re-layouts  0.83 us (1%)
    ppermute x18, waiting for transfers between devices, xor(): return lax.ppermute(x, axis, [(i, i ^ step) for i in range(size)])  21.7 us
    ppermute x18, starting transfers between devices, xor(): return lax.ppermute(x, axis, [(i, i ^ step) for i in range(size)])  20.9 us
    ppermute x3, starting transfers between devices, along_z(): return lax.ppermute(x, ('zh', 'c', 'zl'), pairs)  10.8 us
    pallas_call x1, Pallas kernels, per_device(): call(project, [shape(bf16, 512, WIDTH), tall, shape(f32, 512, 1), shape(b...  2.72 us
    ppermute x3, waiting for transfers between devices, along_z(): return lax.ppermute(x, ('zh', 'c', 'zl'), pairs)  2.54 us
    pallas_call x1, Pallas kernels, per_device(): call(far_tile, [shape(bf16, 512, ROWS), tall, shape(bf16, 512, WIDTH)], [...  1.83 us
    pallas_call x1, Pallas kernels, per_device(): call(ahead, [shape(bf16, WIDTH, WIDTH), shape(bf16, 576, WIDTH), shape(jn...  1.78 us
    pallas_call x1, Pallas kernels, per_device(): call(near_tile, [shape(bf16, 512, 384), tall], [VMEM] * 7, 0, block, vmem...  1.67 us
  transfers between devices with their start and end apart: 21, of which 13 were waited for; matrix products, arithmetic and copies ran while one was open for 0% of the time, Pallas kernels for 15%

profile of v10, /device:TPU:1, one launch (start us, length us, event | category | flops | bytes accessed | tf_op | source)
XLA Modules:
  0.0 74.5 jit_solution(15354486083572082551)
XLA Ops:
  2.5 2.1 %collective-permute-start = (bf16[128,1152]{1,0:T(8,128)(2,1)S(1)}, bf16[128,1152]{1,0:T(8,128)(2,1)S(1)}, u32[]{:S(2)}, u32[]{:S(2)}) collective-permute-start(bf16[128,1152]{1,0:T(8,128)(2,1)S(1)} %get-tuple-element.42.after.own), channel_id=1, source_target_pairs={{0,16},{16,0},{1,17},{17,1},{2,18},{18,2},{3,19},{19,3},{4,20},{20... | collective-permute-start | bytes 884744 | tf_op jit(solution)/shard_map/gather/ppermute | solution.py:27
  4.6 2.7 %collective-permute-start.2 = (bf16[128,1152]{1,0:T(8,128)(2,1)S(1)}, bf16[128,1152]{1,0:T(8,128)(2,1)S(1)}, u32[]{:S(2)}, u32[]{:S(2)}) collective-permute-start(bf16[128,1152]{1,0:T(8,128)(2,1)S(1)} %get-tuple-element.47.t0), channel_id=1, source_target_pairs={{0,12},{4,8},{8,4},{12,0},{1,13},{5,9},{9,5},{13,1},{2,14},{6,10},... | collective-permute-start | bytes 884744 | tf_op jit(solution)/shard_map/gather/ppermute | solution.py:27
  9.5 1.8 %gather.2 = (bf16[1152,1152]{1,0:T(8,128)(2,1)S(1)}, bf16[576,1152]{1,0:T(8,128)(2,1)S(1)}, s32[512,1]{1,0:T(8,128)S(1)}, s32[1,512]{1,0:T(1,128)S(1)}, f32[2,128]{1,0:T(2,128)S(1)}) custom-call(bf16[128,1152]{1,0:T(8,128)(2,1)S(1)} %get-tuple-element.42.after.own, f32[1]{0:T(128)} %bitcast.2.scale, f32[1]{0:T(128)} %bitcast.3.bias, s32[1,16384]{1,0:T(1,128)S(1)} %copy-done, ...), custom_call_target="tpu_custom_call" | custom-call | flops 147456000 | bytes 147456 | tf_op jit(solution)/shard_map/gather/pallas_call | solution.py:231
  11.3 1.9 %collective-permute-done.2.t3 = bf16[128,1152]{1,0:T(8,128)(2,1)S(1)} collective-permute-done((bf16[128,1152]{1,0:T(8,128)(2,1)S(1)}, bf16[128,1152]{1,0:T(8,128)(2,1)S(1)}, u32[]{:S(2)}, u32[]{:S(2)}) %collective-permute-start.2) | collective-permute-done | bytes 294944 | tf_op jit(solution)/shard_map/gather/ppermute | solution.py:27
  13.1 1.5 %collective-permute-done.1.t1 = bf16[128,1152]{1,0:T(8,128)(2,1)S(1)} collective-permute-done((bf16[128,1152]{1,0:T(8,128)(2,1)S(1)}, bf16[128,1152]{1,0:T(8,128)(2,1)S(1)}, u32[]{:S(2)}, u32[]{:S(2)}) %collective-permute-start.1) | collective-permute-done | bytes 294944 | tf_op jit(solution)/shard_map/gather/ppermute | solution.py:27
  14.7 2.2 %collective-permute-start.3 = (bf16[256,1152]{1,0:T(8,128)(2,1)S(1)}, bf16[256,1152]{1,0:T(8,128)(2,1)S(1)}, u32[]{:S(2)}, u32[]{:S(2)}) collective-permute-start(bf16[256,1152]{1,0:T(8,128)(2,1)S(1)} %get-tuple-element.48.both), channel_id=1, source_target_pairs={{0,2},{2,0},{1,3},{3,1},{4,6},{6,4},{5,7},{7,5},{8,10},{10,8},{9,1... | collective-permute-start | bytes 1769480 | tf_op jit(solution)/shard_map/gather/ppermute | solution.py:27
  18.5 2.7 %project.1 = (bf16[512,1152]{1,0:T(8,128)(2,1)S(1)}, f32[512,1152]{1,0:T(8,128)S(1)}, f32[512,1]{1,0:T(8,128)S(1)}, bf16[576,512]{1,0:T(8,128)(2,1)S(1)}) custom-call(bf16[256,1152]{1,0:T(8,128)(2,1)S(1)} %get-tuple-element.48.both, bf16[256,1152]{1,0:T(8,128)(2,1)S(1)} %collective-permute-done.3.cores, bf16[1152,1152]{1,0:T(8,128)(2,1)S(1)} %get-tuple-element.49.weight, ...), custom_call_target="tpu_custom_call" | custom-call | bytes 147456 | tf_op jit(solution)/shard_map/project/pallas_call | solution.py:256
  21.3 1.7 %tile.2 = (bf16[512,384]{1,0:T(8,128)(2,1)S(1)}, f32[512,1152]{1,0:T(8,128)S(1)}) custom-call(f32[2,128]{1,0:T(2,128)S(1)} %get-tuple-element.43.settings, s32[512,1]{1,0:T(8,128)S(1)} %get-tuple-element.44.left, s32[1,512]{1,0:T(1,128)S(1)} %get-tuple-element.45.right, bf16[512,1152]{1,0:T(8,128)(2,1)S(1)} %get-tuple-element.50.embed, ...), custom_call_target="tpu_custom_call" | custom-call | bytes 147456 | tf_op jit(solution)/shard_map/tile/pallas_call | solution.py:265
  23.1 1.8 %tile.3 = (bf16[512,128]{1,0:T(8,128)(2,1)S(1)}, f32[512,1152]{1,0:T(8,128)S(1)}, bf16[512,1152]{1,0:T(8,128)(2,1)S(1)}) custom-call(f32[2,128]{1,0:T(2,128)S(1)} %get-tuple-element.43.settings, s32[512,1]{1,0:T(8,128)S(1)} %get-tuple-element.44.left, s32[1,512]{1,0:T(1,128)S(1)} %get-tuple-element.45.right, bf16[512,1152]{1,0:T(8,128)(2,1)S(1)} %get-tuple-element.50.embed, ...), custom_call_target="tpu_custom_call" | custom-call | bytes 147456 | tf_op jit(solution)/shard_map/tile/pallas_call | solution.py:268
  26.3 1.5 %collective-permute-start.11 = (bf16[128,1152]{1,0:T(8,128)(2,1)S(1)}, bf16[128,1152]{1,0:T(8,128)(2,1)S(1)}, u32[]{:S(2)}, u32[]{:S(2)}) collective-permute-start(bf16[128,1152]{1,0:T(8,128)(2,1)S(1)} %text.4), channel_id=1, source_target_pairs={{0,8},{4,12},{8,0},{12,4},{1,9},{5,13},{9,1},{13,5},{2,10},{6,14},... | collective-permute-start | bytes 884744 | tf_op jit(solution)/shard_map/text/ppermute | solution.py:27
  29.7 2.5 %collective-permute-start.8 = (bf16[144,1152]{1,0:T(8,128)(2,1)S(1)}, bf16[144,1152]{1,0:T(8,128)(2,1)S(1)}, u32[]{:S(2)}, u32[]{:S(2)}) collective-permute-start(bf16[144,1152]{1,0:T(8,128)(2,1)S(1)} %get-tuple-element.62), channel_id=1, source_target_pairs={{0,48},{16,32},{32,16},{48,0},{1,49},{17,33},{33,17},{49,1},{2,50}... | collective-permute-start | bytes 995336 | tf_op jit(solution)/shard_map/weight/ppermute | solution.py:27
  33.6 3.1 %collective-permute-done.11.b2 = bf16[128,1152]{1,0:T(8,128)(2,1)S(1)} collective-permute-done((bf16[128,1152]{1,0:T(8,128)(2,1)S(1)}, bf16[128,1152]{1,0:T(8,128)(2,1)S(1)}, u32[]{:S(2)}, u32[]{:S(2)}) %collective-permute-start.11) | collective-permute-done | bytes 294944 | tf_op jit(solution)/shard_map/text/ppermute | solution.py:27
  37.9 2.9 %collective-permute-done.10.b1 = bf16[128,1152]{1,0:T(8,128)(2,1)S(1)} collective-permute-done((bf16[128,1152]{1,0:T(8,128)(2,1)S(1)}, bf16[128,1152]{1,0:T(8,128)(2,1)S(1)}, u32[]{:S(2)}, u32[]{:S(2)}) %collective-permute-start.10) | collective-permute-done | bytes 294944 | tf_op jit(solution)/shard_map/weight/ppermute | solution.py:27
  40.8 4.8 %collective-permute-done.12.b3 = bf16[128,1152]{1,0:T(8,128)(2,1)S(1)} collective-permute-done((bf16[128,1152]{1,0:T(8,128)(2,1)S(1)}, bf16[128,1152]{1,0:T(8,128)(2,1)S(1)}, u32[]{:S(2)}, u32[]{:S(2)}) %collective-permute-start.12) | collective-permute-done | bytes 294944 | tf_op jit(solution)/shard_map/weight/ppermute | solution.py:27
  45.6 1.5 %collective-permute-done.9.a2 = bf16[144,1152]{1,0:T(8,128)(2,1)S(1)} collective-permute-done((bf16[144,1152]{1,0:T(8,128)(2,1)S(1)}, bf16[144,1152]{1,0:T(8,128)(2,1)S(1)}, u32[]{:S(2)}, u32[]{:S(2)}) %collective-permute-start.9) | collective-permute-done | bytes 331808 | tf_op jit(solution)/shard_map/weight/ppermute | solution.py:27
  47.4 1.4 %collective-permute-start.13 = (bf16[36,1152]{1,0:T(8,128)(2,1)S(1)}, bf16[36,1152]{1,0:T(8,128)(2,1)S(1)}, u32[]{:S(2)}, u32[]{:S(2)}) collective-permute-start(bf16[36,1152]{1,0:T(8,128)(2,1)S(1)} %get-tuple-element.69), channel_id=1, source_target_pairs={{0,8},{4,12},{8,0},{12,4},{1,9},{5,13},{9,1},{13,5},{2,10},{6,14},... | collective-permute-start | bytes 248840 | tf_op jit(solution)/shard_map/weight/ppermute | solution.py:27
  49.3 1.5 %collective-permute-start.15 = (bf16[36,1152]{1,0:T(8,128)(2,1)S(1)}, bf16[36,1152]{1,0:T(8,128)(2,1)S(1)}, u32[]{:S(2)}, u32[]{:S(2)}) collective-permute-start(bf16[36,1152]{1,0:T(8,128)(2,1)S(1)} %get-tuple-element.71), channel_id=1, source_target_pairs={{0,12},{4,8},{8,4},{12,0},{1,13},{5,9},{9,5},{13,1},{2,14},{6,10},... | collective-permute-start | bytes 248840 | tf_op jit(solution)/shard_map/weight/ppermute | solution.py:27
  50.7 1.7 %collective-permute-done.13.a2 = bf16[36,1152]{1,0:T(8,128)(2,1)S(1)} collective-permute-done((bf16[36,1152]{1,0:T(8,128)(2,1)S(1)}, bf16[36,1152]{1,0:T(8,128)(2,1)S(1)}, u32[]{:S(2)}, u32[]{:S(2)}) %collective-permute-start.13) | collective-permute-done | bytes 82976 | tf_op jit(solution)/shard_map/weight/ppermute | solution.py:27
  52.4 2.4 %collective-permute-done.15.a3 = bf16[36,1152]{1,0:T(8,128)(2,1)S(1)} collective-permute-done((bf16[36,1152]{1,0:T(8,128)(2,1)S(1)}, bf16[36,1152]{1,0:T(8,128)(2,1)S(1)}, u32[]{:S(2)}, u32[]{:S(2)}) %collective-permute-start.15) | collective-permute-done | bytes 82976 | tf_op jit(solution)/shard_map/weight/ppermute | solution.py:27
  55.4 1.6 %collective-permute-start.17 = (bf16[27,1152]{1,0:T(8,128)(2,1)S(1)}, bf16[27,1152]{1,0:T(8,128)(2,1)S(1)}, u32[]{:S(2)}, u32[]{:S(2)}) collective-permute-start(bf16[27,1152]{1,0:T(8,128)(2,1)S(1)} %get-tuple-element.76.after), channel_id=1, source_target_pairs={{0,1},{1,0},{2,3},{3,2},{4,5},{5,4},{6,7},{7,6},{8,9},{9,8},{10,11... | collective-permute-start | bytes 186632 | tf_op jit(solution)/shard_map/weight/ppermute | solution.py:27
  58.8 9.2 %collective-permute-start.20 = (bf16[9,1152]{1,0:T(8,128)(2,1)S(1)}, bf16[9,1152]{1,0:T(8,128)(2,1)S(1)}, u32[]{:S(2)}, u32[]{:S(2)}) collective-permute-start(bf16[9,1152]{1,0:T(8,128)(2,1)S(1)} %get-tuple-element.78), channel_id=1, source_target_pairs={{0,194},{2,192},{1,67},{3,65},{64,2},{66,0},{65,131},{67,129},{128... | collective-permute-start | bytes 62216 | tf_op jit(solution)/shard_map/weight/ppermute | solution.py:211
  68.0 1.6 %collective-permute-start.19 = (bf16[9,1152]{1,0:T(8,128)(2,1)S(1)}, bf16[9,1152]{1,0:T(8,128)(2,1)S(1)}, u32[]{:S(2)}, u32[]{:S(2)}) collective-permute-start(bf16[9,1152]{1,0:T(8,128)(2,1)S(1)} %get-tuple-element.79), channel_id=1, source_target_pairs={{0,129},{2,131},{1,128},{3,130},{64,193},{66,195},{65,192},{67,194... | collective-permute-start | bytes 62216 | tf_op jit(solution)/shard_map/weight/ppermute | solution.py:211
  69.6 1.6 %hidden.3 = (bf16[128,1152]{1,0:T(8,128)(2,1)}, f32[8,128]{1,0:T(8,128)S(1)}) custom-call(s32[1]{0:T(128)S(6)} %copy.10.count, f32[256,1152]{1,0:T(8,128)S(1)} %get-tuple-element.59.rows, bf16[128,1152]{1,0:T(8,128)(2,1)S(1)} %collective-permute-done.16.arrived, bf16[1152,1152]{1,0:T(8,128)(2,1)S(1)} %get-tuple-element.49.weight), custom_call_target="tpu_custom_call" | custom-call | flops 339738624 | bytes 2654208 | tf_op jit(solution)/shard_map/hidden/pallas_call | solution.py:326
  71.3 2.5 %collective-permute-done.19.a3 = bf16[9,1152]{1,0:T(8,128)(2,1)S(1)} collective-permute-done((bf16[9,1152]{1,0:T(8,128)(2,1)S(1)}, bf16[9,1152]{1,0:T(8,128)(2,1)S(1)}, u32[]{:S(2)}, u32[]{:S(2)}) %collective-permute-start.19) | collective-permute-done | bytes 20768 | tf_op jit(solution)/shard_map/weight/ppermute | solution.py:211
  (35 shorter events, 13.6 us)
Async XLA Ops:
  2.5 8.8 %collective-permute-start = (bf16[128,1152]{1,0:T(8,128)(2,1)S(1)}, bf16[128,1152]{1,0:T(8,128)(2,1)S(1)}, u32[]{:S(2)}, u32[]{:S(2)}) collective-permute-start(bf16[128,1152]{1,0:T(8,128)(2,1)S(1)} %get-tuple-element.42.after.own), channel_id=1, source_target_pairs={{0,16},{16,0},{1,17},{17,1},{2,18},{18,2},{3,19},{19,3},{4,20},{20... | collective-permute-start | bytes 884744 | tf_op jit(solution)/shard_map/gather/ppermute | solution.py:27
  4.6 8.5 %collective-permute-start.2 = (bf16[128,1152]{1,0:T(8,128)(2,1)S(1)}, bf16[128,1152]{1,0:T(8,128)(2,1)S(1)}, u32[]{:S(2)}, u32[]{:S(2)}) collective-permute-start(bf16[128,1152]{1,0:T(8,128)(2,1)S(1)} %get-tuple-element.47.t0), channel_id=1, source_target_pairs={{0,12},{4,8},{8,4},{12,0},{1,13},{5,9},{9,5},{13,1},{2,14},{6,10},... | collective-permute-start | bytes 884744 | tf_op jit(solution)/shard_map/gather/ppermute | solution.py:27
  7.3 7.3 %collective-permute-start.1 = (bf16[128,1152]{1,0:T(8,128)(2,1)S(1)}, bf16[128,1152]{1,0:T(8,128)(2,1)S(1)}, u32[]{:S(2)}, u32[]{:S(2)}) collective-permute-start(bf16[128,1152]{1,0:T(8,128)(2,1)S(1)} %get-tuple-element.47.t0), channel_id=1, source_target_pairs={{0,4},{4,0},{8,12},{12,8},{1,5},{5,1},{9,13},{13,9},{2,6},{6,2},{1... | collective-permute-start | bytes 884744 | tf_op jit(solution)/shard_map/gather/ppermute | solution.py:27
  8.6 0.8 %copy-start = (s32[1,16384]{1,0:T(1,128)S(1)}, s32[1,16384]{1,0:T(1,128)}, u32[]{:S(2)}) copy-start(s32[1,16384]{1,0:T(1,128)} %pair_ids.1) | copy-start | bytes 196612
  14.7 3.9 %collective-permute-start.3 = (bf16[256,1152]{1,0:T(8,128)(2,1)S(1)}, bf16[256,1152]{1,0:T(8,128)(2,1)S(1)}, u32[]{:S(2)}, u32[]{:S(2)}) collective-permute-start(bf16[256,1152]{1,0:T(8,128)(2,1)S(1)} %get-tuple-element.48.both), channel_id=1, source_target_pairs={{0,2},{2,0},{1,3},{3,1},{4,6},{6,4},{5,7},{7,5},{8,10},{10,8},{9,1... | collective-permute-start | bytes 1769480 | tf_op jit(solution)/shard_map/gather/ppermute | solution.py:27
  16.9 6.2 %collective-permute-start.4 = (bf16[80,1152]{1,0:T(8,128)(2,1)S(1)}, bf16[80,1152]{1,0:T(8,128)(2,1)S(1)}, u32[]{:S(2)}, u32[]{:S(2)}) collective-permute-start(bf16[80,1152]{1,0:T(8,128)(2,1)S(1)} %get-tuple-element.53), channel_id=1, source_target_pairs={{0,4},{4,0},{8,12},{12,8},{1,5},{5,1},{9,13},{13,9},{2,6},{6,2},{1... | collective-permute-start | bytes 552968 | tf_op jit(solution)/shard_map/gather/ppermute | solution.py:27
  16.9 6.0 %collective-permute-start.5 = (bf16[48,1152]{1,0:T(8,128)(2,1)S(1)}, bf16[48,1152]{1,0:T(8,128)(2,1)S(1)}, u32[]{:S(2)}, u32[]{:S(2)}) collective-permute-start(bf16[48,1152]{1,0:T(8,128)(2,1)S(1)} %get-tuple-element.54), channel_id=1, source_target_pairs={{0,12},{4,8},{8,4},{12,0},{1,13},{5,9},{9,5},{13,1},{2,14},{6,10},... | collective-permute-start | bytes 331784 | tf_op jit(solution)/shard_map/gather/ppermute | solution.py:27
  24.9 3.4 %collective-permute-start.6 = (bf16[512,1152]{1,0:T(8,128)(2,1)S(1)}, bf16[512,1152]{1,0:T(8,128)(2,1)S(1)}, u32[]{:S(2)}, u32[]{:S(2)}) collective-permute-start(bf16[512,1152]{1,0:T(8,128)(2,1)S(1)} %get-tuple-element.57), channel_id=1, source_target_pairs={{0,2},{2,0},{1,3},{3,1},{4,6},{6,4},{5,7},{7,5},{8,10},{10,8},{9,1... | collective-permute-start | bytes 3538952 | tf_op jit(solution)/shard_map/core/ppermute | solution.py:27
  26.3 10.4 %collective-permute-start.11 = (bf16[128,1152]{1,0:T(8,128)(2,1)S(1)}, bf16[128,1152]{1,0:T(8,128)(2,1)S(1)}, u32[]{:S(2)}, u32[]{:S(2)}) collective-permute-start(bf16[128,1152]{1,0:T(8,128)(2,1)S(1)} %text.4), channel_id=1, source_target_pairs={{0,8},{4,12},{8,0},{12,4},{1,9},{5,13},{9,1},{13,5},{2,10},{6,14},... | collective-permute-start | bytes 884744 | tf_op jit(solution)/shard_map/text/ppermute | solution.py:27
  29.4 16.2 %collective-permute-start.7 = (bf16[144,1152]{1,0:T(8,128)(2,1)S(1)}, bf16[144,1152]{1,0:T(8,128)(2,1)S(1)}, u32[]{:S(2)}, u32[]{:S(2)}) collective-permute-start(bf16[144,1152]{1,0:T(8,128)(2,1)S(1)} %get-tuple-element.61), channel_id=1, source_target_pairs={{0,16},{16,0},{32,48},{48,32},{1,17},{17,1},{33,49},{49,33},{2,18}... | collective-permute-start | bytes 995336 | tf_op jit(solution)/shard_map/weight/ppermute | solution.py:27
  29.7 15.9 %collective-permute-start.8 = (bf16[144,1152]{1,0:T(8,128)(2,1)S(1)}, bf16[144,1152]{1,0:T(8,128)(2,1)S(1)}, u32[]{:S(2)}, u32[]{:S(2)}) collective-permute-start(bf16[144,1152]{1,0:T(8,128)(2,1)S(1)} %get-tuple-element.62), channel_id=1, source_target_pairs={{0,48},{16,32},{32,16},{48,0},{1,49},{17,33},{33,17},{49,1},{2,50}... | collective-permute-start | bytes 995336 | tf_op jit(solution)/shard_map/weight/ppermute | solution.py:27
  32.2 14.9 %collective-permute-start.9 = (bf16[144,1152]{1,0:T(8,128)(2,1)S(1)}, bf16[144,1152]{1,0:T(8,128)(2,1)S(1)}, u32[]{:S(2)}, u32[]{:S(2)}) collective-permute-start(bf16[144,1152]{1,0:T(8,128)(2,1)S(1)} %get-tuple-element.63), channel_id=1, source_target_pairs={{0,32},{16,48},{32,0},{48,16},{1,33},{17,49},{33,1},{49,17},{2,34}... | collective-permute-start | bytes 995336 | tf_op jit(solution)/shard_map/weight/ppermute | solution.py:27
  33.4 7.4 %collective-permute-start.10 = (bf16[128,1152]{1,0:T(8,128)(2,1)S(1)}, bf16[128,1152]{1,0:T(8,128)(2,1)S(1)}, u32[]{:S(2)}, u32[]{:S(2)}) collective-permute-start(bf16[128,1152]{1,0:T(8,128)(2,1)S(1)} %get-tuple-element.65), channel_id=1, source_target_pairs={{0,4},{4,0},{8,12},{12,8},{1,5},{5,1},{9,13},{13,9},{2,6},{6,2},{1... | collective-permute-start | bytes 884744 | tf_op jit(solution)/shard_map/weight/ppermute | solution.py:27
  36.7 8.9 %collective-permute-start.12 = (bf16[128,1152]{1,0:T(8,128)(2,1)S(1)}, bf16[128,1152]{1,0:T(8,128)(2,1)S(1)}, u32[]{:S(2)}, u32[]{:S(2)}) collective-permute-start(bf16[128,1152]{1,0:T(8,128)(2,1)S(1)} %get-tuple-element.67), channel_id=1, source_target_pairs={{0,12},{4,8},{8,4},{12,0},{1,13},{5,9},{9,5},{13,1},{2,14},{6,10},... | collective-permute-start | bytes 884744 | tf_op jit(solution)/shard_map/weight/ppermute | solution.py:27
  47.4 5.0 %collective-permute-start.13 = (bf16[36,1152]{1,0:T(8,128)(2,1)S(1)}, bf16[36,1152]{1,0:T(8,128)(2,1)S(1)}, u32[]{:S(2)}, u32[]{:S(2)}) collective-permute-start(bf16[36,1152]{1,0:T(8,128)(2,1)S(1)} %get-tuple-element.69), channel_id=1, source_target_pairs={{0,8},{4,12},{8,0},{12,4},{1,9},{5,13},{9,1},{13,5},{2,10},{6,14},... | collective-permute-start | bytes 248840 | tf_op jit(solution)/shard_map/weight/ppermute | solution.py:27
  48.8 3.7 %collective-permute-start.14 = (bf16[36,1152]{1,0:T(8,128)(2,1)S(1)}, bf16[36,1152]{1,0:T(8,128)(2,1)S(1)}, u32[]{:S(2)}, u32[]{:S(2)}) collective-permute-start(bf16[36,1152]{1,0:T(8,128)(2,1)S(1)} %get-tuple-element.70), channel_id=1, source_target_pairs={{0,4},{4,0},{8,12},{12,8},{1,5},{5,1},{9,13},{13,9},{2,6},{6,2},{1... | collective-permute-start | bytes 248840 | tf_op jit(solution)/shard_map/weight/ppermute | solution.py:27
  49.3 5.6 %collective-permute-start.15 = (bf16[36,1152]{1,0:T(8,128)(2,1)S(1)}, bf16[36,1152]{1,0:T(8,128)(2,1)S(1)}, u32[]{:S(2)}, u32[]{:S(2)}) collective-permute-start(bf16[36,1152]{1,0:T(8,128)(2,1)S(1)} %get-tuple-element.71), channel_id=1, source_target_pairs={{0,12},{4,8},{8,4},{12,0},{1,13},{5,9},{9,5},{13,1},{2,14},{6,10},... | collective-permute-start | bytes 248840 | tf_op jit(solution)/shard_map/weight/ppermute | solution.py:27
  55.0 14.6 %collective-permute-start.16 = (bf16[128,1152]{1,0:T(8,128)(2,1)S(1)}, bf16[128,1152]{1,0:T(8,128)(2,1)S(1)}, u32[]{:S(2)}, u32[]{:S(2)}) collective-permute-start(bf16[128,1152]{1,0:T(8,128)(2,1)S(1)} %get-tuple-element.72), channel_id=1, source_target_pairs={{0,16},{16,0},{1,17},{17,1},{2,18},{18,2},{3,19},{19,3},{4,20},{20... | collective-permute-start | bytes 884744 | tf_op jit(solution)/shard_map/hidden/ppermute | solution.py:27
  55.4 3.4 %collective-permute-start.17 = (bf16[27,1152]{1,0:T(8,128)(2,1)S(1)}, bf16[27,1152]{1,0:T(8,128)(2,1)S(1)}, u32[]{:S(2)}, u32[]{:S(2)}) collective-permute-start(bf16[27,1152]{1,0:T(8,128)(2,1)S(1)} %get-tuple-element.76.after), channel_id=1, source_target_pairs={{0,1},{1,0},{2,3},{3,2},{4,5},{5,4},{6,7},{7,6},{8,9},{9,8},{10,11... | collective-permute-start | bytes 186632 | tf_op jit(solution)/shard_map/weight/ppermute | solution.py:27
  58.8 15.0 %collective-permute-start.20 = (bf16[9,1152]{1,0:T(8,128)(2,1)S(1)}, bf16[9,1152]{1,0:T(8,128)(2,1)S(1)}, u32[]{:S(2)}, u32[]{:S(2)}) collective-permute-start(bf16[9,1152]{1,0:T(8,128)(2,1)S(1)} %get-tuple-element.78), channel_id=1, source_target_pairs={{0,194},{2,192},{1,67},{3,65},{64,2},{66,0},{65,131},{67,129},{128... | collective-permute-start | bytes 62216 | tf_op jit(solution)/shard_map/weight/ppermute | solution.py:211
  68.0 5.8 %collective-permute-start.18 = (bf16[9,1152]{1,0:T(8,128)(2,1)S(1)}, bf16[9,1152]{1,0:T(8,128)(2,1)S(1)}, u32[]{:S(2)}, u32[]{:S(2)}) collective-permute-start(bf16[9,1152]{1,0:T(8,128)(2,1)S(1)} %get-tuple-element.78), channel_id=1, source_target_pairs={{0,195},{2,193},{1,66},{3,64},{64,3},{66,1},{65,130},{67,128},{128... | collective-permute-start | bytes 62216 | tf_op jit(solution)/shard_map/weight/ppermute | solution.py:211
  68.0 5.8 %collective-permute-start.19 = (bf16[9,1152]{1,0:T(8,128)(2,1)S(1)}, bf16[9,1152]{1,0:T(8,128)(2,1)S(1)}, u32[]{:S(2)}, u32[]{:S(2)}) collective-permute-start(bf16[9,1152]{1,0:T(8,128)(2,1)S(1)} %get-tuple-element.79), channel_id=1, source_target_pairs={{0,129},{2,131},{1,128},{3,130},{64,193},{66,195},{65,192},{67,194... | collective-permute-start | bytes 62216 | tf_op jit(solution)/shard_map/weight/ppermute | solution.py:211
